TPU v7x, 256 devices: a whole 4x4x8 slice. The times are simulated.
256 devices in a mesh: dp: 32 (over z_hi, y, core), mp: 8 (over z_lo, x).
Axes of the slice: x: 4, y: 4, z: 8 (z_hi: 4, z_lo: 2; z = z_hi * 2 + z_lo), core: 2. Of those that a mesh axis runs over, the one named last changes fastest.
Arguments:
- features: bfloat16 [2, 8192, 1024], P(None, 'dp'), may hold values from -8 to 8
- projections: bfloat16 [2, 1024, 768], P(None, 'mp'), may hold values from -1 to 1
- solution: float32 [2, 1024, 768], P(None, 'mp'), may hold values from -6 to 6
- residual: float32 [2, 1024, 768], P(None, 'mp'), may hold values from -6 to 6
- direction: float32 [2, 1024, 768], P(None, 'mp'), may hold values from -6 to 6
Outputs:
- new_solution: float32 [2, 1024, 768], P(None, 'mp')
- new_residual: float32 [2, 1024, 768], P(None, 'mp')
- new_direction: float32 [2, 1024, 768], P(None, 'mp')
All inputs are finite; a program needn't handle non-finite values.
Results may differ from a plain program's by a relative error of at most 0.0016.
The roundings to bfloat16 on the way count: a program that leaves them out, or rounds other values in their place, can miss the bound.
Values may be sent and summed in bfloat16 or wider, within the bound.
A program may use at most 64 MiB of HBM per device.

v0:
```python
import jax
import jax.numpy as jnp
from jax import lax
from jax.sharding import PartitionSpec as P

LOGIT_SCALE = 100.0
DAMPING = 1.0
EPSILON = 1e-06


def merged(value, axis, join):
    pieces = jax.tree.map(lambda part: lax.all_gather(part, axis), value)
    head = jax.tree.map(lambda part: part[0], pieces)
    tail = jax.tree.map(lambda part: part[1:], pieces)
    subtotal, _ = lax.scan(lambda subtotal, piece: (join(subtotal, piece), None), head, tail)
    return subtotal


def softmax_merge(first, second):
    top = jnp.maximum(first[0], second[0])
    return (top, first[1] * jnp.exp(first[0] - top) + second[1] * jnp.exp(second[0] - top))


def unit_rows(raw):
    inverse = lax.rsqrt(jnp.sum(raw * raw, -1, keepdims=True) + EPSILON)
    return (raw * inverse, inverse)


def turn_rows(tangent, unit_vec, inverse):
    return (tangent - unit_vec * jnp.sum(unit_vec * tangent, -1, keepdims=True)) * inverse


def grad_tangent(unit_vec, turned, inverse, tangent, grads, tgrads):
    along = jnp.sum(unit_vec * grads, -1, keepdims=True)
    plain = (grads - unit_vec * along) * inverse
    mixed = jnp.sum(turned * grads, -1, keepdims=True) + jnp.sum(
        unit_vec * tgrads, -1, keepdims=True
    )
    result = (tgrads - turned * along - unit_vec * mixed) * inverse
    return result - plain * inverse * jnp.sum(unit_vec * tangent, -1, keepdims=True)


def inner(left_mat, right_mat):
    return jnp.einsum("ip,jp->ij", left_mat, right_mat, preferred_element_type=jnp.float32)


def body(features, projections, solution, residual, direction):
    rows = features.shape[1]
    part = projections.shape[1]
    width = projections.shape[2]
    model_count = lax.axis_size("mp")
    data_count = lax.axis_size("dp")
    model_index = lax.axis_index("mp")
    data_index = lax.axis_index("dp")
    share = rows // model_count
    columns = share * data_count
    total = rows * data_count
    local_feats = lax.dynamic_slice_in_dim(features, model_index * part, part, 2)
    packed = direction.astype(jnp.bfloat16)

    def embed_term(pairs):
        return jnp.concatenate(
            [
                jnp.dot(local_feats[tower], matrix, preferred_element_type=jnp.float32)
                for tower, matrix in pairs
            ],
            1,
        )

    primal_pairs = [(0, projections[0]), (1, projections[1])]
    tangent_pairs = [(0, packed[0]), (1, packed[1])]
    primal = lax.psum_scatter(embed_term(primal_pairs), "mp", scatter_dimension=0, tiled=True)
    unit_vec, inverse = unit_rows(primal.reshape(share, 2, width))
    unit_low = unit_vec.astype(jnp.bfloat16)
    rows_p = lax.all_gather(unit_low[:, 0], "mp", axis=0, tiled=True)
    cols_p = lax.all_gather(unit_low[:, 1], "dp", axis=0, tiled=True)
    scores = LOGIT_SCALE * inner(rows_p, cols_p)
    row_max = jnp.max(scores, 1)
    row_sum = jnp.sum(jnp.exp(scores - row_max[:, None]), 1)
    row_max, row_sum = merged((row_max, row_sum), "mp", softmax_merge)
    col_max = jnp.max(scores, 0)
    col_sum = jnp.sum(jnp.exp(scores - col_max[None, :]), 0)
    col_max, col_sum = merged((col_max, col_sum), "dp", softmax_merge)
    statistics_row_w = jnp.exp(scores - (row_max + jnp.log(row_sum))[:, None])
    statistics_col_w = jnp.exp(scores - (col_max + jnp.log(col_sum))[None, :])
    tangent = lax.psum_scatter(
        embed_term(tangent_pairs), "mp", scatter_dimension=0, tiled=True
    ).reshape(share, 2, width)
    turned = turn_rows(tangent, unit_vec, inverse)
    turned_low = turned.astype(jnp.bfloat16)
    rows_t = lax.all_gather(turned_low[:, 0], "mp", axis=0, tiled=True)
    cols_t = lax.all_gather(turned_low[:, 1], "dp", axis=0, tiled=True)
    tscores = LOGIT_SCALE * (inner(rows_t, cols_p) + inner(rows_p, cols_t))
    row_ids = data_index * rows + jnp.arange(rows, dtype=jnp.int32)
    col_iota = jnp.arange(columns, dtype=jnp.int32)
    col_ids = col_iota // share * rows + model_index * share + col_iota % share
    positive = (row_ids[:, None] == col_ids[None, :]).astype(jnp.float32)
    dscore = ((statistics_row_w + statistics_col_w - 2.0 * positive) / (2.0 * total)).astype(
        jnp.bfloat16
    )

    def row_moving(tdscore):

        def term(start, count):
            return LOGIT_SCALE * (
                jnp.dot(tdscore, cols_p, preferred_element_type=jnp.float32)
                + jnp.dot(dscore, cols_t, preferred_element_type=jnp.float32)
            )

        return term

    def col_moving(tdscore):

        def term(start, count):
            return LOGIT_SCALE * (
                jnp.einsum("ic,ip->cp", tdscore, rows_p, preferred_element_type=jnp.float32)
                + jnp.einsum("ic,ip->cp", dscore, rows_t, preferred_element_type=jnp.float32)
            )

        return term

    row_dot = lax.psum(jnp.sum(statistics_row_w * tscores, 1), "mp")
    col_dot = lax.psum(jnp.sum(statistics_col_w * tscores, 0), "dp")
    tdscore = (
        (
            statistics_row_w * (tscores - row_dot[:, None])
            + statistics_col_w * (tscores - col_dot[None, :])
        )
        / (2.0 * total)
    ).astype(jnp.bfloat16)
    row_extra = row_moving(tdscore)
    col_extra = col_moving(tdscore)
    plain = dscore
    row_part = lax.psum_scatter(
        jnp.concatenate(
            [
                LOGIT_SCALE * jnp.dot(plain, cols_p, preferred_element_type=jnp.float32),
                row_extra(jnp.int32(0), lax.axis_size("mp") * share),
            ],
            1,
        ),
        "mp",
        scatter_dimension=0,
        tiled=True,
    )
    plain = dscore
    col_part = lax.psum_scatter(
        jnp.concatenate(
            [
                LOGIT_SCALE
                * jnp.einsum("ic,ip->cp", plain, rows_p, preferred_element_type=jnp.float32),
                col_extra(jnp.int32(0), lax.axis_size("dp") * share),
            ],
            1,
        ),
        "dp",
        scatter_dimension=0,
        tiled=True,
    )
    row_first, row_second = (row_part[:, :width], row_part[:, width:])
    col_first, col_second = (col_part[:, :width], col_part[:, width:])
    grads = jnp.stack([row_first, col_first], 1)
    tgrads = jnp.stack([row_second, col_second], 1)
    tdz = (
        grad_tangent(unit_vec, turned, inverse, tangent, grads, tgrads)
        .astype(jnp.bfloat16)
        .reshape(share, 2 * width)
    )
    piece = lax.all_gather(tdz, "mp", axis=0, tiled=True)
    partial_hess = jnp.stack(
        [
            jnp.einsum(
                "rd,rp->dp",
                local_feats[tower],
                piece[:, tower * width : (tower + 1) * width],
                preferred_element_type=jnp.float32,
            )
            for tower in range(2)
        ]
    )
    hess = lax.psum(partial_hess, "dp") + DAMPING * direction
    norm_old = lax.psum(jnp.sum(residual * residual), "mp")
    curve = lax.psum(jnp.sum(direction * hess), "mp")
    alpha = norm_old / curve
    new_solution = solution + alpha * direction
    new_residual = residual - alpha * hess
    norm_new = lax.psum(jnp.sum(new_residual * new_residual), "mp")
    new_direction = new_residual + norm_new / norm_old * direction
    return (new_solution, new_residual, new_direction)


def solution(mesh):
    placed = (
        P(None, "dp", None),
        P(None, "mp", None),
        P(None, "mp", None),
        P(None, "mp", None),
        P(None, "mp", None),
    )
    return jax.shard_map(
        body,
        mesh=mesh,
        in_specs=placed,
        out_specs=(P(None, "mp", None), P(None, "mp", None), P(None, "mp", None)),
        check_vma=False,
    )
```

profile of v0, /device:TPU:1, one launch (start us, length us, event | category | flops | bytes accessed | tf_op | source)
XLA Modules:
  0.0 895.6 jit_solution(16088415107788603355)
XLA Ops:
  7.2 1.2 copy-done
  9.6 1.2 fusion.46
  10.7 1.3 pad_maximum_fusion.1
  13.8 1.3 pad_maximum_fusion.2
  15.2 39.3 %reduce-scatter.5.cloned.1.call-done = f32[32,1536]{1,0:T(8,128)} async-done(((f32[256,1536]{1,0:T(8,128)}), f32[32,1536]{1,0:T(8,128)}) %reduce-scatter.5.cloned.1.call-update) | async-done | bytes 196624 | tf_op jit(solution)/shard_map/reduce_scatter | solution.py:72
  55.8 43.5 %reduce-scatter.7.cloned.1.call-done = f32[32,1536]{1,0:T(8,128)} async-done(((f32[256,1536]{1,0:T(8,128)}), f32[32,1536]{1,0:T(8,128)}) %reduce-scatter.7.cloned.1.call-update) | async-done | bytes 196624 | tf_op jit(solution)/shard_map/reduce_scatter | solution.py:86
  99.3 1.2 fusion.43
  103.0 22.4 %all-gather = bf16[256,1,768]{2,0,1:T(8,128)(2,1)S(1)} all-gather(bf16[32,1,768]{2,0,1:T(8,128)(2,1)S(1)} %get-tuple-element.121), channel_id=2, replica_groups=mesh['dp'=32,'mp'=8] {'mp'}, dimensions={0}, use_global_device_ids=true | all-gather | bytes 442368 | tf_op jit(solution)/shard_map/all_gather | solution.py:75
  126.0 23.3 %all-gather.6 = bf16[256,1,768]{2,0,1:T(8,128)(2,1)S(1)} all-gather(bf16[32,1,768]{2,0,1:T(8,128)(2,1)S(1)} %get-tuple-element.118), channel_id=8, replica_groups=mesh['dp'=32,'mp'=8] {'mp'}, dimensions={0}, use_global_device_ids=true | all-gather | bytes 442368 | tf_op jit(solution)/shard_map/all_gather | solution.py:91
  149.4 10.9 %all-gather.13.cloned.1.call-done = bf16[1024,1,768]{2,0,1:T(8,128)(2,1)} async-done(((bf16[32,1,768]{2,0,1:T(8,128)(2,1)}), bf16[1024,1,768]{2,0,1:T(8,128)(2,1)}) %all-gather.13.cloned.1.call-update) | async-done | bytes 1572880 | tf_op jit(solution)/shard_map/all_gather | solution.py:76
  160.3 2.1 fusion.72
  162.4 51.7 %all-gather.4 = f32[32768]{0:T(1024)S(1)} all-gather(f32[1024]{0:T(1024)S(1)} %get-tuple-element.68), channel_id=6, replica_groups=mesh['dp'=32,'mp'=8] {'dp'}, dimensions={0}, use_global_device_ids=true | all-gather | bytes 135168 | tf_op jit(solution)/shard_map/all_gather | solution.py:12
  214.5 39.5 %all-gather.5 = f32[32768]{0:T(1024)S(1)} all-gather(f32[1024]{0:T(1024)S(1)} %get-tuple-element.66), channel_id=7, replica_groups=mesh['dp'=32,'mp'=8] {'dp'}, dimensions={0}, use_global_device_ids=true | all-gather | bytes 135168 | tf_op jit(solution)/shard_map/all_gather | solution.py:12
  254.1 1.7 while.25
  255.8 13.7 %all-gather.9 = f32[8,1,256]{2,1,0:T(1,128)S(1)} all-gather(f32[1,1,256]{2,1,0:T(1,128)S(1)} %bitcast.178), channel_id=5, replica_groups=mesh['dp'=32,'mp'=8] {'mp'}, dimensions={0}, use_global_device_ids=true | all-gather | bytes 9216 | tf_op jit(solution)/shard_map/all_gather | solution.py:12
  269.5 11.6 %all-gather.8 = f32[8,1,256]{2,1,0:T(1,128)S(1)} all-gather(f32[1,1,256]{2,1,0:T(1,128)S(1)} %bitcast.177), channel_id=4, replica_groups=mesh['dp'=32,'mp'=8] {'mp'}, dimensions={0}, use_global_device_ids=true | all-gather | bytes 9216 | tf_op jit(solution)/shard_map/all_gather | solution.py:12
  281.6 2.2 fusion.2
  283.7 1.7 multiply_reduce_fusion.1
  285.5 76.6 %psum.44 = f32[1024]{0:T(1024)S(1)} all-reduce(f32[1024]{0:T(1024)S(1)} %get-tuple-element.64), channel_id=1, replica_groups=mesh['dp'=32,'mp'=8] {'dp'}, use_global_device_ids=true, to_apply=%region_17.18 | all-reduce | flops 1024 | bytes 8192 | tf_op jit(solution)/shard_map/psum | solution.py:123
  362.1 14.7 %psum.43 = f32[256]{0:T(256)} all-reduce(f32[256]{0:T(256)S(1)} %get-tuple-element.63), channel_id=1, replica_groups=mesh['dp'=32,'mp'=8] {'mp'}, use_global_device_ids=true, to_apply=%region_15.16 | all-reduce | flops 256 | bytes 2048 | tf_op jit(solution)/shard_map/psum | solution.py:122
  376.8 2.4 multiply_convert_fusion.1
  381.0 1.3 pad_maximum_fusion.3
  385.1 3.6 pad_maximum_fusion
  389.8 27.4 %reduce-scatter.9.cloned.1.call-done = f32[32,1536]{1,0:T(8,128)} async-done(((f32[256,1536]{1,0:T(8,128)}), f32[32,1536]{1,0:T(8,128)}) %reduce-scatter.9.cloned.1.call-update) | async-done | bytes 196624 | tf_op jit(solution)/shard_map/reduce_scatter | solution.py:134
  418.2 115.4 %reduce-scatter.11.cloned.1.call-done = f32[32,1536]{1,0:T(8,128)} async-done(((f32[1024,1536]{1,0:T(8,128)}), f32[32,1536]{1,0:T(8,128)}) %reduce-scatter.11.cloned.1.call-update) | async-done | bytes 196624 | tf_op jit(solution)/shard_map/reduce_scatter | solution.py:147
  535.4 24.4 %all_gather.51 = bf16[256,1536]{1,0:T(8,128)(2,1)S(1)} all-gather(bf16[32,1536]{1,0:T(8,128)(2,1)S(1)} %fusion.41), channel_id=1, replica_groups=mesh['dp'=32,'mp'=8] {'mp'}, dimensions={0}, use_global_device_ids=true | all-gather | bytes 884736 | tf_op jit(solution)/shard_map/all_gather | solution.py:169
  562.1 289.0 %all-reduce.3.cloned.1.call-done = f32[2,128,768]{2,1,0:T(8,128)} async-done(((f32[2,128,768]{2,1,0:T(8,128)}), f32[2,128,768]{2,1,0:T(8,128)}) %all-reduce.3.cloned.1.call-update) | async-done | bytes 786448 | tf_op jit(solution)/shard_map/psum | solution.py:181
  851.2 2.0 multiply_reduce_fusion.3
  853.1 15.6 %all-reduce = (f32[]{:T(128)}, f32[]{:T(128)}) all-reduce(f32[]{:T(128)} %multiply_reduce_fusion.4, f32[]{:T(128)} %get-tuple-element.100), channel_id=1, replica_groups=mesh['dp'=32,'mp'=8] {'mp'}, use_global_device_ids=true, to_apply=%region_1.0 | all-reduce | flops 2 | bytes 16 | tf_op jit(solution)/shard_map/psum | solution.py:182
  870.0 1.6 multiply_reduce_fusion.2
  871.6 13.1 %psum.47 = f32[]{:T(128)} all-reduce(f32[]{:T(128)} %get-tuple-element.98), channel_id=1, replica_groups=mesh['dp'=32,'mp'=8] {'mp'}, use_global_device_ids=true, to_apply=%region_27.28 | all-reduce | flops 1 | bytes 8 | tf_op jit(solution)/shard_map/psum | solution.py:187
  886.1 2.7 multiply_add_fusion.2
  (182 shorter events, 19.6 us)
Async XLA Ops:
  7.2 1.2 copy-start
  7.2 47.3 %reduce-scatter.5.cloned.1.call-start = ((), (), s32[]{:S(2)}) async-start(), calls=%async_computation.4 | async-start | bytes 1769472 | tf_op jit(solution)/shard_map/reduce_scatter | solution.py:72
  12.1 1.1 copy-start.4
  12.1 87.2 %reduce-scatter.7.cloned.1.call-start = ((), (), s32[]{:S(2)}) async-start(), calls=%async_computation.5 | async-start | bytes 1769472 | tf_op jit(solution)/shard_map/reduce_scatter | solution.py:86
  15.1 145.2 %all-gather.13.cloned.1.call-start = ((), (), s32[]{:S(2)}) async-start(), calls=%async_computation.9 | async-start | bytes 1622016 | tf_op jit(solution)/shard_map/all_gather | solution.py:76
  100.5 1.1 copy-start.14
  102.3 179.2 %all-gather.15.cloned.1.call-start = ((), (), s32[]{:S(2)}) async-start(), calls=%async_computation.10 | async-start | bytes 1622016 | tf_op jit(solution)/shard_map/all_gather | solution.py:92
  149.3 134.4 %copy-start.10 = (bf16[256,1,768]{2,0,1:T(8,128)(2,1)}, bf16[256,1,768]{2,0,1:T(8,128)(2,1)S(1)}, u32[]{:S(2)}) copy-start(bf16[256,1,768]{2,0,1:T(8,128)(2,1)S(1)} %all-gather.6) | copy-start | bytes 1179652
  149.3 267.9 %reduce-scatter.9.cloned.1.call-start = ((), (), s32[]{:S(2)}) async-start(), calls=%async_computation.6 | async-start | bytes 1769472 | tf_op jit(solution)/shard_map/reduce_scatter | solution.py:134
  162.4 51.7 %copy-start.2 = (f32[256,1024]{1,0:T(8,128)}, f32[256,1024]{1,0:T(8,128)S(1)}, u32[]{:S(2)}) copy-start(f32[256,1024]{1,0:T(8,128)S(1)} %get-tuple-element.122) | copy-start | bytes 3145732
  281.5 2.3 copy-start.1
  281.5 4.0 copy-start.16
  281.5 2.2 copy-start.3
  376.8 2.4 copy-start.6
  379.2 1.2 copy-start.8
  382.4 1.0 copy-start.9
  382.4 151.2 %reduce-scatter.11.cloned.1.call-start = ((), (), s32[]{:S(2)}) async-start(), calls=%async_computation.7 | async-start | bytes 6488064 | tf_op jit(solution)/shard_map/reduce_scatter | solution.py:147
  383.4 1.0 copy-start.11
  388.7 0.6 copy-start.15
  388.7 145.8 %copy-start.7 = (f32[32,1536]{1,0:T(8,128)S(1)}, f32[32,1536]{1,0:T(8,128)}, u32[]{:S(2)}) copy-start(f32[32,1536]{1,0:T(8,128)} %reduce-scatter.5.cloned.1.call-done) | copy-start | bytes 589828
  388.7 145.8 %copy-start.13 = (f32[32,1536]{1,0:T(8,128)S(1)}, f32[32,1536]{1,0:T(8,128)}, u32[]{:S(2)}) copy-start(f32[32,1536]{1,0:T(8,128)} %reduce-scatter.7.cloned.1.call-done) | copy-start | bytes 589828
  388.7 462.4 %all-reduce.3.cloned.1.call-start = ((), (), s32[]{:S(2)}) async-start(), calls=%async_computation.8 | async-start | bytes 1572864 | tf_op jit(solution)/shard_map/psum | solution.py:181
  560.1 1.2 copy-start.12
  560.4 290.8 %copy-start.5 = (f32[2,128,768]{2,1,0:T(8,128)S(1)}, f32[2,128,768]{2,1,0:T(8,128)}, u32[]{:S(2)}) copy-start(f32[2,128,768]{2,1,0:T(8,128)} %param.13) | copy-start | bytes 2359300
Sparse Core Ops, SparseCore 0:
  12.2 42.2 reduce-scatter.4
  57.0 42.2 reduce-scatter.6
  102.4 57.8 all-gather.12
  163.3 56.6 all-gather.14
  382.5 34.6 reduce-scatter.8
  421.1 112.4 reduce-scatter.10
  561.5 289.6 all-reduce.2
where the time goes:
time: 903 us; the launch traced here: 896 us
  waiting for transfers between devices  526 us (58%)
  blocking collectives  307 us (34%)
  other arithmetic  22.3 us (2%)
  between operations  17.3 us (2%)
  matrix products  12.9 us (1%)
  local copies, waits for them, and re-layouts  9.31 us (1%)
    psum x1, waiting for transfers between devices, body(): hess = lax.psum(partial_hess, 'dp') + DAMPING * direction  289 us
    all_gather x4, blocking collectives, merged(): pieces = jax.tree.map(lambda part: lax.all_gather(part, axis), value)  116 us
    reduce_scatter x1, waiting for transfers between devices, body(): lax.psum_scatter(jnp.concatenate([LOGIT_SCALE * jnp.einsum('ic,ip->cp', p...  115 us
    psum x1, blocking collectives, body(): col_dot = lax.psum(jnp.sum(statistics_col_w * tscores, 0), 'dp')  76.6 us
    reduce_scatter x1, waiting for transfers between devices, body(): lax.psum_scatter(embed_term(tangent_pairs), 'mp', scatter_dimension=0, ti...  43.5 us
    reduce_scatter x1, waiting for transfers between devices, body(): lax.psum_scatter(embed_term(primal_pairs), 'mp', scatter_dimension=0, til...  39.3 us
    reduce_scatter x1, waiting for transfers between devices, body(): lax.psum_scatter(jnp.concatenate([LOGIT_SCALE * jnp.dot(plain, cols_p, pr...  27.4 us
    all_gather x1, blocking collectives, body(): piece = lax.all_gather(tdz, 'mp', axis=0, tiled=True)  24.4 us
  transfers between devices with their start and end apart: 7, of which 6 were waited for; matrix products, arithmetic and copies ran while one was open for 2% of the time, Pallas kernels for 0%

commit v1 on v0

v1 whole, which is shorter than its diff:
```python
import functools

import jax
import jax.numpy as jnp
from jax import lax
from jax.experimental import pallas as pl
from jax.experimental.pallas import tpu as pltpu
from jax.sharding import PartitionSpec as P

LOGIT_SCALE = 100.0
DAMPING = 1.0
EPSILON = 1e-06

NC, NY, NH, NX, NL = 2, 4, 4, 4, 2
NM = NX * NL
ROWS, DEPTH, WIDTH = 256, 1024, 768
PART = DEPTH // NM
SHARE = ROWS // NM
COLS = SHARE * NC * NY * NH
HALF = COLS // NC
PAIRS = ROWS * NC * NY * NH
TILE = 256
SEMS = 224
F32, BF16 = jnp.float32, jnp.bfloat16
MESH = pl.DeviceIdType.MESH


def dot(left, right, dims=((1,), (0,))):
    return lax.dot_general(left, right, (dims, ((), ())), preferred_element_type=F32)


def unit_of(raw):
    inverse = lax.rsqrt(jnp.sum(raw * raw, -1, keepdims=True) + EPSILON)
    return raw * inverse, inverse


def turn_of(tangent, unit, inverse):
    along = jnp.sum(unit * tangent, -1, keepdims=True)
    return (tangent - unit * along) * inverse, along


def pack_lanes(columns):
    size = columns[0].shape[0]
    lane = lax.broadcasted_iota(jnp.int32, (size, 128), 1)
    wide = jnp.zeros((size, 128), F32)
    for place, column in enumerate(columns):
        wide = jnp.where(lane == place, column, wide)
    return wide.T[0:8]


def unpack_lanes(rows):
    return jnp.concatenate([rows, jnp.zeros((120, rows.shape[1]), F32)], 0).T


def stack_rows(rows):
    size = rows[0].shape[1]
    return jnp.concatenate(list(rows) + [jnp.zeros((8 - len(rows), size), F32)], 0)


def softmax_join(slots):
    top = functools.reduce(jnp.maximum, [slot[0] for slot in slots])
    total = 0.0
    weighted = 0.0
    for slot in slots:
        factor = jnp.exp(slot[0] - top)
        total = total + factor * slot[1]
        weighted = weighted + factor * slot[2]
    return top, total, weighted


def kernel(
    feats, proj, direc, resid, solu,
    out_sol, out_res, out_dir,
    weights, rawbuf, tanbuf, rows_u, rows_t, cols_u, cols_t,
    scores, left_ts, right_ts, dsc, tdsc, cvec,
    row_slots, core_stat, y_stat, z_stat,
    grad_slots, core_grad, y_grad, z_grad,
    row_part, row_recv, col_part, col_recv, y_recv, z_recv,
    grad_cols, grad_rows, tdz, part_hess, core_hess, y_hess, z_hess, hess,
    scal_m, scal_c, scal_y, scal_z, norm_m, norm_c, norm_y, norm_z,
    send_sem, recv_sem,
):
    dp, mp = lax.axis_index("dp"), lax.axis_index("mp")
    c, y, zh = dp % NC, (dp // NC) % NY, dp // (NC * NY)
    x, zl = mp % NX, mp // NX
    counter = [0]

    def device(core=None, row=None, high=None, model=None):
        core, row, high = c if core is None else core, y if row is None else row, zh if high is None else high
        return {"dp": (high * NY + row) * NC + core, "mp": mp if model is None else model}

    def m_at(step):
        return ((zl + step // NX) % NL) * NX + (x + step % NX) % NX

    def m_from(step):
        return ((zl + step // NX) % NL) * NX + (x + NX - step % NX) % NX

    def y_at(step):
        return (y + step) % NY

    def h_at(step):
        return (zh + step) % NH

    def send(source, target, where):
        place = counter[0]
        counter[0] += 1
        copy = pltpu.make_async_remote_copy(
            src_ref=source, dst_ref=target, send_sem=send_sem.at[place], recv_sem=recv_sem.at[place],
            device_id=where, device_id_type=MESH,
        )
        copy.start()
        pending.append(copy)
        return copy

    pending = []

    def arrive(copies):
        for copy in copies:
            copy.wait_recv()

    def over_m(source, target):
        return [send(source(m_at(q)), target(q), device(model=m_at(q))) for q in range(1, NM)]

    def over_y(source, target):
        return [send(source(y_at(q)), target(q), device(row=y_at(q))) for q in range(1, NY)]

    def over_h(source, target):
        return [send(source(h_at(q)), target(q), device(high=h_at(q))) for q in range(1, NH)]

    def over_c(source, target):
        return [send(source, target, device(core=1 - c))]

    barrier = pltpu.get_barrier_semaphore()
    for q in range(1, NM):
        pl.semaphore_signal(barrier, inc=1, device_id=device(model=m_at(q)), device_id_type=MESH)
    for q in range(1, NY):
        pl.semaphore_signal(barrier, inc=1, device_id=device(row=y_at(q)), device_id_type=MESH)
    for q in range(1, NH):
        pl.semaphore_signal(barrier, inc=1, device_id=device(high=h_at(q)), device_id_type=MESH)
    pl.semaphore_signal(barrier, inc=1, device_id=device(core=1 - c), device_id_type=MESH)
    pl.semaphore_wait(barrier, NM + NY + NH - 2)

    for tower in range(2):
        weights[0, tower, pl.ds(mp, 1)] = proj[tower][None]
        weights[1, tower, pl.ds(mp, 1)] = direc[tower].astype(BF16)[None]

    def fetch(kind):
        return over_m(lambda m: weights.at[kind, c, mp], lambda q: weights.at[kind, c, mp])

    def hand_over(kind, copies):
        passed = []
        for q, copy in enumerate(copies, 1):
            copy.wait_recv()
            block = weights.at[kind, c, m_from(q)]
            passed += over_c(block, block)
        return passed

    def embed(kind, into):
        for tile in range(WIDTH // TILE):
            span = slice(tile * TILE, (tile + 1) * TILE)
            total = jnp.zeros((ROWS, TILE), F32)
            other = jnp.zeros((SHARE, TILE), F32)
            for block in range(0, NM, 2):
                deep = slice(block * PART, (block + 2) * PART)
                piece = weights[kind, 0, block : block + 2, :, span].reshape(2 * PART, TILE)
                total += dot(feats[0, :, deep], piece)
                piece = weights[kind, 1, block : block + 2, :, span].reshape(2 * PART, TILE)
                other += dot(feats[1, pl.ds(pl.multiple_of(mp * SHARE, SHARE), SHARE), deep], piece)
            into[0:ROWS, span] = total
            into[ROWS : ROWS + SHARE, span] = other

    first = fetch(0)
    passed = hand_over(0, first)
    second = fetch(1)
    arrive(passed)
    embed(0, rawbuf)
    unit_all, inverse_all = unit_of(rawbuf[...])
    low = unit_all.astype(BF16)
    rows_u[...] = low[0:ROWS]
    cols_u[c, y, zh] = low[ROWS : ROWS + SHARE]

    def columns_high(cols):
        block = cols.at[c, y, zh]
        return over_h(lambda h: block, lambda q: block)

    def columns_row(cols):
        block = cols.at[c, y]
        return over_y(lambda r: block, lambda q: block)

    def columns_core(cols, copies):
        passed = over_c(cols.at[c, y], cols.at[c, y])
        for q, copy in enumerate(copies, 1):
            copy.wait_recv()
            block = cols.at[c, (y + NY - q) % NY]
            passed += over_c(block, block)
        return passed

    copies = columns_high(cols_u)
    arrive(copies)
    copies = columns_row(cols_u)
    passed_t = hand_over(1, second)
    passed_u = columns_core(cols_u, copies)
    arrive(passed_t)
    embed(1, tanbuf)
    unit_all, inverse_all = unit_of(rawbuf[...])
    turned_all, along_all = turn_of(tanbuf[...], unit_all, inverse_all)
    low = turned_all.astype(BF16)
    rows_t[...] = low[0:ROWS]
    cols_t[c, y, zh] = low[ROWS : ROWS + SHARE]
    slope = inverse_all * along_all
    copies = columns_high(cols_t)
    first_col = pl.multiple_of(((c * NY + y) * NH + zh) * SHARE, SHARE)
    cvec[...] = jnp.zeros_like(cvec)
    cvec[pl.ds(first_col, SHARE)] = jnp.broadcast_to(slope[ROWS : ROWS + SHARE], (SHARE, 128))
    slope_row = cvec[...].T[0:1]
    row_slope = slope[0:ROWS]
    own = pl.ds(pl.multiple_of(mp * SHARE, SHARE), SHARE)
    arrive(passed_u)
    arrive(copies)
    copies = columns_row(cols_t)

    def column_tile(cols, tile):
        return cols[tile // 2, (tile % 2) * 2 : (tile % 2) * 2 + 2].reshape(TILE, WIDTH)

    NT = ((1,), (1,))
    tiles = COLS // TILE
    for tile in range(tiles):
        span = slice(tile * TILE, (tile + 1) * TILE)
        piece = column_tile(cols_u, tile)
        scores[:, span] = LOGIT_SCALE * dot(rows_u[...], piece, NT)
        left_ts[:, span] = LOGIT_SCALE * dot(rows_t[...], piece, NT)
    passed = columns_core(cols_t, copies)
    row_max = jnp.max(scores[...], 1, keepdims=True)
    col_max = jnp.max(scores[...], 0, keepdims=True)
    arrive(passed)
    for tile in range(tiles):
        span = slice(tile * TILE, (tile + 1) * TILE)
        right_ts[:, span] = LOGIT_SCALE * dot(rows_u[...], column_tile(cols_t, tile), NT)

    row_sum = jnp.zeros((ROWS, 1), F32)
    row_weighted = jnp.zeros((ROWS, 1), F32)
    col_sum, col_weighted = [], []
    for tile in range(tiles):
        span = slice(tile * TILE, (tile + 1) * TILE)
        score = scores[:, span]
        tscore = left_ts[:, span] + right_ts[:, span]
        weight = jnp.exp(score - row_max)
        row_sum += jnp.sum(weight, 1, keepdims=True)
        row_weighted += jnp.sum(weight * tscore, 1, keepdims=True)
        weight = jnp.exp(score - col_max[:, span])
        col_sum.append(jnp.sum(weight, 0, keepdims=True))
        col_weighted.append(jnp.sum(weight * tscore, 0, keepdims=True))
    resid_norm = jnp.sum(resid[...] * resid[...])
    direc_norm = jnp.sum(direc[...] * direc[...])
    constant = lambda value: jnp.full((ROWS, 1), value, F32)
    row_slots[pl.ds(mp, 1)] = pack_lanes(
        [row_max, row_sum, row_weighted, constant(resid_norm), constant(direc_norm)]
    )[None]
    core_stat[pl.ds(c, 1)] = stack_rows(
        [col_max, jnp.concatenate(col_sum, 1), jnp.concatenate(col_weighted, 1), slope_row]
    )[None]

    def join_columns(slots, count):
        parts = [slots[k] for k in range(count)]
        top, total, weighted = softmax_join([(part[0:1], part[1:2], part[2:3]) for part in parts])
        slopes = functools.reduce(jnp.add, [part[3:4] for part in parts])
        return top, total, weighted, slopes

    def sum_slots(slots, count):
        return functools.reduce(jnp.add, [slots[k] for k in range(count)])

    def spread_c(slots):
        return over_c(slots.at[c], slots.at[c])

    def spread_y(slots):
        return over_y(lambda r: slots.at[y], lambda q: slots.at[y])

    def spread_h(slots):
        return over_h(lambda h: slots.at[zh], lambda q: slots.at[zh])

    def spread_m(slots):
        return over_m(lambda m: slots.at[mp], lambda q: slots.at[mp])

    copies = spread_c(core_stat)
    row_copies = spread_m(row_slots)
    arrive(copies)
    y_stat[pl.ds(y, 1)] = stack_rows(join_columns(core_stat, NC))[None]
    copies = spread_y(y_stat)
    arrive(copies)
    z_stat[pl.ds(zh, 1)] = stack_rows(join_columns(y_stat, NY))[None]
    copies = spread_h(z_stat)
    arrive(row_copies)
    parts = [row_slots[k] for k in range(NM)]
    top, total, weighted = softmax_join([(part[0:1], part[1:2], part[2:3]) for part in parts])
    norms = functools.reduce(jnp.add, [part[3:5] for part in parts])
    norm_old = norms[0:1, 0:1]
    norm_direc = norms[1:2, 0:1]
    row_info = unpack_lanes(stack_rows([top + jnp.log(total), weighted / total]))
    row_lse, row_dot = row_info[:, 0:1], row_info[:, 1:2]
    arrive(copies)
    top, total, weighted, slopes = join_columns(z_stat, NH)
    col_lse, col_dot = top + jnp.log(total), weighted / total
    col_slope = unpack_lanes(stack_rows([slopes]))

    row_ids = lax.broadcasted_iota(jnp.int32, (ROWS, TILE), 0)
    col_ids = lax.broadcasted_iota(jnp.int32, (ROWS, TILE), 1)
    offset = mp * SHARE - first_col
    row_along = jnp.zeros((ROWS, 1), F32)
    row_turned = jnp.zeros((ROWS, 1), F32)
    col_along, col_turned = [], []
    for tile in range(tiles):
        span = slice(tile * TILE, (tile + 1) * TILE)
        score = scores[:, span]
        left, right = left_ts[:, span], right_ts[:, span]
        tscore = left + right
        row_w = jnp.exp(score - row_lse)
        col_w = jnp.exp(score - col_lse[:, span])
        place = col_ids + tile * TILE
        mine = (place >= first_col) & (place < first_col + SHARE) & (row_ids == place + offset)
        low = ((row_w + col_w - 2.0 * mine.astype(F32)) / (2.0 * PAIRS)).astype(BF16)
        dsc[:, span] = low
        tdsc[:, span] = (
            (row_w * (tscore - row_dot) + col_w * (tscore - col_dot[:, span])) / (2.0 * PAIRS)
        ).astype(BF16)
        wide = low.astype(F32)
        row_along += jnp.sum(wide * score, 1, keepdims=True)
        row_turned += jnp.sum(wide * left, 1, keepdims=True)
        col_along.append(jnp.sum(wide * score, 0, keepdims=True))
        col_turned.append(jnp.sum(wide * right, 0, keepdims=True))
    grad_slots[pl.ds(mp, 1)] = pack_lanes([row_along, row_turned])[None]
    core_grad[pl.ds(c, 1)] = stack_rows([jnp.concatenate(col_along, 1), jnp.concatenate(col_turned, 1)])[None]
    grad_copies = spread_m(grad_slots)
    core_copies = spread_c(core_grad)

    TN = ((0,), (0,))
    cvec[...] = col_slope

    def column_terms(tile):
        start = pl.multiple_of(tile * TILE, TILE)
        d_low, t_low = dsc[:, pl.ds(start, TILE)], tdsc[:, pl.ds(start, TILE)]
        total = dot(t_low, rows_u[...], TN) + dot(d_low, rows_t[...], TN)
        total -= cvec[pl.ds(start, TILE), 0:1] * dot(d_low, rows_u[...], TN)
        return LOGIT_SCALE * total

    half_tiles = HALF // TILE
    passed = []
    for tile in range(half_tiles):
        terms = column_terms((1 - c) * half_tiles + tile)
        block = col_part.at[0, tile]
        block[...] = terms.reshape(block.shape)
        passed += over_c(block, col_recv.at[tile])
    for tile in range(half_tiles):
        terms = column_terms(c * half_tiles + tile)
        col_part[1, tile] = terms.reshape(col_part.shape[2:])
    for tile in range(half_tiles):
        passed[tile].wait_recv()
        col_part[1, tile] += col_recv[tile]
    copies = over_y(lambda r: col_part.at[1, r // 2, r % 2], lambda q: y_recv.at[q - 1])
    arrive(core_copies)
    y_grad[pl.ds(y, 1)] = sum_slots(core_grad, NC)[None]
    y_copies = spread_y(y_grad)

    for tile in range(WIDTH // TILE):
        span = slice(tile * TILE, (tile + 1) * TILE)
        u_piece = cols_u[:, :, :, :, span].reshape(COLS, TILE)
        t_piece = cols_t[:, :, :, :, span].reshape(COLS, TILE)
        total = dot(tdsc[...], u_piece) + dot(dsc[...], t_piece) - row_slope * dot(dsc[...], u_piece)
        row_part[:, :, span] = (LOGIT_SCALE * total).reshape(NM, SHARE, TILE)
    row_copies = over_m(lambda m: row_part.at[m], lambda q: row_recv.at[q - 1])

    arrive(y_copies)
    z_grad[pl.ds(zh, 1)] = sum_slots(y_grad, NY)[None]
    z_copies = spread_h(z_grad)
    arrive(grad_copies)
    grad_rows[...] = unpack_lanes(sum_slots(grad_slots, NM))
    arrive(copies)
    col_total = col_part[1, y // 2, y % 2] + y_recv[0] + y_recv[1] + y_recv[2]
    col_part[1, y // 2, y % 2] = col_total
    copies = over_h(lambda h: col_part.at[1, y // 2, y % 2, h], lambda q: z_recv.at[q - 1])
    arrive(z_copies)
    grad_cols[...] = unpack_lanes(sum_slots(z_grad, NH))

    def finish(raw, tangent, value, info):
        unit, inverse = unit_of(raw)
        turned, _ = turn_of(tangent, unit, inverse)
        mixed = info[:, 1:2] + jnp.sum(unit * value, -1, keepdims=True)
        return ((value - turned * info[:, 0:1] - unit * mixed) * inverse).astype(BF16)

    arrive(row_copies)
    value = row_part[mp]
    for q in range(NM - 1):
        value = value + row_recv[q]
    tdz[0, mp] = finish(rawbuf[own], tanbuf[own], value, grad_rows[own])
    arrive(copies)
    value = col_part[1, y // 2, y % 2, zh] + z_recv[0] + z_recv[1] + z_recv[2]
    tdz[1, mp] = finish(
        rawbuf[ROWS : ROWS + SHARE], tanbuf[ROWS : ROWS + SHARE], value, grad_cols[pl.ds(first_col, SHARE)]
    )
    copies = over_m(lambda m: tdz.at[:, mp], lambda q: tdz.at[:, mp])
    arrive(copies)

    curve = 0.0
    for tower in range(2):
        part = dot(feats[tower, :, pl.ds(pl.multiple_of(mp * PART, PART), PART)], tdz[tower].reshape(ROWS, WIDTH), TN)
        part_hess[tower] = part.reshape(part_hess.shape[1:])
        curve += jnp.sum(direc[tower] * part)
    passed = over_c(part_hess.at[1 - c], core_hess)
    scal_m[pl.ds(mp, 1)] = jnp.full((1, 8, 128), curve, F32)
    scal_copies = spread_m(scal_m)
    arrive(passed)
    part_hess[pl.ds(c, 1)] += core_hess[...][None]
    copies = over_y(lambda r: part_hess.at[c, r], lambda q: y_hess.at[q - 1])
    arrive(scal_copies)
    scal_c[pl.ds(c, 1)] = sum_slots(scal_m, NM)[None]
    scal_copies = spread_c(scal_c)
    arrive(scal_copies)
    scal_y[pl.ds(y, 1)] = sum_slots(scal_c, NC)[None]
    scal_copies = spread_y(scal_y)
    arrive(copies)
    part_hess[c, y] += y_hess[0] + y_hess[1] + y_hess[2]
    copies = over_h(lambda h: part_hess.at[c, y, h], lambda q: z_hess.at[q - 1])
    arrive(scal_copies)
    scal_z[pl.ds(zh, 1)] = sum_slots(scal_y, NY)[None]
    scal_copies = spread_h(scal_z)
    arrive(copies)
    hess[c, y, zh] = part_hess[c, y, zh] + z_hess[0] + z_hess[1] + z_hess[2]
    copies = over_h(lambda h: hess.at[c, y, zh], lambda q: hess.at[c, y, zh])
    arrive(scal_copies)
    curve = sum_slots(scal_z, NH)[0:1, 0:1] + DAMPING * norm_direc
    alpha = norm_old / curve
    piece = pl.ds(pl.multiple_of((y * NH + zh) * 8, 8), 8)
    after = resid[c, piece] - alpha * (hess[c, y, zh] + DAMPING * direc[c, piece])
    norm_m[pl.ds(mp, 1)] = jnp.full((1, 8, 128), jnp.sum(after * after), F32)
    scal_copies = spread_m(norm_m)
    arrive(copies)
    block = hess.at[c, y]
    copies = over_y(lambda r: block, lambda q: block)
    out_sol[...] = solu[...] + alpha * direc[...]
    arrive(scal_copies)
    norm_c[pl.ds(c, 1)] = sum_slots(norm_m, NM)[None]
    scal_copies = spread_c(norm_c)
    arrive(scal_copies)
    norm_y[pl.ds(y, 1)] = sum_slots(norm_c, NC)[None]
    scal_copies = spread_y(norm_y)
    arrive(copies)
    copies = over_c(hess.at[c], hess.at[c])
    arrive(scal_copies)
    norm_z[pl.ds(zh, 1)] = sum_slots(norm_y, NY)[None]
    scal_copies = spread_h(norm_z)
    arrive(copies)
    after = resid[...] - alpha * (hess[...].reshape(2, PART, WIDTH) + DAMPING * direc[...])
    out_res[...] = after
    arrive(scal_copies)
    norm_new = sum_slots(norm_z, NH)[0:1, 0:1]
    out_dir[...] = after + norm_new / norm_old * direc[...]
    for copy in pending:
        copy.wait_send()
    assert counter[0] <= SEMS


def body(features, projections, solution, residual, direction):
    vmem = pl.BlockSpec(memory_space=pltpu.VMEM)
    shape = jax.ShapeDtypeStruct((2, PART, WIDTH), F32)
    f32 = lambda *size: pltpu.VMEM(size, F32)
    bf16 = lambda *size: pltpu.VMEM(size, BF16)
    scratch = [
        bf16(2, 2, NM, PART, WIDTH),
        f32(ROWS + SHARE, WIDTH), f32(ROWS + SHARE, WIDTH),
        bf16(ROWS, WIDTH), bf16(ROWS, WIDTH),
        bf16(NC, NY, NH, SHARE, WIDTH), bf16(NC, NY, NH, SHARE, WIDTH),
        f32(ROWS, COLS), f32(ROWS, COLS), f32(ROWS, COLS),
        bf16(ROWS, COLS), bf16(ROWS, COLS), f32(COLS, 128),
        f32(NM, 8, ROWS), f32(NC, 8, COLS), f32(NY, 8, COLS), f32(NH, 8, COLS),
        f32(NM, 8, ROWS), f32(NC, 8, COLS), f32(NY, 8, COLS), f32(NH, 8, COLS),
        f32(NM, SHARE, WIDTH), f32(NM - 1, SHARE, WIDTH),
        f32(2, 2, 2, NH, SHARE, WIDTH), f32(2, 2, NH, SHARE, WIDTH),
        f32(NY - 1, NH, SHARE, WIDTH), f32(NH - 1, SHARE, WIDTH),
        f32(COLS, 128), f32(ROWS, 128),
        bf16(2, NM, SHARE, WIDTH),
        f32(2, NY, NH, 8, WIDTH), f32(NY, NH, 8, WIDTH),
        f32(NY - 1, NH, 8, WIDTH), f32(NH - 1, 8, WIDTH), f32(2, NY, NH, 8, WIDTH),
        f32(NM, 8, 128), f32(NC, 8, 128), f32(NY, 8, 128), f32(NH, 8, 128),
        f32(NM, 8, 128), f32(NC, 8, 128), f32(NY, 8, 128), f32(NH, 8, 128),
        pltpu.SemaphoreType.DMA((SEMS,)), pltpu.SemaphoreType.DMA((SEMS,)),
    ]
    return pl.pallas_call(
        kernel,
        name="cg_step",
        out_shape=(shape, shape, shape),
        in_specs=[vmem] * 5,
        out_specs=(vmem, vmem, vmem),
        scratch_shapes=scratch,
        compiler_params=pltpu.CompilerParams(
            collective_id=0, has_side_effects=True, vmem_limit_bytes=60 * 2**20
        ),
    )(features, projections, direction, residual, solution)


def solution(mesh):
    placed = (
        P(None, "dp", None),
        P(None, "mp", None),
        P(None, "mp", None),
        P(None, "mp", None),
        P(None, "mp", None),
    )
    return jax.shard_map(
        body,
        mesh=mesh,
        in_specs=placed,
        out_specs=(P(None, "mp", None), P(None, "mp", None), P(None, "mp", None)),
        check_vma=False,
    )
```

time: 903 us -> 182 us (0.20)
  waiting for transfers between devices: 526 us -> 0 us
  blocking collectives: 307 us -> 0 us
  Pallas kernels: 0 us -> 175 us
  other arithmetic: 22.3 us -> 0 us
  between operations: 17.3 us -> 0.65 us
  matrix products: 12.9 us -> 0 us
    psum x1 -> x0, waiting for transfers between devices: 289 us -> none  [body(): hess = lax.psum(partial_hess, 'dp') + DAMPING * direction]
    reduce_scatter x4 -> x0, waiting for transfers between devices: 226 us -> none  [the longest x1 115 us: body(): lax.psum_scatter(jnp.concatenate([LOGIT_SCALE * jnp.einsum('ic,ip->cp', p...]
    all_gather x7 -> x0, blocking collectives: 187 us -> none  [the longest x4 116 us: merged(): pieces = jax.tree.map(lambda part: lax.all_gather(part, axis), value)]
    pallas_call x0 -> x1, Pallas kernels: none -> 175 us  [body(): pl.pallas_call(kernel, name='cg_step', out_shape=(shape, shape, shape), i...]
    psum x4 -> x0, blocking collectives: 120 us -> none  [the longest x1 76.6 us: body(): col_dot = lax.psum(jnp.sum(statistics_col_w * tscores, 0), 'dp')]
    dot_general x15 -> x0, matrix products: 12.9 us -> none  [the longest x3 5.98 us: inner(): jnp.einsum('ip,jp->ij', left_mat, right_mat, preferred_element_type=jnp.f...]
    all_gather x2 -> x0, waiting for transfers between devices: 11 us -> none  [the longest x1 10.9 us: body(): cols_p = lax.all_gather(unit_low[:, 1], 'dp', axis=0, tiled=True)]
  transfers between devices with their start and end apart: 7 -> 0, of which waited for: 6 -> 0; matrix products, arithmetic and copies ran while one was open for 2% -> 0% of each run, Pallas kernels for 0% -> 0%
where the time goes in v1:
time: 182 us; the launch traced here: 180 us
  Pallas kernels  175 us (96%)
  local copies, waits for them, and re-layouts  4.44 us (2%)
    pallas_call x1, Pallas kernels, body(): pl.pallas_call(kernel, name='cg_step', out_shape=(shape, shape, shape), i...  175 us
    unnamed x7, local copies, waits for them, and re-layouts  4.44 us

profile of v1, /device:TPU:1, one launch (start us, length us, event | category | flops | bytes accessed | tf_op | source)
XLA Modules:
  0.0 180.2 jit_solution(17149225139266156950)
XLA Ops:
  0.6 175.2 %cg_step.1 = (f32[2,128,768]{2,1,0:T(8,128)}, f32[2,128,768]{2,1,0:T(8,128)}, f32[2,128,768]{2,1,0:T(8,128)}) custom-call(bf16[2,256,1024]{2,1,0:T(8,128)(2,1)} %feats.1, bf16[2,128,768]{2,1,0:T(8,128)(2,1)} %proj.1, f32[2,128,768]{2,1,0:T(8,128)} %direc.1, f32[2,128,768]{2,1,0:T(8,128)} %resid.1, f32[2,128,768]{2,1,0:T(8,128)} %solu.1), custom_call_target="tpu_custom_call" | custom-call | tf_op jit(solution)/shard_map/cg_step/pallas_call | solution.py:486
  175.8 0.0 copy-start.1
  175.8 2.1 %copy.11 = f32[2,128,768]{2,1,0:T(8,128)} copy(f32[2,128,768]{2,1,0:T(8,128)} %get-tuple-element.6) | data formatting | bytes 1572864
  177.9 0.0 copy-done.1
  177.9 0.0 copy-start
  178.0 0.9 copy.12
  178.8 0.5 copy-done
  179.4 0.9 copy.13
Async XLA Ops:
  175.8 2.1 %copy-start.1 = (f32[2,128,768]{2,1,0:T(8,128)S(1)}, f32[2,128,768]{2,1,0:T(8,128)}, u32[]{:S(2)}) copy-start(f32[2,128,768]{2,1,0:T(8,128)} %get-tuple-element.7) | copy-start | bytes 2359300
  177.9 1.4 copy-start

commit v2 on v1

--- a/solution.py
+++ b/solution.py
@@ -21,6 +21,8 @@
 PAIRS = ROWS * NC * NY * NH
 TILE = 256
 SEMS = 224
+QUARTER = 16
+DIRECT = PART - NY * QUARTER
 F32, BF16 = jnp.float32, jnp.bfloat16
 MESH = pl.DeviceIdType.MESH
 
@@ -69,16 +71,16 @@
 
 
 def kernel(
-    feats, proj, direc, resid, solu,
-    out_sol, out_res, out_dir,
-    weights, rawbuf, tanbuf, rows_u, rows_t, cols_u, cols_t,
+    feats_in, proj_in, direc_in, resid_in,
+    hess_out, info_out,
+    feats, direc, resid, weights, quarters, rawbuf, tanbuf, rows_u, rows_t, cols_u, cols_t,
     scores, left_ts, right_ts, dsc, tdsc, cvec,
     row_slots, core_stat, y_stat, z_stat,
     grad_slots, core_grad, y_grad, z_grad,
     row_part, row_recv, col_part, col_recv, y_recv, z_recv,
     grad_cols, grad_rows, tdz, part_hess, core_hess, y_hess, z_hess, hess,
     scal_m, scal_c, scal_y, scal_z, norm_m, norm_c, norm_y, norm_z,
-    send_sem, recv_sem,
+    send_sem, recv_sem, load_sem,
 ):
     dp, mp = lax.axis_index("dp"), lax.axis_index("mp")
     c, y, zh = dp % NC, (dp // NC) % NY, dp // (NC * NY)
@@ -130,6 +132,16 @@
     def over_c(source, target):
         return [send(source, target, device(core=1 - c))]
 
+    def load(source, target, place):
+        copy = pltpu.make_async_copy(source, target, load_sem.at[place])
+        copy.start()
+        return copy
+
+    load_direc = [load(direc_in.at[tower], direc.at[tower], tower) for tower in (1, 0)]
+    load_proj = [load(proj_in.at[tower], weights.at[0, tower, mp], 2 + tower) for tower in (1, 0)]
+    load_feats = [load(feats_in.at[tower], feats.at[tower], 4 + tower) for tower in (1, 0)]
+    load_resid = load(resid_in, resid, 6)
+
     barrier = pltpu.get_barrier_semaphore()
     for q in range(1, NM):
         pl.semaphore_signal(barrier, inc=1, device_id=device(model=m_at(q)), device_id_type=MESH)
@@ -138,46 +150,58 @@
     for q in range(1, NH):
         pl.semaphore_signal(barrier, inc=1, device_id=device(high=h_at(q)), device_id_type=MESH)
     pl.semaphore_signal(barrier, inc=1, device_id=device(core=1 - c), device_id_type=MESH)
+    load_direc[0].wait()
+    weights[1, 1, pl.ds(mp, 1)] = direc[1].astype(BF16)[None]
+    load_proj[0].wait()
     pl.semaphore_wait(barrier, NM + NY + NH - 2)
 
-    for tower in range(2):
-        weights[0, tower, pl.ds(mp, 1)] = proj[tower][None]
-        weights[1, tower, pl.ds(mp, 1)] = direc[tower].astype(BF16)[None]
-
-    def fetch(kind):
-        return over_m(lambda m: weights.at[kind, c, mp], lambda q: weights.at[kind, c, mp])
-
-    def hand_over(kind, copies):
-        passed = []
-        for q, copy in enumerate(copies, 1):
-            copy.wait_recv()
-            block = weights.at[kind, c, m_from(q)]
-            passed += over_c(block, block)
-        return passed
-
-    def embed(kind, into):
+    part = weights.at[c, 1, mp, pl.ds(pl.multiple_of(DIRECT + y * QUARTER, QUARTER), QUARTER)]
+    quarter_copies = over_m(lambda m: part, lambda q: quarters.at[c, y, q - 1])
+    whole = weights.at[c, 1, mp, pl.ds(0, DIRECT)]
+    direct_copies = over_m(lambda m: whole, lambda q: whole)
+    load_direc[1].wait()
+    weights[1, 0, pl.ds(mp, 1)] = direc[0].astype(BF16)[None]
+    load_proj[1].wait()
+    arrive(quarter_copies)
+    mine = quarters.at[c, y]
+    row_copies = over_y(lambda r: mine, lambda q: mine)
+    passed = over_c(mine, mine)
+    for q, copy in enumerate(direct_copies, 1):
+        copy.wait_recv()
+        block = weights.at[c, 1, m_from(q), pl.ds(0, DIRECT)]
+        passed += over_c(block, block)
+
+    whole_sar = weights.at[c, 0, mp]
+    sar_copies = over_m(lambda m: whole_sar, lambda q: whole_sar)
+    for q, copy in enumerate(row_copies, 1):
+        copy.wait_recv()
+        block = quarters.at[c, (y + NY - q) % NY]
+        passed += over_c(block, block)
+    load_feats[0].wait()
+    arrive(passed)
+    for kind in range(2):
+        for q in range(1, NM):
+            for r in range(NY):
+                weights[kind, 1, m_from(q), DIRECT + r * QUARTER : DIRECT + (r + 1) * QUARTER] = quarters[kind, r, q - 1]
+
+    def embed(kind, tower, rows, into, first):
         for tile in range(WIDTH // TILE):
             span = slice(tile * TILE, (tile + 1) * TILE)
-            total = jnp.zeros((ROWS, TILE), F32)
-            other = jnp.zeros((SHARE, TILE), F32)
+            total = 0.0
             for block in range(0, NM, 2):
                 deep = slice(block * PART, (block + 2) * PART)
-                piece = weights[kind, 0, block : block + 2, :, span].reshape(2 * PART, TILE)
-                total += dot(feats[0, :, deep], piece)
-                piece = weights[kind, 1, block : block + 2, :, span].reshape(2 * PART, TILE)
-                other += dot(feats[1, pl.ds(pl.multiple_of(mp * SHARE, SHARE), SHARE), deep], piece)
-            into[0:ROWS, span] = total
-            into[ROWS : ROWS + SHARE, span] = other
-
-    first = fetch(0)
-    passed = hand_over(0, first)
-    second = fetch(1)
-    arrive(passed)
-    embed(0, rawbuf)
-    unit_all, inverse_all = unit_of(rawbuf[...])
-    low = unit_all.astype(BF16)
-    rows_u[...] = low[0:ROWS]
-    cols_u[c, y, zh] = low[ROWS : ROWS + SHARE]
+                piece = weights[kind, tower, block : block + 2, :, span].reshape(2 * PART, TILE)
+                total += dot(feats[tower, rows, deep], piece)
+            into[first : first + total.shape[0], span] = total
+
+    own = pl.ds(pl.multiple_of(mp * SHARE, SHARE), SHARE)
+    embed(0, 1, own, rawbuf, ROWS)
+    embed(1, 1, own, tanbuf, ROWS)
+    unit, inverse = unit_of(rawbuf[ROWS : ROWS + SHARE])
+    turned, along = turn_of(tanbuf[ROWS : ROWS + SHARE], unit, inverse)
+    cols_u[c, y, zh] = unit.astype(BF16)
+    cols_t[c, y, zh] = turned.astype(BF16)
+    slope = inverse * along
 
     def columns_high(cols):
         block = cols.at[c, y, zh]
@@ -195,29 +219,34 @@
             passed += over_c(block, block)
         return passed
 
-    copies = columns_high(cols_u)
-    arrive(copies)
-    copies = columns_row(cols_u)
-    passed_t = hand_over(1, second)
-    passed_u = columns_core(cols_u, copies)
-    arrive(passed_t)
-    embed(1, tanbuf)
-    unit_all, inverse_all = unit_of(rawbuf[...])
-    turned_all, along_all = turn_of(tanbuf[...], unit_all, inverse_all)
-    low = turned_all.astype(BF16)
-    rows_t[...] = low[0:ROWS]
-    cols_t[c, y, zh] = low[ROWS : ROWS + SHARE]
-    slope = inverse_all * along_all
-    copies = columns_high(cols_t)
+    high_u = columns_high(cols_u)
+    high_t = columns_high(cols_t)
     first_col = pl.multiple_of(((c * NY + y) * NH + zh) * SHARE, SHARE)
     cvec[...] = jnp.zeros_like(cvec)
-    cvec[pl.ds(first_col, SHARE)] = jnp.broadcast_to(slope[ROWS : ROWS + SHARE], (SHARE, 128))
+    cvec[pl.ds(first_col, SHARE)] = jnp.broadcast_to(slope, (SHARE, 128))
     slope_row = cvec[...].T[0:1]
-    row_slope = slope[0:ROWS]
-    own = pl.ds(pl.multiple_of(mp * SHARE, SHARE), SHARE)
+    arrive(high_u)
+    copies_u = columns_row(cols_u)
+    arrive(high_t)
+    copies_t = columns_row(cols_t)
+    passed_u = columns_core(cols_u, copies_u)
+    passed = []
+    for q, copy in enumerate(sar_copies, 1):
+        copy.wait_recv()
+        block = weights.at[c, 0, m_from(q)]
+        passed += over_c(block, block)
+    load_feats[1].wait()
+    arrive(passed)
+    passed_t = columns_core(cols_t, copies_t)
+    every = slice(0, ROWS)
+    embed(0, 0, every, rawbuf, 0)
+    embed(1, 0, every, tanbuf, 0)
+    unit, inverse = unit_of(rawbuf[every])
+    turned, along = turn_of(tanbuf[every], unit, inverse)
+    rows_u[...] = unit.astype(BF16)
+    rows_t[...] = turned.astype(BF16)
+    row_slope = inverse * along
     arrive(passed_u)
-    arrive(copies)
-    copies = columns_row(cols_t)
 
     def column_tile(cols, tile):
         return cols[tile // 2, (tile % 2) * 2 : (tile % 2) * 2 + 2].reshape(TILE, WIDTH)
@@ -229,10 +258,9 @@
         piece = column_tile(cols_u, tile)
         scores[:, span] = LOGIT_SCALE * dot(rows_u[...], piece, NT)
         left_ts[:, span] = LOGIT_SCALE * dot(rows_t[...], piece, NT)
-    passed = columns_core(cols_t, copies)
     row_max = jnp.max(scores[...], 1, keepdims=True)
     col_max = jnp.max(scores[...], 0, keepdims=True)
-    arrive(passed)
+    arrive(passed_t)
     for tile in range(tiles):
         span = slice(tile * TILE, (tile + 1) * TILE)
         right_ts[:, span] = LOGIT_SCALE * dot(rows_u[...], column_tile(cols_t, tile), NT)
@@ -250,6 +278,7 @@
         weight = jnp.exp(score - col_max[:, span])
         col_sum.append(jnp.sum(weight, 0, keepdims=True))
         col_weighted.append(jnp.sum(weight * tscore, 0, keepdims=True))
+    load_resid.wait()
     resid_norm = jnp.sum(resid[...] * resid[...])
     direc_norm = jnp.sum(direc[...] * direc[...])
     constant = lambda value: jnp.full((ROWS, 1), value, F32)
@@ -435,7 +464,6 @@
     arrive(copies)
     block = hess.at[c, y]
     copies = over_y(lambda r: block, lambda q: block)
-    out_sol[...] = solu[...] + alpha * direc[...]
     arrive(scal_copies)
     norm_c[pl.ds(c, 1)] = sum_slots(norm_m, NM)[None]
     scal_copies = spread_c(norm_c)
@@ -448,11 +476,12 @@
     norm_z[pl.ds(zh, 1)] = sum_slots(norm_y, NY)[None]
     scal_copies = spread_h(norm_z)
     arrive(copies)
-    after = resid[...] - alpha * (hess[...].reshape(2, PART, WIDTH) + DAMPING * direc[...])
-    out_res[...] = after
-    arrive(scal_copies)
+    arrive(scal_copies)
+    store = load(hess, hess_out, 7)
     norm_new = sum_slots(norm_z, NH)[0:1, 0:1]
-    out_dir[...] = after + norm_new / norm_old * direc[...]
+    first_row = lax.broadcasted_iota(jnp.int32, (8, 128), 0) == 0
+    info_out[...] = jnp.where(first_row, alpha, norm_new / norm_old)
+    store.wait()
     for copy in pending:
         copy.wait_send()
     assert counter[0] <= SEMS
@@ -460,11 +489,12 @@
 
 def body(features, projections, solution, residual, direction):
     vmem = pl.BlockSpec(memory_space=pltpu.VMEM)
-    shape = jax.ShapeDtypeStruct((2, PART, WIDTH), F32)
+    hbm = pl.BlockSpec(memory_space=pl.ANY)
     f32 = lambda *size: pltpu.VMEM(size, F32)
     bf16 = lambda *size: pltpu.VMEM(size, BF16)
     scratch = [
-        bf16(2, 2, NM, PART, WIDTH),
+        bf16(2, ROWS, DEPTH), f32(2, PART, WIDTH), f32(2, PART, WIDTH),
+        bf16(2, 2, NM, PART, WIDTH), bf16(2, NY, NM - 1, QUARTER, WIDTH),
         f32(ROWS + SHARE, WIDTH), f32(ROWS + SHARE, WIDTH),
         bf16(ROWS, WIDTH), bf16(ROWS, WIDTH),
         bf16(NC, NY, NH, SHARE, WIDTH), bf16(NC, NY, NH, SHARE, WIDTH),
@@ -481,19 +511,26 @@
         f32(NY - 1, NH, 8, WIDTH), f32(NH - 1, 8, WIDTH), f32(2, NY, NH, 8, WIDTH),
         f32(NM, 8, 128), f32(NC, 8, 128), f32(NY, 8, 128), f32(NH, 8, 128),
         f32(NM, 8, 128), f32(NC, 8, 128), f32(NY, 8, 128), f32(NH, 8, 128),
-        pltpu.SemaphoreType.DMA((SEMS,)), pltpu.SemaphoreType.DMA((SEMS,)),
+        pltpu.SemaphoreType.DMA((SEMS,)), pltpu.SemaphoreType.DMA((SEMS,)), pltpu.SemaphoreType.DMA((8,)),
     ]
-    return pl.pallas_call(
+    hess, info = pl.pallas_call(
         kernel,
         name="cg_step",
-        out_shape=(shape, shape, shape),
-        in_specs=[vmem] * 5,
-        out_specs=(vmem, vmem, vmem),
+        out_shape=(
+            jax.ShapeDtypeStruct((2, NY, NH, 8, WIDTH), F32),
+            jax.ShapeDtypeStruct((8, 128), F32),
+        ),
+        in_specs=[hbm] * 4,
+        out_specs=(hbm, vmem),
         scratch_shapes=scratch,
         compiler_params=pltpu.CompilerParams(
             collective_id=0, has_side_effects=True, vmem_limit_bytes=60 * 2**20
         ),
-    )(features, projections, direction, residual, solution)
+    )(features, projections, direction, residual)
+    alpha, beta = info[0, 0], info[1, 0]
+    hess = hess.reshape(direction.shape) + DAMPING * direction
+    new_residual = residual - alpha * hess
+    return solution + alpha * direction, new_residual, new_residual + beta * direction
 
 
 def solution(mesh):

time: 182 us -> 172 us (0.945)
  Pallas kernels: 175 us -> 165 us
  other arithmetic: 0 us -> 3.96 us
  local copies, waits for them, and re-layouts: 4.44 us -> 1.35 us
    pallas_call x1, Pallas kernels: 175 us -> 165 us  [body(): pl.pallas_call(kernel, name='cg_step', out_shape=(jax.ShapeDtypeStruct((2...]
    unnamed x7 -> x6, local copies, waits for them, and re-layouts: 4.44 us -> 0.01 us
    add x0 -> x1, other arithmetic: none -> 3.96 us  [body(): new_residual + beta * direction]
where the time goes in v2:
time: 172 us; the launch traced here: 171 us
  Pallas kernels  165 us (96%)
  other arithmetic  3.96 us (2%)
    pallas_call x1, Pallas kernels, body(): pl.pallas_call(kernel, name='cg_step', out_shape=(jax.ShapeDtypeStruct((2...  165 us
    add x1, other arithmetic, body(): new_residual + beta * direction  3.96 us

profile of v2, /device:TPU:1, one launch (start us, length us, event | category | flops | bytes accessed | tf_op | source)
XLA Modules:
  0.0 170.9 jit_solution(1930830697296095393)
XLA Ops:
  0.6 0.0 copy-start
  0.6 0.0 copy-start.1
  0.7 0.0 copy-start.2
  0.7 164.9 %cg_step.1 = (f32[2,4,4,8,768]{4,3,2,1,0:T(8,128)}, f32[8,128]{1,0:T(8,128)}) custom-call(bf16[2,256,1024]{2,1,0:T(8,128)(2,1)} %feats_in.1, bf16[2,128,768]{2,1,0:T(8,128)(2,1)} %proj_in.1, f32[2,128,768]{2,1,0:T(8,128)} %direc_in.1, f32[2,128,768]{2,1,0:T(8,128)} %resid_in.1), custom_call_target="tpu_custom_call" | custom-call | tf_op jit(solution)/shard_map/cg_step/pallas_call | solution.py:516
  165.6 1.3 fusion.3
  166.9 0.0 copy-done
  166.9 0.0 copy-done.1
  167.0 0.0 copy-done.2
  167.0 4.0 %multiply_add_fusion = (f32[2,128,768]{2,1,0:T(8,128)}, f32[2,128,768]{2,1,0:T(8,128)}, f32[2,128,768]{2,1,0:T(8,128)}) fusion(f32[2,128,768]{2,1,0:T(8,128)S(1)} %copy-done, f32[]{:T(128)} %bitcast.2, f32[2,128,768]{2,1,0:T(8,128)S(1)} %copy-done.1, f32[2,4,4,8,768]{4,3,2,1,0:T(8,128)} %get-tuple-element.6, f32[]{:T(128)} %bitcast, ...), kind=kLoop, calls=%fused_computation.3 | loop fusion | flops 1376256 | bytes 5505032 | tf_op jit(solution)/shard_map/add | solution.py:533
Async XLA Ops:
  0.6 166.3 %copy-start = (f32[2,128,768]{2,1,0:T(8,128)S(1)}, f32[2,128,768]{2,1,0:T(8,128)}, u32[]{:S(2)}) copy-start(f32[2,128,768]{2,1,0:T(8,128)} %direc_in.1) | copy-start | bytes 2359300
  0.6 166.3 %copy-start.1 = (f32[2,128,768]{2,1,0:T(8,128)S(1)}, f32[2,128,768]{2,1,0:T(8,128)}, u32[]{:S(2)}) copy-start(f32[2,128,768]{2,1,0:T(8,128)} %resid_in.1) | copy-start | bytes 2359300
  0.7 166.3 %copy-start.2 = (f32[2,128,768]{2,1,0:T(8,128)S(1)}, f32[2,128,768]{2,1,0:T(8,128)}, u32[]{:S(2)}) copy-start(f32[2,128,768]{2,1,0:T(8,128)} %param.7) | copy-start | bytes 2359300

commit v3 on v2

--- a/solution.py
+++ b/solution.py
@@ -23,6 +23,8 @@
 SEMS = 224
 QUARTER = 16
 DIRECT = PART - NY * QUARTER
+WIDE = WIDTH // 2
+BLOCK = PART // NY
 F32, BF16 = jnp.float32, jnp.bfloat16
 MESH = pl.DeviceIdType.MESH
 
@@ -51,12 +53,17 @@
 
 
 def unpack_lanes(rows):
-    return jnp.concatenate([rows, jnp.zeros((120, rows.shape[1]), F32)], 0).T
-
-
-def stack_rows(rows):
-    size = rows[0].shape[1]
-    return jnp.concatenate(list(rows) + [jnp.zeros((8 - len(rows), size), F32)], 0)
+    return jnp.concatenate([rows, jnp.zeros((128 - rows.shape[0], rows.shape[1]), F32)], 0).T
+
+
+def fold(rows):
+    size = rows[0].shape[1] * len(rows) // 8
+    stacked = jnp.concatenate(rows, 0)
+    return jnp.concatenate([stacked[:, k : k + size] for k in range(0, stacked.shape[1], size)], 0)
+
+
+def unfold(block, count):
+    return jnp.concatenate([block[k : k + count] for k in range(0, 8, count)], 1)
 
 
 def softmax_join(slots):
@@ -77,14 +84,15 @@
     scores, left_ts, right_ts, dsc, tdsc, cvec,
     row_slots, core_stat, y_stat, z_stat,
     grad_slots, core_grad, y_grad, z_grad,
-    row_part, row_recv, col_part, col_recv, y_recv, z_recv,
+    row_part, x_recv, l_recv, col_part, col_recv, y_recv, z_recv,
     grad_cols, grad_rows, tdz, part_hess, core_hess, y_hess, z_hess, hess,
-    scal_m, scal_c, scal_y, scal_z, norm_m, norm_c, norm_y, norm_z,
+    scal_m, scal_p, scal_z, norm_p, norm_m,
     send_sem, recv_sem, load_sem,
 ):
     dp, mp = lax.axis_index("dp"), lax.axis_index("mp")
     c, y, zh = dp % NC, (dp // NC) % NY, dp // (NC * NY)
     x, zl = mp % NX, mp // NX
+    partner = (1 - zl) * NX + x
     counter = [0]
 
     def device(core=None, row=None, high=None, model=None):
@@ -96,6 +104,9 @@
 
     def m_from(step):
         return ((zl + step // NX) % NL) * NX + (x + NX - step % NX) % NX
+
+    def x_at(step):
+        return (x + step) % NX
 
     def y_at(step):
         return (y + step) % NY
@@ -129,6 +140,18 @@
     def over_h(source, target):
         return [send(source(h_at(q)), target(q), device(high=h_at(q))) for q in range(1, NH)]
 
+    def over_x(source, target):
+        return [send(source(x_at(q)), target(q), device(model=zl * NX + x_at(q))) for q in range(1, NX)]
+
+    def over_l(source, target):
+        return [send(source, target, device(model=partner))]
+
+    def over_plane(slots):
+        place = slots.at[c * NY + y]
+        return [
+            send(place, place, device(core=(c + q // NY) % NC, row=(y + q % NY) % NY)) for q in range(1, NC * NY)
+        ]
+
     def over_c(source, target):
         return [send(source, target, device(core=1 - c))]
 
@@ -145,34 +168,52 @@
     barrier = pltpu.get_barrier_semaphore()
     for q in range(1, NM):
         pl.semaphore_signal(barrier, inc=1, device_id=device(model=m_at(q)), device_id_type=MESH)
-    for q in range(1, NY):
-        pl.semaphore_signal(barrier, inc=1, device_id=device(row=y_at(q)), device_id_type=MESH)
+    for q in range(1, NC * NY):
+        where = device(core=(c + q // NY) % NC, row=(y + q % NY) % NY)
+        pl.semaphore_signal(barrier, inc=1, device_id=where, device_id_type=MESH)
     for q in range(1, NH):
         pl.semaphore_signal(barrier, inc=1, device_id=device(high=h_at(q)), device_id_type=MESH)
-    pl.semaphore_signal(barrier, inc=1, device_id=device(core=1 - c), device_id_type=MESH)
     load_direc[0].wait()
     weights[1, 1, pl.ds(mp, 1)] = direc[1].astype(BF16)[None]
     load_proj[0].wait()
-    pl.semaphore_wait(barrier, NM + NY + NH - 2)
+    pl.semaphore_wait(barrier, NM + NC * NY + NH - 3)
 
     part = weights.at[c, 1, mp, pl.ds(pl.multiple_of(DIRECT + y * QUARTER, QUARTER), QUARTER)]
     quarter_copies = over_m(lambda m: part, lambda q: quarters.at[c, y, q - 1])
-    whole = weights.at[c, 1, mp, pl.ds(0, DIRECT)]
-    direct_copies = over_m(lambda m: whole, lambda q: whole)
+    def optical(m):
+        return weights.at[c, 1, m, pl.ds(0, DIRECT)]
+
+    def sar(m):
+        return weights.at[c, 0, m]
+
+    def spread_x(block):
+        return over_x(lambda m: block, lambda q: block)
+
+    def pass_on(blocks, low, copies):
+        passed = []
+        for q, copy in enumerate(copies, 1):
+            copy.wait_recv()
+            block = blocks(low * NX + (x + NX - q) % NX)
+            passed += over_c(block, block)
+        return passed
+
+    l_copies = over_l(optical(mp), optical(mp))
+    x_copies = spread_x(optical(mp))
     load_direc[1].wait()
     weights[1, 0, pl.ds(mp, 1)] = direc[0].astype(BF16)[None]
     load_proj[1].wait()
+    sar_l_copies = over_l(sar(mp), sar(mp))
     arrive(quarter_copies)
     mine = quarters.at[c, y]
     row_copies = over_y(lambda r: mine, lambda q: mine)
-    passed = over_c(mine, mine)
-    for q, copy in enumerate(direct_copies, 1):
-        copy.wait_recv()
-        block = weights.at[c, 1, m_from(q), pl.ds(0, DIRECT)]
-        passed += over_c(block, block)
-
-    whole_sar = weights.at[c, 0, mp]
-    sar_copies = over_m(lambda m: whole_sar, lambda q: whole_sar)
+    arrive(l_copies)
+    x_relays = spread_x(optical(partner))
+    passed = over_c(mine, mine) + over_c(optical(partner), optical(partner))
+    passed += pass_on(optical, zl, x_copies)
+    sar_x_copies = spread_x(sar(mp))
+    passed += pass_on(optical, 1 - zl, x_relays)
+    arrive(sar_l_copies)
+    sar_x_relays = spread_x(sar(partner))
     for q, copy in enumerate(row_copies, 1):
         copy.wait_recv()
         block = quarters.at[c, (y + NY - q) % NY]
@@ -230,11 +271,9 @@
     arrive(high_t)
     copies_t = columns_row(cols_t)
     passed_u = columns_core(cols_u, copies_u)
-    passed = []
-    for q, copy in enumerate(sar_copies, 1):
-        copy.wait_recv()
-        block = weights.at[c, 0, m_from(q)]
-        passed += over_c(block, block)
+    passed = over_c(sar(partner), sar(partner))
+    passed += pass_on(sar, zl, sar_x_copies)
+    passed += pass_on(sar, 1 - zl, sar_x_relays)
     load_feats[1].wait()
     arrive(passed)
     passed_t = columns_core(cols_t, copies_t)
@@ -285,12 +324,12 @@
     row_slots[pl.ds(mp, 1)] = pack_lanes(
         [row_max, row_sum, row_weighted, constant(resid_norm), constant(direc_norm)]
     )[None]
-    core_stat[pl.ds(c, 1)] = stack_rows(
+    core_stat[pl.ds(c, 1)] = fold(
         [col_max, jnp.concatenate(col_sum, 1), jnp.concatenate(col_weighted, 1), slope_row]
     )[None]
 
     def join_columns(slots, count):
-        parts = [slots[k] for k in range(count)]
+        parts = [unfold(slots[k], 4) for k in range(count)]
         top, total, weighted = softmax_join([(part[0:1], part[1:2], part[2:3]) for part in parts])
         slopes = functools.reduce(jnp.add, [part[3:4] for part in parts])
         return top, total, weighted, slopes
@@ -313,10 +352,10 @@
     copies = spread_c(core_stat)
     row_copies = spread_m(row_slots)
     arrive(copies)
-    y_stat[pl.ds(y, 1)] = stack_rows(join_columns(core_stat, NC))[None]
+    y_stat[pl.ds(y, 1)] = fold(join_columns(core_stat, NC))[None]
     copies = spread_y(y_stat)
     arrive(copies)
-    z_stat[pl.ds(zh, 1)] = stack_rows(join_columns(y_stat, NY))[None]
+    z_stat[pl.ds(zh, 1)] = fold(join_columns(y_stat, NY))[None]
     copies = spread_h(z_stat)
     arrive(row_copies)
     parts = [row_slots[k] for k in range(NM)]
@@ -324,12 +363,12 @@
     norms = functools.reduce(jnp.add, [part[3:5] for part in parts])
     norm_old = norms[0:1, 0:1]
     norm_direc = norms[1:2, 0:1]
-    row_info = unpack_lanes(stack_rows([top + jnp.log(total), weighted / total]))
+    row_info = unpack_lanes(jnp.concatenate([top + jnp.log(total), weighted / total], 0))
     row_lse, row_dot = row_info[:, 0:1], row_info[:, 1:2]
     arrive(copies)
     top, total, weighted, slopes = join_columns(z_stat, NH)
     col_lse, col_dot = top + jnp.log(total), weighted / total
-    col_slope = unpack_lanes(stack_rows([slopes]))
+    col_slope = unpack_lanes(slopes)
 
     row_ids = lax.broadcasted_iota(jnp.int32, (ROWS, TILE), 0)
     col_ids = lax.broadcasted_iota(jnp.int32, (ROWS, TILE), 1)
@@ -357,57 +396,67 @@
         col_along.append(jnp.sum(wide * score, 0, keepdims=True))
         col_turned.append(jnp.sum(wide * right, 0, keepdims=True))
     grad_slots[pl.ds(mp, 1)] = pack_lanes([row_along, row_turned])[None]
-    core_grad[pl.ds(c, 1)] = stack_rows([jnp.concatenate(col_along, 1), jnp.concatenate(col_turned, 1)])[None]
+    core_grad[pl.ds(c, 1)] = fold([jnp.concatenate(col_along, 1), jnp.concatenate(col_turned, 1)])[None]
     grad_copies = spread_m(grad_slots)
     core_copies = spread_c(core_grad)
 
     TN = ((0,), (0,))
     cvec[...] = col_slope
 
-    def column_terms(tile):
+    def column_terms(tile, half):
         start = pl.multiple_of(tile * TILE, TILE)
         d_low, t_low = dsc[:, pl.ds(start, TILE)], tdsc[:, pl.ds(start, TILE)]
-        total = dot(t_low, rows_u[...], TN) + dot(d_low, rows_t[...], TN)
-        total -= cvec[pl.ds(start, TILE), 0:1] * dot(d_low, rows_u[...], TN)
+        span = slice(half * WIDE, (half + 1) * WIDE)
+        total = dot(t_low, rows_u[:, span], TN) + dot(d_low, rows_t[:, span], TN)
+        total -= cvec[pl.ds(start, TILE), 0:1] * dot(d_low, rows_u[:, span], TN)
         return LOGIT_SCALE * total
 
     half_tiles = HALF // TILE
     passed = []
-    for tile in range(half_tiles):
-        terms = column_terms((1 - c) * half_tiles + tile)
-        block = col_part.at[0, tile]
-        block[...] = terms.reshape(block.shape)
-        passed += over_c(block, col_recv.at[tile])
-    for tile in range(half_tiles):
-        terms = column_terms(c * half_tiles + tile)
-        col_part[1, tile] = terms.reshape(col_part.shape[2:])
-    for tile in range(half_tiles):
-        passed[tile].wait_recv()
-        col_part[1, tile] += col_recv[tile]
-    copies = over_y(lambda r: col_part.at[1, r // 2, r % 2], lambda q: y_recv.at[q - 1])
+    for half in range(2):
+        for tile in range(half_tiles):
+            terms = column_terms((1 - c) * half_tiles + tile, half)
+            block = col_part.at[half, 0, tile]
+            block[...] = terms.reshape(block.shape)
+            passed += over_c(block, col_recv.at[half, tile])
+    y_copies = []
+    for half in range(2):
+        for tile in range(half_tiles):
+            terms = column_terms(c * half_tiles + tile, half).reshape(col_part.shape[3:])
+            passed[half * half_tiles + tile].wait_recv()
+            col_part[half, 1, tile] = terms + col_recv[half, tile]
+        y_copies.append(
+            over_y(lambda r: col_part.at[half, 1, r // 2, r % 2], lambda q: y_recv.at[half, q - 1])
+        )
     arrive(core_copies)
     y_grad[pl.ds(y, 1)] = sum_slots(core_grad, NC)[None]
-    y_copies = spread_y(y_grad)
+    y_grad_copies = spread_y(y_grad)
 
     for tile in range(WIDTH // TILE):
         span = slice(tile * TILE, (tile + 1) * TILE)
         u_piece = cols_u[:, :, :, :, span].reshape(COLS, TILE)
         t_piece = cols_t[:, :, :, :, span].reshape(COLS, TILE)
         total = dot(tdsc[...], u_piece) + dot(dsc[...], t_piece) - row_slope * dot(dsc[...], u_piece)
-        row_part[:, :, span] = (LOGIT_SCALE * total).reshape(NM, SHARE, TILE)
-    row_copies = over_m(lambda m: row_part.at[m], lambda q: row_recv.at[q - 1])
-
-    arrive(y_copies)
+        row_part[:, :, :, span] = (LOGIT_SCALE * total).reshape(NL, NX, SHARE, TILE)
+    x_copies = over_x(lambda k: row_part.at[:, k], lambda q: x_recv.at[q - 1])
+
+    arrive(y_grad_copies)
     z_grad[pl.ds(zh, 1)] = sum_slots(y_grad, NY)[None]
-    z_copies = spread_h(z_grad)
+    z_grad_copies = spread_h(z_grad)
+
+    def column_high(half):
+        arrive(y_copies[half])
+        here = col_part[half, 1, y // 2, y % 2]
+        col_part[half, 1, y // 2, y % 2] = here + y_recv[half, 0] + y_recv[half, 1] + y_recv[half, 2]
+        return over_h(lambda h: col_part.at[half, 1, y // 2, y % 2, h], lambda q: z_recv.at[half, q - 1])
+
+    high_first = column_high(0)
+    arrive(x_copies)
+    for low in range(NL):
+        row_part[low, x] += x_recv[0, low] + x_recv[1, low] + x_recv[2, low]
+    l_copies = over_l(row_part.at[1 - zl, x], l_recv)
     arrive(grad_copies)
     grad_rows[...] = unpack_lanes(sum_slots(grad_slots, NM))
-    arrive(copies)
-    col_total = col_part[1, y // 2, y % 2] + y_recv[0] + y_recv[1] + y_recv[2]
-    col_part[1, y // 2, y % 2] = col_total
-    copies = over_h(lambda h: col_part.at[1, y // 2, y % 2, h], lambda q: z_recv.at[q - 1])
-    arrive(z_copies)
-    grad_cols[...] = unpack_lanes(sum_slots(z_grad, NH))
 
     def finish(raw, tangent, value, info):
         unit, inverse = unit_of(raw)
@@ -415,21 +464,33 @@
         mixed = info[:, 1:2] + jnp.sum(unit * value, -1, keepdims=True)
         return ((value - turned * info[:, 0:1] - unit * mixed) * inverse).astype(BF16)
 
-    arrive(row_copies)
-    value = row_part[mp]
-    for q in range(NM - 1):
-        value = value + row_recv[q]
-    tdz[0, mp] = finish(rawbuf[own], tanbuf[own], value, grad_rows[own])
-    arrive(copies)
-    value = col_part[1, y // 2, y % 2, zh] + z_recv[0] + z_recv[1] + z_recv[2]
+    def spread_tdz(tower):
+        block = tdz.at[tower, mp]
+        return over_m(lambda m: block, lambda q: block)
+
+    high_second = column_high(1)
+    arrive(z_grad_copies)
+    grad_cols[...] = unpack_lanes(unfold(sum_slots(z_grad, NH), 2))
+    arrive(l_copies)
+    tdz[0, mp] = finish(rawbuf[own], tanbuf[own], row_part[zl, x] + l_recv[...], grad_rows[own])
+    sar_copies = spread_tdz(0)
+    arrive(high_first)
+    arrive(high_second)
+    halves = [
+        col_part[half, 1, y // 2, y % 2, zh] + z_recv[half, 0] + z_recv[half, 1] + z_recv[half, 2]
+        for half in range(2)
+    ]
     tdz[1, mp] = finish(
-        rawbuf[ROWS : ROWS + SHARE], tanbuf[ROWS : ROWS + SHARE], value, grad_cols[pl.ds(first_col, SHARE)]
+        rawbuf[ROWS : ROWS + SHARE],
+        tanbuf[ROWS : ROWS + SHARE],
+        jnp.concatenate(halves, 1),
+        grad_cols[pl.ds(first_col, SHARE)],
     )
-    copies = over_m(lambda m: tdz.at[:, mp], lambda q: tdz.at[:, mp])
-    arrive(copies)
+    optical_copies = spread_tdz(1)
 
     curve = 0.0
-    for tower in range(2):
+    for tower, copies in enumerate((sar_copies, optical_copies)):
+        arrive(copies)
         part = dot(feats[tower, :, pl.ds(pl.multiple_of(mp * PART, PART), PART)], tdz[tower].reshape(ROWS, WIDTH), TN)
         part_hess[tower] = part.reshape(part_hess.shape[1:])
         curve += jnp.sum(direc[tower] * part)
@@ -440,51 +501,54 @@
     part_hess[pl.ds(c, 1)] += core_hess[...][None]
     copies = over_y(lambda r: part_hess.at[c, r], lambda q: y_hess.at[q - 1])
     arrive(scal_copies)
-    scal_c[pl.ds(c, 1)] = sum_slots(scal_m, NM)[None]
-    scal_copies = spread_c(scal_c)
+    scal_p[pl.ds(c * NY + y, 1)] = sum_slots(scal_m, NM)[None]
+    scal_copies = over_plane(scal_p)
+    arrive(copies)
+    z_hess[zh] = part_hess[c, y] + y_hess[0] + y_hess[1] + y_hess[2]
+    copies = spread_h(z_hess)
     arrive(scal_copies)
-    scal_y[pl.ds(y, 1)] = sum_slots(scal_c, NC)[None]
-    scal_copies = spread_y(scal_y)
-    arrive(copies)
-    part_hess[c, y] += y_hess[0] + y_hess[1] + y_hess[2]
-    copies = over_h(lambda h: part_hess.at[c, y, h], lambda q: z_hess.at[q - 1])
-    arrive(scal_copies)
-    scal_z[pl.ds(zh, 1)] = sum_slots(scal_y, NY)[None]
+    scal_z[pl.ds(zh, 1)] = sum_slots(scal_p, NC * NY)[None]
     scal_copies = spread_h(scal_z)
     arrive(copies)
-    hess[c, y, zh] = part_hess[c, y, zh] + z_hess[0] + z_hess[1] + z_hess[2]
-    copies = over_h(lambda h: hess.at[c, y, zh], lambda q: hess.at[c, y, zh])
+    block_hess = sum_slots(z_hess, NH)
+    hess[c, y] = block_hess
+    block = hess.at[c, y]
+    copies = over_y(lambda r: block, lambda q: block)
     arrive(scal_copies)
     curve = sum_slots(scal_z, NH)[0:1, 0:1] + DAMPING * norm_direc
     alpha = norm_old / curve
-    piece = pl.ds(pl.multiple_of((y * NH + zh) * 8, 8), 8)
-    after = resid[c, piece] - alpha * (hess[c, y, zh] + DAMPING * direc[c, piece])
-    norm_m[pl.ds(mp, 1)] = jnp.full((1, 8, 128), jnp.sum(after * after), F32)
+    piece = pl.ds(pl.multiple_of(y * BLOCK, BLOCK), BLOCK)
+    after = resid[c, piece] - alpha * (block_hess + DAMPING * direc[c, piece])
+    norm_p[pl.ds(c * NY + y, 1)] = jnp.full((1, 8, 128), jnp.sum(after * after), F32)
+    scal_copies = over_plane(norm_p)
+    passed = over_c(block, block)
+    for q, copy in enumerate(copies, 1):
+        copy.wait_recv()
+        block = hess.at[c, (y + NY - q) % NY]
+        passed += over_c(block, block)
+    arrive(scal_copies)
+    norm_m[pl.ds(mp, 1)] = sum_slots(norm_p, NC * NY)[None]
     scal_copies = spread_m(norm_m)
-    arrive(copies)
-    block = hess.at[c, y]
-    copies = over_y(lambda r: block, lambda q: block)
+    arrive(passed)
+    store = load(hess, hess_out, 7)
     arrive(scal_copies)
-    norm_c[pl.ds(c, 1)] = sum_slots(norm_m, NM)[None]
-    scal_copies = spread_c(norm_c)
-    arrive(scal_copies)
-    norm_y[pl.ds(y, 1)] = sum_slots(norm_c, NC)[None]
-    scal_copies = spread_y(norm_y)
-    arrive(copies)
-    copies = over_c(hess.at[c], hess.at[c])
-    arrive(scal_copies)
-    norm_z[pl.ds(zh, 1)] = sum_slots(norm_y, NY)[None]
-    scal_copies = spread_h(norm_z)
-    arrive(copies)
-    arrive(scal_copies)
-    store = load(hess, hess_out, 7)
-    norm_new = sum_slots(norm_z, NH)[0:1, 0:1]
+    norm_new = sum_slots(norm_m, NM)[0:1, 0:1]
     first_row = lax.broadcasted_iota(jnp.int32, (8, 128), 0) == 0
     info_out[...] = jnp.where(first_row, alpha, norm_new / norm_old)
     store.wait()
     for copy in pending:
         copy.wait_send()
     assert counter[0] <= SEMS
+
+
+def last_kernel(info, hess, direc, resid, solu, out_sol, out_res, out_dir):
+    alpha, beta = info[0:1, 0:1], info[1:2, 0:1]
+    for tower in range(2):
+        direction = direc[tower]
+        out_sol[tower] = solu[tower] + alpha * direction
+        after = resid[tower] - alpha * (hess[tower] + DAMPING * direction)
+        out_res[tower] = after
+        out_dir[tower] = after + beta * direction
 
 
 def body(features, projections, solution, residual, direction):
@@ -500,24 +564,24 @@
         bf16(NC, NY, NH, SHARE, WIDTH), bf16(NC, NY, NH, SHARE, WIDTH),
         f32(ROWS, COLS), f32(ROWS, COLS), f32(ROWS, COLS),
         bf16(ROWS, COLS), bf16(ROWS, COLS), f32(COLS, 128),
-        f32(NM, 8, ROWS), f32(NC, 8, COLS), f32(NY, 8, COLS), f32(NH, 8, COLS),
-        f32(NM, 8, ROWS), f32(NC, 8, COLS), f32(NY, 8, COLS), f32(NH, 8, COLS),
-        f32(NM, SHARE, WIDTH), f32(NM - 1, SHARE, WIDTH),
-        f32(2, 2, 2, NH, SHARE, WIDTH), f32(2, 2, NH, SHARE, WIDTH),
-        f32(NY - 1, NH, SHARE, WIDTH), f32(NH - 1, SHARE, WIDTH),
+        f32(NM, 8, ROWS), f32(NC, 8, COLS // 2), f32(NY, 8, COLS // 2), f32(NH, 8, COLS // 2),
+        f32(NM, 8, ROWS), f32(NC, 8, COLS // 4), f32(NY, 8, COLS // 4), f32(NH, 8, COLS // 4),
+        f32(NL, NX, SHARE, WIDTH), f32(NX - 1, NL, SHARE, WIDTH), f32(SHARE, WIDTH),
+        f32(2, 2, 2, 2, NH, SHARE, WIDE), f32(2, 2, 2, NH, SHARE, WIDE),
+        f32(2, NY - 1, NH, SHARE, WIDE), f32(2, NH - 1, SHARE, WIDE),
         f32(COLS, 128), f32(ROWS, 128),
         bf16(2, NM, SHARE, WIDTH),
-        f32(2, NY, NH, 8, WIDTH), f32(NY, NH, 8, WIDTH),
-        f32(NY - 1, NH, 8, WIDTH), f32(NH - 1, 8, WIDTH), f32(2, NY, NH, 8, WIDTH),
-        f32(NM, 8, 128), f32(NC, 8, 128), f32(NY, 8, 128), f32(NH, 8, 128),
-        f32(NM, 8, 128), f32(NC, 8, 128), f32(NY, 8, 128), f32(NH, 8, 128),
+        f32(2, NY, BLOCK, WIDTH), f32(NY, BLOCK, WIDTH),
+        f32(NY - 1, BLOCK, WIDTH), f32(NH, BLOCK, WIDTH), f32(2, NY, BLOCK, WIDTH),
+        f32(NM, 8, 128), f32(NC * NY, 8, 128), f32(NH, 8, 128),
+        f32(NC * NY, 8, 128), f32(NM, 8, 128),
         pltpu.SemaphoreType.DMA((SEMS,)), pltpu.SemaphoreType.DMA((SEMS,)), pltpu.SemaphoreType.DMA((8,)),
     ]
     hess, info = pl.pallas_call(
         kernel,
         name="cg_step",
         out_shape=(
-            jax.ShapeDtypeStruct((2, NY, NH, 8, WIDTH), F32),
+            jax.ShapeDtypeStruct((2, NY, BLOCK, WIDTH), F32),
             jax.ShapeDtypeStruct((8, 128), F32),
         ),
         in_specs=[hbm] * 4,
@@ -527,10 +591,16 @@
             collective_id=0, has_side_effects=True, vmem_limit_bytes=60 * 2**20
         ),
     )(features, projections, direction, residual)
-    alpha, beta = info[0, 0], info[1, 0]
-    hess = hess.reshape(direction.shape) + DAMPING * direction
-    new_residual = residual - alpha * hess
-    return solution + alpha * direction, new_residual, new_residual + beta * direction
+    whole = pl.BlockSpec((2, BLOCK, WIDTH), lambda step: (0, step, 0))
+    shape = jax.ShapeDtypeStruct(direction.shape, F32)
+    return pl.pallas_call(
+        last_kernel,
+        name="updates",
+        grid=(NY,),
+        out_shape=(shape, shape, shape),
+        in_specs=[pl.BlockSpec((8, 128), lambda step: (0, 0))] + [whole] * 4,
+        out_specs=(whole, whole, whole),
+    )(info, hess.reshape(direction.shape), direction, residual, solution)
 
 
 def solution(mesh):

time: 172 us -> 152 us (0.88)
  Pallas kernels: 165 us -> 151 us
  other arithmetic: 3.96 us -> 0 us
    pallas_call x1, Pallas kernels: 165 us -> 147 us  [body(): pl.pallas_call(kernel, name='cg_step', out_shape=(jax.ShapeDtypeStruct((2...]
    pallas_call x0 -> x1, Pallas kernels: none -> 4.23 us  [body(): pl.pallas_call(last_kernel, name='updates', grid=(NY,), out_shape=(shape,...]
    add x1 -> x0, other arithmetic: 3.96 us -> none  [body(): new_residual + beta * direction]
where the time goes in v3:
time: 152 us
  Pallas kernels  151 us (99%)
    pallas_call x1, Pallas kernels, body(): pl.pallas_call(kernel, name='cg_step', out_shape=(jax.ShapeDtypeStruct((2...  147 us
    pallas_call x1, Pallas kernels, body(): pl.pallas_call(last_kernel, name='updates', grid=(NY,), out_shape=(shape,...  4.23 us

profile of v3, /device:TPU:1, one launch (start us, length us, event | category | flops | bytes accessed | tf_op | source)
XLA Modules:
  0.0 151.7 jit_solution(6675150600428772693)
XLA Ops:
  0.6 146.8 %cg_step.1 = (f32[2,4,32,768]{3,2,1,0:T(8,128)}, f32[8,128]{1,0:T(8,128)}) custom-call(bf16[2,256,1024]{2,1,0:T(8,128)(2,1)} %feats_in.1, bf16[2,128,768]{2,1,0:T(8,128)(2,1)} %proj_in.1, f32[2,128,768]{2,1,0:T(8,128)} %direc.1, f32[2,128,768]{2,1,0:T(8,128)} %resid.1), custom_call_target="tpu_custom_call" | custom-call | tf_op jit(solution)/shard_map/cg_step/pallas_call | solution.py:580
  147.5 4.2 %updates.1 = (f32[2,128,768]{2,1,0:T(8,128)}, f32[2,128,768]{2,1,0:T(8,128)}, f32[2,128,768]{2,1,0:T(8,128)}) custom-call(f32[8,128]{1,0:T(8,128)} %get-tuple-element.5.info, f32[2,128,768]{2,1,0:T(8,128)} %bitcast.1, f32[2,128,768]{2,1,0:T(8,128)} %direc.1, f32[2,128,768]{2,1,0:T(8,128)} %resid.1, f32[2,128,768]{2,1,0:T(8,128)} %solu.1), custom_call_target="tpu_custom_call" | custom-call | tf_op jit(solution)/shard_map/updates/pallas_call | solution.py:596

commit v4 on v3

--- a/solution.py
+++ b/solution.py
@@ -17,14 +17,14 @@
 PART = DEPTH // NM
 SHARE = ROWS // NM
 COLS = SHARE * NC * NY * NH
-HALF = COLS // NC
 PAIRS = ROWS * NC * NY * NH
 TILE = 256
 SEMS = 224
 QUARTER = 16
 DIRECT = PART - NY * QUARTER
-WIDE = WIDTH // 2
 BLOCK = PART // NY
+BLOCKS = SHARE * NY
+HALF = BLOCK // 2
 F32, BF16 = jnp.float32, jnp.bfloat16
 MESH = pl.DeviceIdType.MESH
 
@@ -80,11 +80,11 @@
 def kernel(
     feats_in, proj_in, direc_in, resid_in,
     hess_out, info_out,
-    feats, direc, resid, weights, quarters, rawbuf, tanbuf, rows_u, rows_t, cols_u, cols_t,
+    feats, direc, resid, weights, quarters, rawbuf, tanbuf, rows_u, rows_t, cols,
     scores, left_ts, right_ts, dsc, tdsc, cvec,
-    row_slots, core_stat, y_stat, z_stat,
-    grad_slots, core_grad, y_grad, z_grad,
-    row_part, x_recv, l_recv, col_part, col_recv, y_recv, z_recv,
+    row_slots, plane_stat, z_stat,
+    grad_slots, plane_grad, z_grad,
+    row_part, x_recv, l_recv, col_away, col_part, col_recv, y_recv, z_recv,
     grad_cols, grad_rows, tdz, part_hess, core_hess, y_hess, z_hess, hess,
     scal_m, scal_p, scal_z, norm_p, norm_m,
     send_sem, recv_sem, load_sem,
@@ -240,43 +240,47 @@
     embed(1, 1, own, tanbuf, ROWS)
     unit, inverse = unit_of(rawbuf[ROWS : ROWS + SHARE])
     turned, along = turn_of(tanbuf[ROWS : ROWS + SHARE], unit, inverse)
-    cols_u[c, y, zh] = unit.astype(BF16)
-    cols_t[c, y, zh] = turned.astype(BF16)
+    cols[c, zh, y, 0] = unit.astype(BF16)
+    cols[c, zh, y, 1] = turned.astype(BF16)
     slope = inverse * along
 
-    def columns_high(cols):
-        block = cols.at[c, y, zh]
-        return over_h(lambda h: block, lambda q: block)
-
-    def columns_row(cols):
-        block = cols.at[c, y]
-        return over_y(lambda r: block, lambda q: block)
-
-    def columns_core(cols, copies):
-        passed = over_c(cols.at[c, y], cols.at[c, y])
+    def column_block(high, row):
+        return cols.at[c, high, row]
+
+    def column_rows(high):
+        block = column_block(high, y)
+        return over_c(block, block), over_y(lambda r: block, lambda q: block)
+
+    def column_pass(high, copies):
+        passed = []
         for q, copy in enumerate(copies, 1):
             copy.wait_recv()
-            block = cols.at[c, (y + NY - q) % NY]
+            block = column_block(high, (y + NY - q) % NY)
             passed += over_c(block, block)
         return passed
 
-    high_u = columns_high(cols_u)
-    high_t = columns_high(cols_t)
-    first_col = pl.multiple_of(((c * NY + y) * NH + zh) * SHARE, SHARE)
+    mine = column_block(zh, y)
+    high_copies = over_h(lambda h: mine, lambda q: mine)
+    col_passed, copies = column_rows(zh)
+    waiting = [(zh, copies)]
+    first_col = pl.multiple_of(((c * NH + zh) * NY + y) * SHARE, SHARE)
     cvec[...] = jnp.zeros_like(cvec)
     cvec[pl.ds(first_col, SHARE)] = jnp.broadcast_to(slope, (SHARE, 128))
     slope_row = cvec[...].T[0:1]
-    arrive(high_u)
-    copies_u = columns_row(cols_u)
-    arrive(high_t)
-    copies_t = columns_row(cols_t)
-    passed_u = columns_core(cols_u, copies_u)
+    for q in (1, 3, 2):
+        high_copies[q - 1].wait_recv()
+        high = (zh + NH - q) % NH
+        passed, copies = column_rows(high)
+        col_passed += passed
+        waiting.append((high, copies))
+    col_passed += column_pass(*waiting[0])
     passed = over_c(sar(partner), sar(partner))
     passed += pass_on(sar, zl, sar_x_copies)
+    col_passed += column_pass(*waiting[1])
     passed += pass_on(sar, 1 - zl, sar_x_relays)
     load_feats[1].wait()
     arrive(passed)
-    passed_t = columns_core(cols_t, copies_t)
+    col_passed += column_pass(*waiting[2])
     every = slice(0, ROWS)
     embed(0, 0, every, rawbuf, 0)
     embed(1, 0, every, tanbuf, 0)
@@ -285,24 +289,24 @@
     rows_u[...] = unit.astype(BF16)
     rows_t[...] = turned.astype(BF16)
     row_slope = inverse * along
-    arrive(passed_u)
-
-    def column_tile(cols, tile):
-        return cols[tile // 2, (tile % 2) * 2 : (tile % 2) * 2 + 2].reshape(TILE, WIDTH)
+    col_passed += column_pass(*waiting[3])
+    arrive(col_passed)
+
+    def column_tile(kind, tile):
+        return cols[tile // 2, (tile % 2) * 2 : (tile % 2) * 2 + 2, :, kind].reshape(TILE, WIDTH)
 
     NT = ((1,), (1,))
     tiles = COLS // TILE
     for tile in range(tiles):
         span = slice(tile * TILE, (tile + 1) * TILE)
-        piece = column_tile(cols_u, tile)
+        piece = column_tile(0, tile)
         scores[:, span] = LOGIT_SCALE * dot(rows_u[...], piece, NT)
         left_ts[:, span] = LOGIT_SCALE * dot(rows_t[...], piece, NT)
     row_max = jnp.max(scores[...], 1, keepdims=True)
     col_max = jnp.max(scores[...], 0, keepdims=True)
-    arrive(passed_t)
     for tile in range(tiles):
         span = slice(tile * TILE, (tile + 1) * TILE)
-        right_ts[:, span] = LOGIT_SCALE * dot(rows_u[...], column_tile(cols_t, tile), NT)
+        right_ts[:, span] = LOGIT_SCALE * dot(rows_u[...], column_tile(1, tile), NT)
 
     row_sum = jnp.zeros((ROWS, 1), F32)
     row_weighted = jnp.zeros((ROWS, 1), F32)
@@ -324,7 +328,7 @@
     row_slots[pl.ds(mp, 1)] = pack_lanes(
         [row_max, row_sum, row_weighted, constant(resid_norm), constant(direc_norm)]
     )[None]
-    core_stat[pl.ds(c, 1)] = fold(
+    plane_stat[pl.ds(c * NY + y, 1)] = fold(
         [col_max, jnp.concatenate(col_sum, 1), jnp.concatenate(col_weighted, 1), slope_row]
     )[None]
 
@@ -337,25 +341,16 @@
     def sum_slots(slots, count):
         return functools.reduce(jnp.add, [slots[k] for k in range(count)])
 
-    def spread_c(slots):
-        return over_c(slots.at[c], slots.at[c])
-
-    def spread_y(slots):
-        return over_y(lambda r: slots.at[y], lambda q: slots.at[y])
-
     def spread_h(slots):
         return over_h(lambda h: slots.at[zh], lambda q: slots.at[zh])
 
     def spread_m(slots):
         return over_m(lambda m: slots.at[mp], lambda q: slots.at[mp])
 
-    copies = spread_c(core_stat)
+    copies = over_plane(plane_stat)
     row_copies = spread_m(row_slots)
     arrive(copies)
-    y_stat[pl.ds(y, 1)] = fold(join_columns(core_stat, NC))[None]
-    copies = spread_y(y_stat)
-    arrive(copies)
-    z_stat[pl.ds(zh, 1)] = fold(join_columns(y_stat, NY))[None]
+    z_stat[pl.ds(zh, 1)] = fold(join_columns(plane_stat, NC * NY))[None]
     copies = spread_h(z_stat)
     arrive(row_copies)
     parts = [row_slots[k] for k in range(NM)]
@@ -396,61 +391,55 @@
         col_along.append(jnp.sum(wide * score, 0, keepdims=True))
         col_turned.append(jnp.sum(wide * right, 0, keepdims=True))
     grad_slots[pl.ds(mp, 1)] = pack_lanes([row_along, row_turned])[None]
-    core_grad[pl.ds(c, 1)] = fold([jnp.concatenate(col_along, 1), jnp.concatenate(col_turned, 1)])[None]
+    plane_grad[pl.ds(c * NY + y, 1)] = fold([jnp.concatenate(col_along, 1), jnp.concatenate(col_turned, 1)])[None]
     grad_copies = spread_m(grad_slots)
-    core_copies = spread_c(core_grad)
+    plane_copies = over_plane(plane_grad)
 
     TN = ((0,), (0,))
     cvec[...] = col_slope
 
-    def column_terms(tile, half):
-        start = pl.multiple_of(tile * TILE, TILE)
-        d_low, t_low = dsc[:, pl.ds(start, TILE)], tdsc[:, pl.ds(start, TILE)]
-        span = slice(half * WIDE, (half + 1) * WIDE)
-        total = dot(t_low, rows_u[:, span], TN) + dot(d_low, rows_t[:, span], TN)
-        total -= cvec[pl.ds(start, TILE), 0:1] * dot(d_low, rows_u[:, span], TN)
-        return LOGIT_SCALE * total
-
-    half_tiles = HALF // TILE
+    def column_terms(core, high):
+        start = pl.multiple_of((core * NH + high) * BLOCKS, BLOCKS)
+        d_low, t_low = dsc[:, pl.ds(start, BLOCKS)], tdsc[:, pl.ds(start, BLOCKS)]
+        total = dot(t_low, rows_u[...], TN) + dot(d_low, rows_t[...], TN)
+        total -= cvec[pl.ds(start, BLOCKS), 0:1] * dot(d_low, rows_u[...], TN)
+        return (LOGIT_SCALE * total).reshape(NY, SHARE, WIDTH)
+
+    steps = (2, 1, 3, 0)
     passed = []
-    for half in range(2):
-        for tile in range(half_tiles):
-            terms = column_terms((1 - c) * half_tiles + tile, half)
-            block = col_part.at[half, 0, tile]
-            block[...] = terms.reshape(block.shape)
-            passed += over_c(block, col_recv.at[half, tile])
+    for place, step in enumerate(steps):
+        col_away[place] = column_terms(1 - c, h_at(step))
+        passed += over_c(col_away.at[place], col_recv.at[place])
     y_copies = []
-    for half in range(2):
-        for tile in range(half_tiles):
-            terms = column_terms(c * half_tiles + tile, half).reshape(col_part.shape[3:])
-            passed[half * half_tiles + tile].wait_recv()
-            col_part[half, 1, tile] = terms + col_recv[half, tile]
-        y_copies.append(
-            over_y(lambda r: col_part.at[half, 1, r // 2, r % 2], lambda q: y_recv.at[half, q - 1])
-        )
-    arrive(core_copies)
-    y_grad[pl.ds(y, 1)] = sum_slots(core_grad, NC)[None]
-    y_grad_copies = spread_y(y_grad)
+    for place, step in enumerate(steps):
+        terms = column_terms(c, h_at(step))
+        passed[place].wait_recv()
+        col_part[place] = terms + col_recv[place]
+        y_copies.append(over_y(lambda r: col_part.at[place, r], lambda q: y_recv.at[place, q - 1]))
 
     for tile in range(WIDTH // TILE):
         span = slice(tile * TILE, (tile + 1) * TILE)
-        u_piece = cols_u[:, :, :, :, span].reshape(COLS, TILE)
-        t_piece = cols_t[:, :, :, :, span].reshape(COLS, TILE)
+        u_piece = cols[:, :, :, 0, :, span].reshape(COLS, TILE)
+        t_piece = cols[:, :, :, 1, :, span].reshape(COLS, TILE)
         total = dot(tdsc[...], u_piece) + dot(dsc[...], t_piece) - row_slope * dot(dsc[...], u_piece)
         row_part[:, :, :, span] = (LOGIT_SCALE * total).reshape(NL, NX, SHARE, TILE)
     x_copies = over_x(lambda k: row_part.at[:, k], lambda q: x_recv.at[q - 1])
 
-    arrive(y_grad_copies)
-    z_grad[pl.ds(zh, 1)] = sum_slots(y_grad, NY)[None]
+    arrive(plane_copies)
+    z_grad[pl.ds(zh, 1)] = sum_slots(plane_grad, NC * NY)[None]
     z_grad_copies = spread_h(z_grad)
 
-    def column_high(half):
-        arrive(y_copies[half])
-        here = col_part[half, 1, y // 2, y % 2]
-        col_part[half, 1, y // 2, y % 2] = here + y_recv[half, 0] + y_recv[half, 1] + y_recv[half, 2]
-        return over_h(lambda h: col_part.at[half, 1, y // 2, y % 2, h], lambda q: z_recv.at[half, q - 1])
-
-    high_first = column_high(0)
+    def column_sum(place):
+        arrive(y_copies[place])
+        return col_part[place, y] + y_recv[place, 0] + y_recv[place, 1] + y_recv[place, 2]
+
+    def column_high(place):
+        step = steps[place]
+        col_part[place, y] = column_sum(place)
+        return [send(col_part.at[place, y], z_recv.at[step - 1], device(high=h_at(step)))]
+
+    high_copies = column_high(0)
+    high_copies += column_high(1)
     arrive(x_copies)
     for low in range(NL):
         row_part[low, x] += x_recv[0, low] + x_recv[1, low] + x_recv[2, low]
@@ -468,22 +457,18 @@
         block = tdz.at[tower, mp]
         return over_m(lambda m: block, lambda q: block)
 
-    high_second = column_high(1)
+    high_copies += column_high(2)
     arrive(z_grad_copies)
     grad_cols[...] = unpack_lanes(unfold(sum_slots(z_grad, NH), 2))
     arrive(l_copies)
     tdz[0, mp] = finish(rawbuf[own], tanbuf[own], row_part[zl, x] + l_recv[...], grad_rows[own])
     sar_copies = spread_tdz(0)
-    arrive(high_first)
-    arrive(high_second)
-    halves = [
-        col_part[half, 1, y // 2, y % 2, zh] + z_recv[half, 0] + z_recv[half, 1] + z_recv[half, 2]
-        for half in range(2)
-    ]
+    own_sum = column_sum(3)
+    arrive(high_copies)
     tdz[1, mp] = finish(
         rawbuf[ROWS : ROWS + SHARE],
         tanbuf[ROWS : ROWS + SHARE],
-        jnp.concatenate(halves, 1),
+        own_sum + z_recv[0] + z_recv[1] + z_recv[2],
         grad_cols[pl.ds(first_col, SHARE)],
     )
     optical_copies = spread_tdz(1)
@@ -499,36 +484,51 @@
     scal_copies = spread_m(scal_m)
     arrive(passed)
     part_hess[pl.ds(c, 1)] += core_hess[...][None]
-    copies = over_y(lambda r: part_hess.at[c, r], lambda q: y_hess.at[q - 1])
+    row_copies = [
+        over_y(lambda r: part_hess.at[c, r, half], lambda q: y_hess.at[half, q - 1]) for half in range(2)
+    ]
     arrive(scal_copies)
     scal_p[pl.ds(c * NY + y, 1)] = sum_slots(scal_m, NM)[None]
     scal_copies = over_plane(scal_p)
-    arrive(copies)
-    z_hess[zh] = part_hess[c, y] + y_hess[0] + y_hess[1] + y_hess[2]
-    copies = spread_h(z_hess)
+    high_copies = []
+    for half in range(2):
+        arrive(row_copies[half])
+        z_hess[half, zh] = part_hess[c, y, half] + y_hess[half, 0] + y_hess[half, 1] + y_hess[half, 2]
+        block = z_hess.at[half, zh]
+        high_copies.append(over_h(lambda h: block, lambda q: block))
     arrive(scal_copies)
     scal_z[pl.ds(zh, 1)] = sum_slots(scal_p, NC * NY)[None]
     scal_copies = spread_h(scal_z)
-    arrive(copies)
-    block_hess = sum_slots(z_hess, NH)
-    hess[c, y] = block_hess
-    block = hess.at[c, y]
-    copies = over_y(lambda r: block, lambda q: block)
+
+    def hess_rows(half):
+        block = hess.at[c, y, half]
+        return over_y(lambda r: block, lambda q: block)
+
+    def hess_sum(half):
+        arrive(high_copies[half])
+        hess[c, y, half] = functools.reduce(jnp.add, [z_hess[half, k] for k in range(NH)])
+
+    hess_sum(0)
+    row_copies = [hess_rows(0)]
     arrive(scal_copies)
     curve = sum_slots(scal_z, NH)[0:1, 0:1] + DAMPING * norm_direc
     alpha = norm_old / curve
+    hess_sum(1)
     piece = pl.ds(pl.multiple_of(y * BLOCK, BLOCK), BLOCK)
-    after = resid[c, piece] - alpha * (block_hess + DAMPING * direc[c, piece])
+    after = resid[c, piece] - alpha * (hess[c, y].reshape(BLOCK, WIDTH) + DAMPING * direc[c, piece])
     norm_p[pl.ds(c * NY + y, 1)] = jnp.full((1, 8, 128), jnp.sum(after * after), F32)
     scal_copies = over_plane(norm_p)
-    passed = over_c(block, block)
-    for q, copy in enumerate(copies, 1):
-        copy.wait_recv()
-        block = hess.at[c, (y + NY - q) % NY]
-        passed += over_c(block, block)
-    arrive(scal_copies)
-    norm_m[pl.ds(mp, 1)] = sum_slots(norm_p, NC * NY)[None]
-    scal_copies = spread_m(norm_m)
+    row_copies.append(hess_rows(1))
+    passed = over_c(hess.at[c, y], hess.at[c, y])
+    for half in range(2):
+        for q, copy in enumerate(row_copies[half], 1):
+            copy.wait_recv()
+            block = hess.at[c, (y + NY - q) % NY, half]
+            passed += over_c(block, block)
+        if half == 0:
+            arrive(scal_copies)
+            norm_m[pl.ds(mp, 1)] = sum_slots(norm_p, NC * NY)[None]
+            scal_copies = spread_m(norm_m)
     arrive(passed)
     store = load(hess, hess_out, 7)
     arrive(scal_copies)
@@ -561,18 +561,18 @@
         bf16(2, 2, NM, PART, WIDTH), bf16(2, NY, NM - 1, QUARTER, WIDTH),
         f32(ROWS + SHARE, WIDTH), f32(ROWS + SHARE, WIDTH),
         bf16(ROWS, WIDTH), bf16(ROWS, WIDTH),
-        bf16(NC, NY, NH, SHARE, WIDTH), bf16(NC, NY, NH, SHARE, WIDTH),
+        bf16(NC, NH, NY, 2, SHARE, WIDTH),
         f32(ROWS, COLS), f32(ROWS, COLS), f32(ROWS, COLS),
         bf16(ROWS, COLS), bf16(ROWS, COLS), f32(COLS, 128),
-        f32(NM, 8, ROWS), f32(NC, 8, COLS // 2), f32(NY, 8, COLS // 2), f32(NH, 8, COLS // 2),
-        f32(NM, 8, ROWS), f32(NC, 8, COLS // 4), f32(NY, 8, COLS // 4), f32(NH, 8, COLS // 4),
+        f32(NM, 8, ROWS), f32(NC * NY, 8, COLS // 2), f32(NH, 8, COLS // 2),
+        f32(NM, 8, ROWS), f32(NC * NY, 8, COLS // 4), f32(NH, 8, COLS // 4),
         f32(NL, NX, SHARE, WIDTH), f32(NX - 1, NL, SHARE, WIDTH), f32(SHARE, WIDTH),
-        f32(2, 2, 2, 2, NH, SHARE, WIDE), f32(2, 2, 2, NH, SHARE, WIDE),
-        f32(2, NY - 1, NH, SHARE, WIDE), f32(2, NH - 1, SHARE, WIDE),
+        f32(NH, NY, SHARE, WIDTH), f32(NH, NY, SHARE, WIDTH), f32(NH, NY, SHARE, WIDTH),
+        f32(NH, NY - 1, SHARE, WIDTH), f32(NH - 1, SHARE, WIDTH),
         f32(COLS, 128), f32(ROWS, 128),
         bf16(2, NM, SHARE, WIDTH),
-        f32(2, NY, BLOCK, WIDTH), f32(NY, BLOCK, WIDTH),
-        f32(NY - 1, BLOCK, WIDTH), f32(NH, BLOCK, WIDTH), f32(2, NY, BLOCK, WIDTH),
+        f32(2, NY, 2, HALF, WIDTH), f32(NY, 2, HALF, WIDTH),
+        f32(2, NY - 1, HALF, WIDTH), f32(2, NH, HALF, WIDTH), f32(2, NY, 2, HALF, WIDTH),
         f32(NM, 8, 128), f32(NC * NY, 8, 128), f32(NH, 8, 128),
         f32(NC * NY, 8, 128), f32(NM, 8, 128),
         pltpu.SemaphoreType.DMA((SEMS,)), pltpu.SemaphoreType.DMA((SEMS,)), pltpu.SemaphoreType.DMA((8,)),
@@ -581,7 +581,7 @@
         kernel,
         name="cg_step",
         out_shape=(
-            jax.ShapeDtypeStruct((2, NY, BLOCK, WIDTH), F32),
+            jax.ShapeDtypeStruct((2, NY, 2, HALF, WIDTH), F32),
             jax.ShapeDtypeStruct((8, 128), F32),
         ),
         in_specs=[hbm] * 4,

time: 152 us -> 133 us (0.88)
  Pallas kernels: 151 us -> 132 us
    pallas_call x1, Pallas kernels: 147 us -> 128 us  [body(): pl.pallas_call(kernel, name='cg_step', out_shape=(jax.ShapeDtypeStruct((2...]
where the time goes in v4:
time: 133 us; the launch traced here: 132 us
  Pallas kernels  132 us (99%)
    pallas_call x1, Pallas kernels, body(): pl.pallas_call(kernel, name='cg_step', out_shape=(jax.ShapeDtypeStruct((2...  128 us
    pallas_call x1, Pallas kernels, body(): pl.pallas_call(last_kernel, name='updates', grid=(NY,), out_shape=(shape,...  4.23 us

profile of v4, /device:TPU:1, one launch (start us, length us, event | category | flops | bytes accessed | tf_op | source)
XLA Modules:
  0.0 132.4 jit_solution(13697913891063582522)
XLA Ops:
  0.6 127.6 %cg_step.1 = (f32[2,4,2,16,768]{4,3,2,1,0:T(8,128)}, f32[8,128]{1,0:T(8,128)}) custom-call(bf16[2,256,1024]{2,1,0:T(8,128)(2,1)} %feats_in.1, bf16[2,128,768]{2,1,0:T(8,128)(2,1)} %proj_in.1, f32[2,128,768]{2,1,0:T(8,128)} %direc.1, f32[2,128,768]{2,1,0:T(8,128)} %resid.1), custom_call_target="tpu_custom_call" | custom-call | tf_op jit(solution)/shard_map/cg_step/pallas_call | solution.py:580
  128.2 4.2 %updates.1 = (f32[2,128,768]{2,1,0:T(8,128)}, f32[2,128,768]{2,1,0:T(8,128)}, f32[2,128,768]{2,1,0:T(8,128)}) custom-call(f32[8,128]{1,0:T(8,128)} %get-tuple-element.5.info, f32[2,128,768]{2,1,0:T(8,128)} %bitcast.1, f32[2,128,768]{2,1,0:T(8,128)} %direc.1, f32[2,128,768]{2,1,0:T(8,128)} %resid.1, f32[2,128,768]{2,1,0:T(8,128)} %solu.1), custom_call_target="tpu_custom_call" | custom-call | tf_op jit(solution)/shard_map/updates/pallas_call | solution.py:596

commit v5 on v4

--- a/solution.py
+++ b/solution.py
@@ -84,7 +84,7 @@
     scores, left_ts, right_ts, dsc, tdsc, cvec,
     row_slots, plane_stat, z_stat,
     grad_slots, plane_grad, z_grad,
-    row_part, x_recv, l_recv, col_away, col_part, col_recv, y_recv, z_recv,
+    row_part, x_recv, l_recv, col_away, col_part, col_low, col_recv, y_recv, z_recv,
     grad_cols, grad_rows, tdz, part_hess, core_hess, y_hess, z_hess, hess,
     scal_m, scal_p, scal_z, norm_p, norm_m,
     send_sem, recv_sem, load_sem,
@@ -160,19 +160,18 @@
         copy.start()
         return copy
 
-    load_direc = [load(direc_in.at[tower], direc.at[tower], tower) for tower in (1, 0)]
-    load_proj = [load(proj_in.at[tower], weights.at[0, tower, mp], 2 + tower) for tower in (1, 0)]
-    load_feats = [load(feats_in.at[tower], feats.at[tower], 4 + tower) for tower in (1, 0)]
-    load_resid = load(resid_in, resid, 6)
-
     barrier = pltpu.get_barrier_semaphore()
+    for q in (2, 1, 3):
+        pl.semaphore_signal(barrier, inc=1, device_id=device(high=h_at(q)), device_id_type=MESH)
     for q in range(1, NM):
         pl.semaphore_signal(barrier, inc=1, device_id=device(model=m_at(q)), device_id_type=MESH)
     for q in range(1, NC * NY):
         where = device(core=(c + q // NY) % NC, row=(y + q % NY) % NY)
         pl.semaphore_signal(barrier, inc=1, device_id=where, device_id_type=MESH)
-    for q in range(1, NH):
-        pl.semaphore_signal(barrier, inc=1, device_id=device(high=h_at(q)), device_id_type=MESH)
+    load_direc = [load(direc_in.at[tower], direc.at[tower], tower) for tower in (1, 0)]
+    load_proj = [load(proj_in.at[tower], weights.at[0, tower, mp], 2 + tower) for tower in (1, 0)]
+    load_feats = [load(feats_in.at[tower], feats.at[tower], 4 + tower) for tower in (1, 0)]
+    load_resid = load(resid_in, resid, 6)
     load_direc[0].wait()
     weights[1, 1, pl.ds(mp, 1)] = direc[1].astype(BF16)[None]
     load_proj[0].wait()
@@ -261,7 +260,8 @@
 
     mine = column_block(zh, y)
     high_copies = over_h(lambda h: mine, lambda q: mine)
-    col_passed, copies = column_rows(zh)
+    passed, copies = column_rows(zh)
+    col_passed = [passed]
     waiting = [(zh, copies)]
     first_col = pl.multiple_of(((c * NH + zh) * NY + y) * SHARE, SHARE)
     cvec[...] = jnp.zeros_like(cvec)
@@ -271,16 +271,16 @@
         high_copies[q - 1].wait_recv()
         high = (zh + NH - q) % NH
         passed, copies = column_rows(high)
-        col_passed += passed
+        col_passed.append(passed)
         waiting.append((high, copies))
-    col_passed += column_pass(*waiting[0])
+    col_passed[0] += column_pass(*waiting[0])
     passed = over_c(sar(partner), sar(partner))
     passed += pass_on(sar, zl, sar_x_copies)
-    col_passed += column_pass(*waiting[1])
+    col_passed[1] += column_pass(*waiting[1])
     passed += pass_on(sar, 1 - zl, sar_x_relays)
     load_feats[1].wait()
     arrive(passed)
-    col_passed += column_pass(*waiting[2])
+    col_passed[2] += column_pass(*waiting[2])
     every = slice(0, ROWS)
     embed(0, 0, every, rawbuf, 0)
     embed(1, 0, every, tanbuf, 0)
@@ -289,25 +289,20 @@
     rows_u[...] = unit.astype(BF16)
     rows_t[...] = turned.astype(BF16)
     row_slope = inverse * along
-    col_passed += column_pass(*waiting[3])
-    arrive(col_passed)
-
-    def column_tile(kind, tile):
-        return cols[tile // 2, (tile % 2) * 2 : (tile % 2) * 2 + 2, :, kind].reshape(TILE, WIDTH)
-
     NT = ((1,), (1,))
     tiles = COLS // TILE
-    for tile in range(tiles):
-        span = slice(tile * TILE, (tile + 1) * TILE)
-        piece = column_tile(0, tile)
-        scores[:, span] = LOGIT_SCALE * dot(rows_u[...], piece, NT)
-        left_ts[:, span] = LOGIT_SCALE * dot(rows_t[...], piece, NT)
+    for place, (high, copies) in enumerate(waiting):
+        if place == NH - 1:
+            col_passed[place] += column_pass(high, copies)
+        arrive(col_passed[place])
+        piece = [cols[:, high, :, kind].reshape(NC * BLOCKS, WIDTH) for kind in range(2)]
+        for target, rows, kind in ((scores, rows_u, 0), (left_ts, rows_t, 0), (right_ts, rows_u, 1)):
+            product = LOGIT_SCALE * dot(rows[...], piece[kind], NT)
+            for core in range(NC):
+                start = pl.multiple_of((core * NH + high) * BLOCKS, BLOCKS)
+                target[:, pl.ds(start, BLOCKS)] = product[:, core * BLOCKS : (core + 1) * BLOCKS]
     row_max = jnp.max(scores[...], 1, keepdims=True)
     col_max = jnp.max(scores[...], 0, keepdims=True)
-    for tile in range(tiles):
-        span = slice(tile * TILE, (tile + 1) * TILE)
-        right_ts[:, span] = LOGIT_SCALE * dot(rows_u[...], column_tile(1, tile), NT)
-
     row_sum = jnp.zeros((ROWS, 1), F32)
     row_weighted = jnp.zeros((ROWS, 1), F32)
     col_sum, col_weighted = [], []
@@ -407,15 +402,23 @@
 
     steps = (2, 1, 3, 0)
     passed = []
-    for place, step in enumerate(steps):
-        col_away[place] = column_terms(1 - c, h_at(step))
-        passed += over_c(col_away.at[place], col_recv.at[place])
+
+    def away(place):
+        col_away[place] = column_terms(1 - c, h_at(steps[place]))
+        passed.extend(over_c(col_away.at[place], col_recv.at[place]))
+
+    away(0)
+    away(1)
     y_copies = []
     for place, step in enumerate(steps):
         terms = column_terms(c, h_at(step))
         passed[place].wait_recv()
-        col_part[place] = terms + col_recv[place]
-        y_copies.append(over_y(lambda r: col_part.at[place, r], lambda q: y_recv.at[place, q - 1]))
+        terms = terms + col_recv[place]
+        col_low[place] = terms.astype(BF16)
+        col_part[place] = terms
+        y_copies.append(over_y(lambda r: col_low.at[place, r], lambda q: y_recv.at[place, q - 1]))
+        if place + 2 < NH:
+            away(place + 2)
 
     for tile in range(WIDTH // TILE):
         span = slice(tile * TILE, (tile + 1) * TILE)
@@ -431,7 +434,7 @@
 
     def column_sum(place):
         arrive(y_copies[place])
-        return col_part[place, y] + y_recv[place, 0] + y_recv[place, 1] + y_recv[place, 2]
+        return functools.reduce(jnp.add, [y_recv[place, q].astype(F32) for q in range(NY - 1)], col_part[place, y])
 
     def column_high(place):
         step = steps[place]
@@ -541,19 +544,31 @@
     assert counter[0] <= SEMS
 
 
-def last_kernel(info, hess, direc, resid, solu, out_sol, out_res, out_dir):
+def last_kernel(info, hess, direc, resid, solu, out_sol, out_res, out_dir, sol, res, way, store_sem):
     alpha, beta = info[0:1, 0:1], info[1:2, 0:1]
+    stores = []
+
+    def store(source, target, tower):
+        copy = pltpu.make_async_copy(source.at[tower], target.at[tower], store_sem.at[len(stores)])
+        copy.start()
+        stores.append(copy)
+
     for tower in range(2):
         direction = direc[tower]
-        out_sol[tower] = solu[tower] + alpha * direction
+        sol[tower] = solu[tower] + alpha * direction
+        store(sol, out_sol, tower)
         after = resid[tower] - alpha * (hess[tower] + DAMPING * direction)
-        out_res[tower] = after
-        out_dir[tower] = after + beta * direction
+        res[tower] = after
+        store(res, out_res, tower)
+        way[tower] = after + beta * direction
+        store(way, out_dir, tower)
+    for copy in stores:
+        copy.wait()
 
 
 def body(features, projections, solution, residual, direction):
     vmem = pl.BlockSpec(memory_space=pltpu.VMEM)
-    hbm = pl.BlockSpec(memory_space=pl.ANY)
+    hbm = pl.BlockSpec(memory_space=pltpu.HBM)
     f32 = lambda *size: pltpu.VMEM(size, F32)
     bf16 = lambda *size: pltpu.VMEM(size, BF16)
     scratch = [
@@ -567,8 +582,8 @@
         f32(NM, 8, ROWS), f32(NC * NY, 8, COLS // 2), f32(NH, 8, COLS // 2),
         f32(NM, 8, ROWS), f32(NC * NY, 8, COLS // 4), f32(NH, 8, COLS // 4),
         f32(NL, NX, SHARE, WIDTH), f32(NX - 1, NL, SHARE, WIDTH), f32(SHARE, WIDTH),
-        f32(NH, NY, SHARE, WIDTH), f32(NH, NY, SHARE, WIDTH), f32(NH, NY, SHARE, WIDTH),
-        f32(NH, NY - 1, SHARE, WIDTH), f32(NH - 1, SHARE, WIDTH),
+        f32(NH, NY, SHARE, WIDTH), f32(NH, NY, SHARE, WIDTH), bf16(NH, NY, SHARE, WIDTH),
+        f32(NH, NY, SHARE, WIDTH), bf16(NH, NY - 1, SHARE, WIDTH), f32(NH - 1, SHARE, WIDTH),
         f32(COLS, 128), f32(ROWS, 128),
         bf16(2, NM, SHARE, WIDTH),
         f32(2, NY, 2, HALF, WIDTH), f32(NY, 2, HALF, WIDTH),
@@ -585,21 +600,21 @@
             jax.ShapeDtypeStruct((8, 128), F32),
         ),
         in_specs=[hbm] * 4,
-        out_specs=(hbm, vmem),
+        out_specs=(pl.BlockSpec(memory_space=pl.ANY), vmem),
         scratch_shapes=scratch,
         compiler_params=pltpu.CompilerParams(
-            collective_id=0, has_side_effects=True, vmem_limit_bytes=60 * 2**20
+            collective_id=0, has_side_effects=True, vmem_limit_bytes=58 * 2**20
         ),
     )(features, projections, direction, residual)
-    whole = pl.BlockSpec((2, BLOCK, WIDTH), lambda step: (0, step, 0))
     shape = jax.ShapeDtypeStruct(direction.shape, F32)
     return pl.pallas_call(
         last_kernel,
         name="updates",
-        grid=(NY,),
         out_shape=(shape, shape, shape),
-        in_specs=[pl.BlockSpec((8, 128), lambda step: (0, 0))] + [whole] * 4,
-        out_specs=(whole, whole, whole),
+        in_specs=[vmem] * 5,
+        out_specs=(hbm, hbm, hbm),
+        scratch_shapes=[f32(2, PART, WIDTH)] * 3 + [pltpu.SemaphoreType.DMA((6,))],
+        compiler_params=pltpu.CompilerParams(vmem_limit_bytes=16 * 2**20),
     )(info, hess.reshape(direction.shape), direction, residual, solution)
 
 

time: 133 us -> 130 us (0.977)
  Pallas kernels: 132 us -> 128 us
  local copies, waits for them, and re-layouts: 0 us -> 1.79 us
    pallas_call x1, Pallas kernels: 4.23 us -> 1.53 us  [body(): pl.pallas_call(last_kernel, name='updates', out_shape=(shape, shape, shap...]
    unnamed x0 -> x10, local copies, waits for them, and re-layouts: none -> 1.79 us
where the time goes in v5:
time: 130 us
  Pallas kernels  128 us (98%)
  local copies, waits for them, and re-layouts  1.79 us (1%)
    pallas_call x1, Pallas kernels, body(): pl.pallas_call(kernel, name='cg_step', out_shape=(jax.ShapeDtypeStruct((2...  126 us

profile of v5, /device:TPU:1, one launch (start us, length us, event | category | flops | bytes accessed | tf_op | source)
XLA Modules:
  0.0 130.3 jit_solution(531829694616132547)
XLA Ops:
  0.6 0.0 copy-start
  0.6 0.0 copy-start.1
  0.7 0.0 copy-start.2
  0.7 126.3 %cg_step.1 = (f32[2,4,2,16,768]{4,3,2,1,0:T(8,128)}, f32[8,128]{1,0:T(8,128)}) custom-call(bf16[2,256,1024]{2,1,0:T(8,128)(2,1)} %feats_in.1, bf16[2,128,768]{2,1,0:T(8,128)(2,1)} %proj_in.1, f32[2,128,768]{2,1,0:T(8,128)} %direc.1, f32[2,128,768]{2,1,0:T(8,128)} %resid.1), custom_call_target="tpu_custom_call" | custom-call | tf_op jit(solution)/shard_map/cg_step/pallas_call | solution.py:595
  127.0 0.0 copy-start.4
  127.0 0.0 copy-done
  127.0 0.0 copy-done.1
  127.0 0.0 copy-done.2
  127.0 0.6 copy-done.4
  127.7 0.0 copy-start.3
  127.7 1.1 copy-done.3
  128.8 1.5 %updates.1 = (f32[2,128,768]{2,1,0:T(8,128)}, f32[2,128,768]{2,1,0:T(8,128)}, f32[2,128,768]{2,1,0:T(8,128)}) custom-call(f32[8,128]{1,0:T(8,128)S(1)} %copy-done.4, f32[2,128,768]{2,1,0:T(8,128)S(1)} %bitcast.1, f32[2,128,768]{2,1,0:T(8,128)S(1)} %copy-done, f32[2,128,768]{2,1,0:T(8,128)S(1)} %copy-done.1, f32[2,128,768]{2,1,0:T(8,128)S(1)} %copy-done.2), custom_call_target="tpu_custom_call" | custom-call | tf_op jit(solution)/shard_map/updates/pallas_call | solution.py:610
Async XLA Ops:
  0.6 126.4 %copy-start = (f32[2,128,768]{2,1,0:T(8,128)S(1)}, f32[2,128,768]{2,1,0:T(8,128)}, u32[]{:S(2)}) copy-start(f32[2,128,768]{2,1,0:T(8,128)} %direc.1) | copy-start | bytes 2359300
  0.6 126.4 %copy-start.1 = (f32[2,128,768]{2,1,0:T(8,128)S(1)}, f32[2,128,768]{2,1,0:T(8,128)}, u32[]{:S(2)}) copy-start(f32[2,128,768]{2,1,0:T(8,128)} %resid.1) | copy-start | bytes 2359300
  0.7 126.4 %copy-start.2 = (f32[2,128,768]{2,1,0:T(8,128)S(1)}, f32[2,128,768]{2,1,0:T(8,128)}, u32[]{:S(2)}) copy-start(f32[2,128,768]{2,1,0:T(8,128)} %solu.1) | copy-start | bytes 2359300
  127.0 0.7 copy-start.4
  127.7 1.1 copy-start.3

commit v6 on v5

--- a/solution.py
+++ b/solution.py
@@ -24,7 +24,7 @@
 DIRECT = PART - NY * QUARTER
 BLOCK = PART // NY
 BLOCKS = SHARE * NY
-HALF = BLOCK // 2
+WIDE = WIDTH // 2
 F32, BF16 = jnp.float32, jnp.bfloat16
 MESH = pl.DeviceIdType.MESH
 
@@ -79,14 +79,14 @@
 
 def kernel(
     feats_in, proj_in, direc_in, resid_in,
-    hess_out, info_out,
+    hess_out,
     feats, direc, resid, weights, quarters, rawbuf, tanbuf, rows_u, rows_t, cols,
     scores, left_ts, right_ts, dsc, tdsc, cvec,
     row_slots, plane_stat, z_stat,
     grad_slots, plane_grad, z_grad,
     row_part, x_recv, l_recv, col_away, col_part, col_low, col_recv, y_recv, z_recv,
     grad_cols, grad_rows, tdz, part_hess, core_hess, y_hess, z_hess, hess,
-    scal_m, scal_p, scal_z, norm_p, norm_m,
+    scal_m, scal_p, scal_z, norm_p, norm_m, info,
     send_sem, recv_sem, load_sem,
 ):
     dp, mp = lax.axis_index("dp"), lax.axis_index("mp")
@@ -138,7 +138,8 @@
         return [send(source(y_at(q)), target(q), device(row=y_at(q))) for q in range(1, NY)]
 
     def over_h(source, target):
-        return [send(source(h_at(q)), target(q), device(high=h_at(q))) for q in range(1, NH)]
+        copies = {q: send(source(h_at(q)), target(q), device(high=h_at(q))) for q in (2, 1, 3)}
+        return [copies[q] for q in range(1, NH)]
 
     def over_x(source, target):
         return [send(source(x_at(q)), target(q), device(model=zl * NX + x_at(q))) for q in range(1, NX)]
@@ -409,6 +410,15 @@
 
     away(0)
     away(1)
+
+    for tile in range(WIDTH // TILE):
+        span = slice(tile * TILE, (tile + 1) * TILE)
+        u_piece = cols[:, :, :, 0, :, span].reshape(COLS, TILE)
+        t_piece = cols[:, :, :, 1, :, span].reshape(COLS, TILE)
+        total = dot(tdsc[...], u_piece) + dot(dsc[...], t_piece) - row_slope * dot(dsc[...], u_piece)
+        row_part[:, :, :, span] = (LOGIT_SCALE * total).reshape(NL, NX, SHARE, TILE)
+    x_copies = over_x(lambda k: row_part.at[:, k], lambda q: x_recv.at[q - 1])
+
     y_copies = []
     for place, step in enumerate(steps):
         terms = column_terms(c, h_at(step))
@@ -420,14 +430,6 @@
         if place + 2 < NH:
             away(place + 2)
 
-    for tile in range(WIDTH // TILE):
-        span = slice(tile * TILE, (tile + 1) * TILE)
-        u_piece = cols[:, :, :, 0, :, span].reshape(COLS, TILE)
-        t_piece = cols[:, :, :, 1, :, span].reshape(COLS, TILE)
-        total = dot(tdsc[...], u_piece) + dot(dsc[...], t_piece) - row_slope * dot(dsc[...], u_piece)
-        row_part[:, :, :, span] = (LOGIT_SCALE * total).reshape(NL, NX, SHARE, TILE)
-    x_copies = over_x(lambda k: row_part.at[:, k], lambda q: x_recv.at[q - 1])
-
     arrive(plane_copies)
     z_grad[pl.ds(zh, 1)] = sum_slots(plane_grad, NC * NY)[None]
     z_grad_copies = spread_h(z_grad)
@@ -443,6 +445,7 @@
 
     high_copies = column_high(0)
     high_copies += column_high(1)
+    high_copies += column_high(2)
     arrive(x_copies)
     for low in range(NL):
         row_part[low, x] += x_recv[0, low] + x_recv[1, low] + x_recv[2, low]
@@ -450,22 +453,21 @@
     arrive(grad_copies)
     grad_rows[...] = unpack_lanes(sum_slots(grad_slots, NM))
 
-    def finish(raw, tangent, value, info):
+    def finish(raw, tangent, value, terms):
         unit, inverse = unit_of(raw)
         turned, _ = turn_of(tangent, unit, inverse)
-        mixed = info[:, 1:2] + jnp.sum(unit * value, -1, keepdims=True)
-        return ((value - turned * info[:, 0:1] - unit * mixed) * inverse).astype(BF16)
+        mixed = terms[:, 1:2] + jnp.sum(unit * value, -1, keepdims=True)
+        return ((value - turned * terms[:, 0:1] - unit * mixed) * inverse).astype(BF16)
 
     def spread_tdz(tower):
         block = tdz.at[tower, mp]
         return over_m(lambda m: block, lambda q: block)
 
-    high_copies += column_high(2)
-    arrive(z_grad_copies)
-    grad_cols[...] = unpack_lanes(unfold(sum_slots(z_grad, NH), 2))
     arrive(l_copies)
     tdz[0, mp] = finish(rawbuf[own], tanbuf[own], row_part[zl, x] + l_recv[...], grad_rows[own])
     sar_copies = spread_tdz(0)
+    arrive(z_grad_copies)
+    grad_cols[...] = unpack_lanes(unfold(sum_slots(z_grad, NH), 2))
     own_sum = column_sum(3)
     arrive(high_copies)
     tdz[1, mp] = finish(
@@ -476,76 +478,99 @@
     )
     optical_copies = spread_tdz(1)
 
-    curve = 0.0
-    for tower, copies in enumerate((sar_copies, optical_copies)):
+    lanes = pl.ds(pl.multiple_of(c * WIDE, 128), WIDE)
+    block_rows = pl.ds(pl.multiple_of(y * BLOCK, BLOCK), BLOCK)
+
+    def hess_terms(tower):
+        part = dot(feats[tower, :, pl.ds(pl.multiple_of(mp * PART, PART), PART)], tdz[tower].reshape(ROWS, WIDTH), TN)
+        for half in range(2):
+            part_hess[tower, half] = part[:, half * WIDE : (half + 1) * WIDE].reshape(NY, BLOCK, WIDE)
+        return jnp.sum(direc[tower] * part), over_c(part_hess.at[tower, 1 - c], core_hess.at[tower])
+
+    def hess_rows(tower, copies):
         arrive(copies)
-        part = dot(feats[tower, :, pl.ds(pl.multiple_of(mp * PART, PART), PART)], tdz[tower].reshape(ROWS, WIDTH), TN)
-        part_hess[tower] = part.reshape(part_hess.shape[1:])
-        curve += jnp.sum(direc[tower] * part)
-    passed = over_c(part_hess.at[1 - c], core_hess)
-    scal_m[pl.ds(mp, 1)] = jnp.full((1, 8, 128), curve, F32)
+        part_hess[tower, c] += core_hess[tower]
+        return over_y(lambda r: part_hess.at[tower, c, r], lambda q: y_hess.at[tower, q - 1])
+
+    def hess_high(tower, copies):
+        arrive(copies)
+        z_hess[tower, zh] = part_hess[tower, c, y] + y_hess[tower, 0] + y_hess[tower, 1] + y_hess[tower, 2]
+        block = z_hess.at[tower, zh]
+        return over_h(lambda h: block, lambda q: block)
+
+    def hess_sum(tower, copies):
+        arrive(copies)
+        hess[tower, c, block_rows] = functools.reduce(jnp.add, [z_hess[tower, k] for k in range(NH)])
+
+    def hess_back(tower):
+        block = hess.at[tower, c, block_rows]
+        return over_c(block, block), over_y(lambda r: block, lambda q: block)
+
+    def hess_pass(tower, copies):
+        passed = []
+        for q, copy in enumerate(copies, 1):
+            copy.wait_recv()
+            row = (y + NY - q) % NY
+            block = hess.at[tower, c, pl.ds(pl.multiple_of(row * BLOCK, BLOCK), BLOCK)]
+            passed += over_c(block, block)
+        return passed
+
+    arrive(sar_copies)
+    first_curve, core_first = hess_terms(0)
+    row_first = hess_rows(0, core_first)
+    arrive(optical_copies)
+    curve, core_second = hess_terms(1)
+    scal_m[pl.ds(mp, 1)] = jnp.full((1, 8, 128), first_curve + curve, F32)
     scal_copies = spread_m(scal_m)
-    arrive(passed)
-    part_hess[pl.ds(c, 1)] += core_hess[...][None]
-    row_copies = [
-        over_y(lambda r: part_hess.at[c, r, half], lambda q: y_hess.at[half, q - 1]) for half in range(2)
-    ]
+    row_second = hess_rows(1, core_second)
+    high_first = hess_high(0, row_first)
     arrive(scal_copies)
     scal_p[pl.ds(c * NY + y, 1)] = sum_slots(scal_m, NM)[None]
     scal_copies = over_plane(scal_p)
-    high_copies = []
-    for half in range(2):
-        arrive(row_copies[half])
-        z_hess[half, zh] = part_hess[c, y, half] + y_hess[half, 0] + y_hess[half, 1] + y_hess[half, 2]
-        block = z_hess.at[half, zh]
-        high_copies.append(over_h(lambda h: block, lambda q: block))
+    high_second = hess_high(1, row_second)
     arrive(scal_copies)
     scal_z[pl.ds(zh, 1)] = sum_slots(scal_p, NC * NY)[None]
     scal_copies = spread_h(scal_z)
-
-    def hess_rows(half):
-        block = hess.at[c, y, half]
-        return over_y(lambda r: block, lambda q: block)
-
-    def hess_sum(half):
-        arrive(high_copies[half])
-        hess[c, y, half] = functools.reduce(jnp.add, [z_hess[half, k] for k in range(NH)])
-
-    hess_sum(0)
-    row_copies = [hess_rows(0)]
+    hess_sum(0, high_first)
+    passed, back_first = hess_back(0)
     arrive(scal_copies)
     curve = sum_slots(scal_z, NH)[0:1, 0:1] + DAMPING * norm_direc
     alpha = norm_old / curve
-    hess_sum(1)
-    piece = pl.ds(pl.multiple_of(y * BLOCK, BLOCK), BLOCK)
-    after = resid[c, piece] - alpha * (hess[c, y].reshape(BLOCK, WIDTH) + DAMPING * direc[c, piece])
-    norm_p[pl.ds(c * NY + y, 1)] = jnp.full((1, 8, 128), jnp.sum(after * after), F32)
+    hess_sum(1, high_second)
+    total = 0.0
+    for tower in range(2):
+        after = resid[tower, block_rows, lanes]
+        after -= alpha * (hess[tower, c, block_rows] + DAMPING * direc[tower, block_rows, lanes])
+        total += jnp.sum(after * after)
+    norm_p[pl.ds(c * NY + y, 1)] = jnp.full((1, 8, 128), total, F32)
     scal_copies = over_plane(norm_p)
-    row_copies.append(hess_rows(1))
-    passed = over_c(hess.at[c, y], hess.at[c, y])
-    for half in range(2):
-        for q, copy in enumerate(row_copies[half], 1):
-            copy.wait_recv()
-            block = hess.at[c, (y + NY - q) % NY, half]
-            passed += over_c(block, block)
-        if half == 0:
-            arrive(scal_copies)
-            norm_m[pl.ds(mp, 1)] = sum_slots(norm_p, NC * NY)[None]
-            scal_copies = spread_m(norm_m)
+    more, back_second = hess_back(1)
+    passed += more
+    passed += hess_pass(0, back_first)
+    arrive(scal_copies)
+    norm_m[pl.ds(mp, 1)] = sum_slots(norm_p, NC * NY)[None]
+    scal_copies = spread_m(norm_m)
+    passed += hess_pass(1, back_second)
     arrive(passed)
-    store = load(hess, hess_out, 7)
+    stores = []
+    for tower in range(2):
+        for half in range(2):
+            target = hess_out.at[tower * PART : (tower + 1) * PART, half * WIDE : (half + 1) * WIDE]
+            stores.append(load(hess.at[tower, half], target, 7 + 2 * tower + half))
     arrive(scal_copies)
     norm_new = sum_slots(norm_m, NM)[0:1, 0:1]
-    first_row = lax.broadcasted_iota(jnp.int32, (8, 128), 0) == 0
-    info_out[...] = jnp.where(first_row, alpha, norm_new / norm_old)
-    store.wait()
+    first_row = lax.broadcasted_iota(jnp.int32, (8, WIDTH), 0) == 0
+    info[...] = jnp.where(first_row, alpha, norm_new / norm_old)
+    stores.append(load(info, hess_out.at[2 * PART : 2 * PART + 8], 11))
+    for store in stores:
+        store.wait()
     for copy in pending:
         copy.wait_send()
     assert counter[0] <= SEMS
 
 
-def last_kernel(info, hess, direc, resid, solu, out_sol, out_res, out_dir, sol, res, way, store_sem):
-    alpha, beta = info[0:1, 0:1], info[1:2, 0:1]
+def last_kernel(hess, direc, resid, solu, out_sol, out_res, out_dir, sol, res, way, store_sem):
+    alpha, beta = hess[2 * PART : 2 * PART + 1, 0:1], hess[2 * PART + 1 : 2 * PART + 2, 0:1]
     stores = []
 
     def store(source, target, tower):
@@ -557,7 +582,8 @@
         direction = direc[tower]
         sol[tower] = solu[tower] + alpha * direction
         store(sol, out_sol, tower)
-        after = resid[tower] - alpha * (hess[tower] + DAMPING * direction)
+        part = hess[tower * PART : (tower + 1) * PART]
+        after = resid[tower] - alpha * (part + DAMPING * direction)
         res[tower] = after
         store(res, out_res, tower)
         way[tower] = after + beta * direction
@@ -586,21 +612,18 @@
         f32(NH, NY, SHARE, WIDTH), bf16(NH, NY - 1, SHARE, WIDTH), f32(NH - 1, SHARE, WIDTH),
         f32(COLS, 128), f32(ROWS, 128),
         bf16(2, NM, SHARE, WIDTH),
-        f32(2, NY, 2, HALF, WIDTH), f32(NY, 2, HALF, WIDTH),
-        f32(2, NY - 1, HALF, WIDTH), f32(2, NH, HALF, WIDTH), f32(2, NY, 2, HALF, WIDTH),
+        f32(2, 2, NY, BLOCK, WIDE), f32(2, NY, BLOCK, WIDE),
+        f32(2, NY - 1, BLOCK, WIDE), f32(2, NH, BLOCK, WIDE), f32(2, 2, PART, WIDE),
         f32(NM, 8, 128), f32(NC * NY, 8, 128), f32(NH, 8, 128),
-        f32(NC * NY, 8, 128), f32(NM, 8, 128),
-        pltpu.SemaphoreType.DMA((SEMS,)), pltpu.SemaphoreType.DMA((SEMS,)), pltpu.SemaphoreType.DMA((8,)),
+        f32(NC * NY, 8, 128), f32(NM, 8, 128), f32(8, WIDTH),
+        pltpu.SemaphoreType.DMA((SEMS,)), pltpu.SemaphoreType.DMA((SEMS,)), pltpu.SemaphoreType.DMA((12,)),
     ]
-    hess, info = pl.pallas_call(
+    hess = pl.pallas_call(
         kernel,
         name="cg_step",
-        out_shape=(
-            jax.ShapeDtypeStruct((2, NY, 2, HALF, WIDTH), F32),
-            jax.ShapeDtypeStruct((8, 128), F32),
-        ),
+        out_shape=jax.ShapeDtypeStruct((2 * PART + 8, WIDTH), F32),
         in_specs=[hbm] * 4,
-        out_specs=(pl.BlockSpec(memory_space=pl.ANY), vmem),
+        out_specs=pl.BlockSpec(memory_space=pl.ANY),
         scratch_shapes=scratch,
         compiler_params=pltpu.CompilerParams(
             collective_id=0, has_side_effects=True, vmem_limit_bytes=58 * 2**20
@@ -611,11 +634,11 @@
         last_kernel,
         name="updates",
         out_shape=(shape, shape, shape),
-        in_specs=[vmem] * 5,
+        in_specs=[vmem] * 4,
         out_specs=(hbm, hbm, hbm),
         scratch_shapes=[f32(2, PART, WIDTH)] * 3 + [pltpu.SemaphoreType.DMA((6,))],
         compiler_params=pltpu.CompilerParams(vmem_limit_bytes=16 * 2**20),
-    )(info, hess.reshape(direction.shape), direction, residual, solution)
+    )(hess, direction, residual, solution)
 
 
 def solution(mesh):

time: 130 us -> 127 us (0.977)
  Pallas kernels: 128 us -> 125 us
    pallas_call x1, Pallas kernels: 126 us -> 124 us  [body(): pl.pallas_call(kernel, name='cg_step', out_shape=jax.ShapeDtypeStruct((2...]
where the time goes in v6:
time: 127 us
  Pallas kernels  125 us (98%)
    pallas_call x1, Pallas kernels, body(): pl.pallas_call(kernel, name='cg_step', out_shape=jax.ShapeDtypeStruct((2...  124 us

profile of v6, /device:TPU:1, one launch (start us, length us, event | category | flops | bytes accessed | tf_op | source)
XLA Modules:
  0.0 127.3 jit_solution(9991786110962358845)
XLA Ops:
  0.6 0.0 copy-start.1
  0.6 0.0 copy-start.2
  0.7 0.0 copy-start.3
  0.7 123.9 %cg_step.1.hess = f32[264,768]{1,0:T(8,128)} custom-call(bf16[2,256,1024]{2,1,0:T(8,128)(2,1)} %feats_in.1, bf16[2,128,768]{2,1,0:T(8,128)(2,1)} %proj_in.1, f32[2,128,768]{2,1,0:T(8,128)} %direc.1, f32[2,128,768]{2,1,0:T(8,128)} %resid.1), custom_call_target="tpu_custom_call" | custom-call | tf_op jit(solution)/shard_map/cg_step/pallas_call | solution.py:621
  124.6 0.0 copy-done.1
  124.6 0.0 copy-done.2
  124.6 0.0 copy-done.3
  124.6 0.0 copy-start
  124.6 1.1 copy-done
  125.7 1.6 %updates.1 = (f32[2,128,768]{2,1,0:T(8,128)}, f32[2,128,768]{2,1,0:T(8,128)}, f32[2,128,768]{2,1,0:T(8,128)}) custom-call(f32[264,768]{1,0:T(8,128)S(1)} %copy-done, f32[2,128,768]{2,1,0:T(8,128)S(1)} %copy-done.1, f32[2,128,768]{2,1,0:T(8,128)S(1)} %copy-done.2, f32[2,128,768]{2,1,0:T(8,128)S(1)} %copy-done.3), custom_call_target="tpu_custom_call" | custom-call | tf_op jit(solution)/shard_map/updates/pallas_call | solution.py:633
Async XLA Ops:
  0.6 123.9 %copy-start.1 = (f32[2,128,768]{2,1,0:T(8,128)S(1)}, f32[2,128,768]{2,1,0:T(8,128)}, u32[]{:S(2)}) copy-start(f32[2,128,768]{2,1,0:T(8,128)} %direc.1) | copy-start | bytes 2359300
  0.6 123.9 %copy-start.2 = (f32[2,128,768]{2,1,0:T(8,128)S(1)}, f32[2,128,768]{2,1,0:T(8,128)}, u32[]{:S(2)}) copy-start(f32[2,128,768]{2,1,0:T(8,128)} %resid.1) | copy-start | bytes 2359300
  0.7 123.9 %copy-start.3 = (f32[2,128,768]{2,1,0:T(8,128)S(1)}, f32[2,128,768]{2,1,0:T(8,128)}, u32[]{:S(2)}) copy-start(f32[2,128,768]{2,1,0:T(8,128)} %solu.1) | copy-start | bytes 2359300
  124.6 1.1 copy-start

commit v7 on v6

--- a/solution.py
+++ b/solution.py
@@ -86,7 +86,7 @@
     grad_slots, plane_grad, z_grad,
     row_part, x_recv, l_recv, col_away, col_part, col_low, col_recv, y_recv, z_recv,
     grad_cols, grad_rows, tdz, part_hess, core_hess, y_hess, z_hess, hess,
-    scal_m, scal_p, scal_z, norm_p, norm_m, info,
+    norm_p, norm_m, info,
     send_sem, recv_sem, load_sem,
 ):
     dp, mp = lax.axis_index("dp"), lax.axis_index("mp")
@@ -319,10 +319,9 @@
         col_weighted.append(jnp.sum(weight * tscore, 0, keepdims=True))
     load_resid.wait()
     resid_norm = jnp.sum(resid[...] * resid[...])
-    direc_norm = jnp.sum(direc[...] * direc[...])
     constant = lambda value: jnp.full((ROWS, 1), value, F32)
     row_slots[pl.ds(mp, 1)] = pack_lanes(
-        [row_max, row_sum, row_weighted, constant(resid_norm), constant(direc_norm)]
+        [row_max, row_sum, row_weighted, constant(resid_norm)]
     )[None]
     plane_stat[pl.ds(c * NY + y, 1)] = fold(
         [col_max, jnp.concatenate(col_sum, 1), jnp.concatenate(col_weighted, 1), slope_row]
@@ -351,9 +350,8 @@
     arrive(row_copies)
     parts = [row_slots[k] for k in range(NM)]
     top, total, weighted = softmax_join([(part[0:1], part[1:2], part[2:3]) for part in parts])
-    norms = functools.reduce(jnp.add, [part[3:5] for part in parts])
+    norms = functools.reduce(jnp.add, [part[3:4] for part in parts])
     norm_old = norms[0:1, 0:1]
-    norm_direc = norms[1:2, 0:1]
     row_info = unpack_lanes(jnp.concatenate([top + jnp.log(total), weighted / total], 0))
     row_lse, row_dot = row_info[:, 0:1], row_info[:, 1:2]
     arrive(copies)
@@ -485,7 +483,7 @@
         part = dot(feats[tower, :, pl.ds(pl.multiple_of(mp * PART, PART), PART)], tdz[tower].reshape(ROWS, WIDTH), TN)
         for half in range(2):
             part_hess[tower, half] = part[:, half * WIDE : (half + 1) * WIDE].reshape(NY, BLOCK, WIDE)
-        return jnp.sum(direc[tower] * part), over_c(part_hess.at[tower, 1 - c], core_hess.at[tower])
+        return over_c(part_hess.at[tower, 1 - c], core_hess.at[tower])
 
     def hess_rows(tower, copies):
         arrive(copies)
@@ -515,34 +513,27 @@
             passed += over_c(block, block)
         return passed
 
+    def hess_inner(tower):
+        old = resid[tower, block_rows, lanes]
+        along = direc[tower, block_rows, lanes]
+        new = hess[tower, c, block_rows] + DAMPING * along
+        return [jnp.sum(along * new), jnp.sum(old * new), jnp.sum(new * new)]
+
     arrive(sar_copies)
-    first_curve, core_first = hess_terms(0)
+    core_first = hess_terms(0)
     row_first = hess_rows(0, core_first)
     arrive(optical_copies)
-    curve, core_second = hess_terms(1)
-    scal_m[pl.ds(mp, 1)] = jnp.full((1, 8, 128), first_curve + curve, F32)
-    scal_copies = spread_m(scal_m)
+    core_second = hess_terms(1)
+    high_first = hess_high(0, row_first)
     row_second = hess_rows(1, core_second)
-    high_first = hess_high(0, row_first)
-    arrive(scal_copies)
-    scal_p[pl.ds(c * NY + y, 1)] = sum_slots(scal_m, NM)[None]
-    scal_copies = over_plane(scal_p)
     high_second = hess_high(1, row_second)
-    arrive(scal_copies)
-    scal_z[pl.ds(zh, 1)] = sum_slots(scal_p, NC * NY)[None]
-    scal_copies = spread_h(scal_z)
     hess_sum(0, high_first)
     passed, back_first = hess_back(0)
-    arrive(scal_copies)
-    curve = sum_slots(scal_z, NH)[0:1, 0:1] + DAMPING * norm_direc
-    alpha = norm_old / curve
+    inner = hess_inner(0)
     hess_sum(1, high_second)
-    total = 0.0
-    for tower in range(2):
-        after = resid[tower, block_rows, lanes]
-        after -= alpha * (hess[tower, c, block_rows] + DAMPING * direc[tower, block_rows, lanes])
-        total += jnp.sum(after * after)
-    norm_p[pl.ds(c * NY + y, 1)] = jnp.full((1, 8, 128), total, F32)
+    inner = [first + second for first, second in zip(inner, hess_inner(1))]
+    place = lax.broadcasted_iota(jnp.int32, (1, 8, 128), 1)
+    norm_p[pl.ds(c * NY + y, 1)] = jnp.where(place == 0, inner[0], jnp.where(place == 1, inner[1], inner[2]))
     scal_copies = over_plane(norm_p)
     more, back_second = hess_back(1)
     passed += more
@@ -558,7 +549,9 @@
             target = hess_out.at[tower * PART : (tower + 1) * PART, half * WIDE : (half + 1) * WIDE]
             stores.append(load(hess.at[tower, half], target, 7 + 2 * tower + half))
     arrive(scal_copies)
-    norm_new = sum_slots(norm_m, NM)[0:1, 0:1]
+    sums = sum_slots(norm_m, NM)
+    alpha = norm_old / sums[0:1, 0:1]
+    norm_new = norm_old - 2.0 * alpha * sums[1:2, 0:1] + alpha * alpha * sums[2:3, 0:1]
     first_row = lax.broadcasted_iota(jnp.int32, (8, WIDTH), 0) == 0
     info[...] = jnp.where(first_row, alpha, norm_new / norm_old)
     stores.append(load(info, hess_out.at[2 * PART : 2 * PART + 8], 11))
@@ -614,7 +607,6 @@
         bf16(2, NM, SHARE, WIDTH),
         f32(2, 2, NY, BLOCK, WIDE), f32(2, NY, BLOCK, WIDE),
         f32(2, NY - 1, BLOCK, WIDE), f32(2, NH, BLOCK, WIDE), f32(2, 2, PART, WIDE),
-        f32(NM, 8, 128), f32(NC * NY, 8, 128), f32(NH, 8, 128),
         f32(NC * NY, 8, 128), f32(NM, 8, 128), f32(8, WIDTH),
         pltpu.SemaphoreType.DMA((SEMS,)), pltpu.SemaphoreType.DMA((SEMS,)), pltpu.SemaphoreType.DMA((12,)),
     ]

time: 127 us -> 126 us (level)
    pallas_call x1, Pallas kernels: 124 us -> 122 us  [body(): pl.pallas_call(kernel, name='cg_step', out_shape=jax.ShapeDtypeStruct((2...]
where the time goes in v7:
time: 126 us
  Pallas kernels  124 us (98%)
    pallas_call x1, Pallas kernels, body(): pl.pallas_call(kernel, name='cg_step', out_shape=jax.ShapeDtypeStruct((2...  122 us

profile of v7, /device:TPU:1, one launch (start us, length us, event | category | flops | bytes accessed | tf_op | source)
XLA Modules:
  0.0 125.8 jit_solution(10116116351225368771)
XLA Ops:
  0.6 0.0 copy-start.1
  0.6 0.0 copy-start.2
  0.7 0.0 copy-start.3
  0.7 122.4 %cg_step.1.hess = f32[264,768]{1,0:T(8,128)} custom-call(bf16[2,256,1024]{2,1,0:T(8,128)(2,1)} %feats_in.1, bf16[2,128,768]{2,1,0:T(8,128)(2,1)} %proj_in.1, f32[2,128,768]{2,1,0:T(8,128)} %direc.1, f32[2,128,768]{2,1,0:T(8,128)} %resid.1), custom_call_target="tpu_custom_call" | custom-call | tf_op jit(solution)/shard_map/cg_step/pallas_call | solution.py:613
  123.1 0.0 copy-done.1
  123.1 0.0 copy-done.2
  123.1 0.0 copy-done.3
  123.1 0.0 copy-start
  123.1 1.1 copy-done
  124.3 1.6 %updates.1 = (f32[2,128,768]{2,1,0:T(8,128)}, f32[2,128,768]{2,1,0:T(8,128)}, f32[2,128,768]{2,1,0:T(8,128)}) custom-call(f32[264,768]{1,0:T(8,128)S(1)} %copy-done, f32[2,128,768]{2,1,0:T(8,128)S(1)} %copy-done.1, f32[2,128,768]{2,1,0:T(8,128)S(1)} %copy-done.2, f32[2,128,768]{2,1,0:T(8,128)S(1)} %copy-done.3), custom_call_target="tpu_custom_call" | custom-call | tf_op jit(solution)/shard_map/updates/pallas_call | solution.py:625
Async XLA Ops:
  0.6 122.5 %copy-start.1 = (f32[2,128,768]{2,1,0:T(8,128)S(1)}, f32[2,128,768]{2,1,0:T(8,128)}, u32[]{:S(2)}) copy-start(f32[2,128,768]{2,1,0:T(8,128)} %direc.1) | copy-start | bytes 2359300
  0.6 122.5 %copy-start.2 = (f32[2,128,768]{2,1,0:T(8,128)S(1)}, f32[2,128,768]{2,1,0:T(8,128)}, u32[]{:S(2)}) copy-start(f32[2,128,768]{2,1,0:T(8,128)} %resid.1) | copy-start | bytes 2359300
  0.7 122.5 %copy-start.3 = (f32[2,128,768]{2,1,0:T(8,128)S(1)}, f32[2,128,768]{2,1,0:T(8,128)}, u32[]{:S(2)}) copy-start(f32[2,128,768]{2,1,0:T(8,128)} %solu.1) | copy-start | bytes 2359300
  123.1 1.1 copy-start

commit v8 on v7

--- a/solution.py
+++ b/solution.py
@@ -19,7 +19,7 @@
 COLS = SHARE * NC * NY * NH
 PAIRS = ROWS * NC * NY * NH
 TILE = 256
-SEMS = 224
+SEMS = 288
 QUARTER = 16
 DIRECT = PART - NY * QUARTER
 BLOCK = PART // NY
@@ -170,21 +170,35 @@
         where = device(core=(c + q // NY) % NC, row=(y + q % NY) % NY)
         pl.semaphore_signal(barrier, inc=1, device_id=where, device_id_type=MESH)
     load_direc = [load(direc_in.at[tower], direc.at[tower], tower) for tower in (1, 0)]
-    load_proj = [load(proj_in.at[tower], weights.at[0, tower, mp], 2 + tower) for tower in (1, 0)]
+    load_proj = [
+        [
+            load(
+                proj_in.at[tower, :, half * WIDE : (half + 1) * WIDE],
+                weights.at[0, tower, half, mp],
+                12 + 2 * tower + half,
+            )
+            for half in range(2)
+        ]
+        for tower in (1, 0)
+    ]
     load_feats = [load(feats_in.at[tower], feats.at[tower], 4 + tower) for tower in (1, 0)]
     load_resid = load(resid_in, resid, 6)
+    def own_direction(tower):
+        for half in range(2):
+            piece = direc[tower, :, half * WIDE : (half + 1) * WIDE].astype(BF16)
+            weights[1, tower, half, pl.ds(mp, 1)] = piece[None]
+
+    for copy in load_proj[0]:
+        copy.wait()
     load_direc[0].wait()
-    weights[1, 1, pl.ds(mp, 1)] = direc[1].astype(BF16)[None]
-    load_proj[0].wait()
+    own_direction(1)
     pl.semaphore_wait(barrier, NM + NC * NY + NH - 3)
 
-    part = weights.at[c, 1, mp, pl.ds(pl.multiple_of(DIRECT + y * QUARTER, QUARTER), QUARTER)]
-    quarter_copies = over_m(lambda m: part, lambda q: quarters.at[c, y, q - 1])
-    def optical(m):
-        return weights.at[c, 1, m, pl.ds(0, DIRECT)]
-
-    def sar(m):
-        return weights.at[c, 0, m]
+    def optical(kind):
+        return lambda m: weights.at[kind, 1, c, m, pl.ds(0, DIRECT)]
+
+    def sar(kind):
+        return lambda m: weights.at[kind, 0, c, m]
 
     def spread_x(block):
         return over_x(lambda m: block, lambda q: block)
@@ -197,104 +211,165 @@
             passed += over_c(block, block)
         return passed
 
-    l_copies = over_l(optical(mp), optical(mp))
-    x_copies = spread_x(optical(mp))
-    load_direc[1].wait()
-    weights[1, 0, pl.ds(mp, 1)] = direc[0].astype(BF16)[None]
-    load_proj[1].wait()
-    sar_l_copies = over_l(sar(mp), sar(mp))
-    arrive(quarter_copies)
-    mine = quarters.at[c, y]
-    row_copies = over_y(lambda r: mine, lambda q: mine)
-    arrive(l_copies)
-    x_relays = spread_x(optical(partner))
-    passed = over_c(mine, mine) + over_c(optical(partner), optical(partner))
-    passed += pass_on(optical, zl, x_copies)
-    sar_x_copies = spread_x(sar(mp))
-    passed += pass_on(optical, 1 - zl, x_relays)
-    arrive(sar_l_copies)
-    sar_x_relays = spread_x(sar(partner))
-    for q, copy in enumerate(row_copies, 1):
-        copy.wait_recv()
-        block = quarters.at[c, (y + NY - q) % NY]
-        passed += over_c(block, block)
-    load_feats[0].wait()
-    arrive(passed)
-    for kind in range(2):
-        for q in range(1, NM):
-            for r in range(NY):
-                weights[kind, 1, m_from(q), DIRECT + r * QUARTER : DIRECT + (r + 1) * QUARTER] = quarters[kind, r, q - 1]
+    def quarter_start(kind):
+        part = weights.at[kind, 1, c, mp, pl.ds(pl.multiple_of(DIRECT + y * QUARTER, QUARTER), QUARTER)]
+        return over_m(lambda m: part, lambda q: quarters.at[kind, c, y, q - 1])
+
+    def quarter_rows(kind, copies):
+        arrive(copies)
+        block = quarters.at[kind, c, y]
+        return over_c(block, block), over_y(lambda r: block, lambda q: block)
+
+    def quarter_pass(kind, copies):
+        passed = []
+        for q, copy in enumerate(copies, 1):
+            copy.wait_recv()
+            block = quarters.at[kind, c, (y + NY - q) % NY]
+            passed += over_c(block, block)
+        return passed
+
+    def over_z(blocks):
+        return over_l(blocks(mp), blocks(mp))
+
+    def relay(blocks, copies):
+        arrive(copies)
+        block = blocks(partner)
+        return spread_x(block), over_c(block, block)
+
+    def assemble(kind):
+        for half in range(2):
+            for q in range(1, NM):
+                for r in range(NY):
+                    rows = slice(DIRECT + r * QUARTER, DIRECT + (r + 1) * QUARTER)
+                    weights[kind, 1, half, m_from(q), rows] = quarters[kind, half, r, q - 1]
 
     def embed(kind, tower, rows, into, first):
-        for tile in range(WIDTH // TILE):
-            span = slice(tile * TILE, (tile + 1) * TILE)
+        for half in range(2):
+            span = slice(half * WIDE, (half + 1) * WIDE)
             total = 0.0
             for block in range(0, NM, 2):
                 deep = slice(block * PART, (block + 2) * PART)
-                piece = weights[kind, tower, block : block + 2, :, span].reshape(2 * PART, TILE)
+                piece = weights[kind, tower, half, block : block + 2].reshape(2 * PART, WIDE)
                 total += dot(feats[tower, rows, deep], piece)
             into[first : first + total.shape[0], span] = total
 
+    def column_block(kind, high, row):
+        return cols.at[c, high, row, kind]
+
+    def column_rows(kind, high):
+        block = column_block(kind, high, y)
+        col_passed[high_place(high)] += over_c(block, block)
+        waiting[kind].append((high, over_y(lambda r: block, lambda q: block)))
+
+    def column_start(kind):
+        block = column_block(kind, zh, y)
+        copies = over_h(lambda h: block, lambda q: block)
+        column_rows(kind, zh)
+        return copies
+
+    def column_relay(kind, copies, q):
+        copies[q - 1].wait_recv()
+        column_rows(kind, highs[q])
+
+    def column_pass(kind, place):
+        high, copies = waiting[kind][place]
+        for q, copy in enumerate(copies, 1):
+            copy.wait_recv()
+            block = column_block(kind, high, (y + NY - q) % NY)
+            col_passed[place] += over_c(block, block)
+
+    highs = {q: (zh + NH - q) % NH for q in (0, 1, 3, 2)}
+    order = list(highs.values())
+
+    def high_place(high):
+        return next(place for place, other in enumerate(order) if other is high)
+
+    waiting = [[], []]
+    col_passed = [[], [], [], []]
+    highs[0] = order[0] = zh
+
+    quarter_copies = quarter_start(0)
+    z_copies = over_z(optical(0))
+    x_copies = spread_x(optical(0)(mp))
+    for copy in load_proj[1]:
+        copy.wait()
+    load_direc[1].wait()
+    own_direction(0)
+    passed_first, quarter_copies = quarter_rows(0, quarter_copies)
+    quarter_second = quarter_start(1)
+    z_second = over_z(optical(1))
+    x_second = spread_x(optical(1)(mp))
+    relays, passed = relay(optical(0), z_copies)
+    passed_first += passed
+    sar_z = [over_z(sar(kind)) for kind in range(2)]
+    passed_first += pass_on(optical(0), zl, x_copies)
+    passed_second, quarter_second = quarter_rows(1, quarter_second)
+    passed_first += quarter_pass(0, quarter_copies)
+    passed_first += pass_on(optical(0), 1 - zl, relays)
+    relays_second, passed = relay(optical(1), z_second)
+    passed_second += passed
+    sar_x = spread_x(sar(0)(mp))
+    load_feats[0].wait()
+    arrive(passed_first)
+    assemble(0)
     own = pl.ds(pl.multiple_of(mp * SHARE, SHARE), SHARE)
+    share = slice(ROWS, ROWS + SHARE)
     embed(0, 1, own, rawbuf, ROWS)
+    unit, inverse = unit_of(rawbuf[share])
+    cols[c, zh, y, 0] = unit.astype(BF16)
+    high_u = column_start(0)
+    passed_second += pass_on(optical(1), zl, x_second)
+    passed_second += quarter_pass(1, quarter_second)
+    passed_second += pass_on(optical(1), 1 - zl, relays_second)
+    sar_relays, sar_passed = relay(sar(0), sar_z[0])
+    arrive(passed_second)
+    assemble(1)
     embed(1, 1, own, tanbuf, ROWS)
-    unit, inverse = unit_of(rawbuf[ROWS : ROWS + SHARE])
-    turned, along = turn_of(tanbuf[ROWS : ROWS + SHARE], unit, inverse)
-    cols[c, zh, y, 0] = unit.astype(BF16)
+    unit, inverse = unit_of(rawbuf[share])
+    turned, along = turn_of(tanbuf[share], unit, inverse)
     cols[c, zh, y, 1] = turned.astype(BF16)
     slope = inverse * along
-
-    def column_block(high, row):
-        return cols.at[c, high, row]
-
-    def column_rows(high):
-        block = column_block(high, y)
-        return over_c(block, block), over_y(lambda r: block, lambda q: block)
-
-    def column_pass(high, copies):
-        passed = []
-        for q, copy in enumerate(copies, 1):
-            copy.wait_recv()
-            block = column_block(high, (y + NY - q) % NY)
-            passed += over_c(block, block)
-        return passed
-
-    mine = column_block(zh, y)
-    high_copies = over_h(lambda h: mine, lambda q: mine)
-    passed, copies = column_rows(zh)
-    col_passed = [passed]
-    waiting = [(zh, copies)]
+    high_t = column_start(1)
+    sar_x_second = spread_x(sar(1)(mp))
+    sar_relays_second, sar_passed_second = relay(sar(1), sar_z[1])
+    column_relay(0, high_u, 1)
+    column_relay(0, high_u, 3)
+    column_pass(0, 0)
+    column_relay(0, high_u, 2)
     first_col = pl.multiple_of(((c * NH + zh) * NY + y) * SHARE, SHARE)
     cvec[...] = jnp.zeros_like(cvec)
     cvec[pl.ds(first_col, SHARE)] = jnp.broadcast_to(slope, (SHARE, 128))
     slope_row = cvec[...].T[0:1]
-    for q in (1, 3, 2):
-        high_copies[q - 1].wait_recv()
-        high = (zh + NH - q) % NH
-        passed, copies = column_rows(high)
-        col_passed.append(passed)
-        waiting.append((high, copies))
-    col_passed[0] += column_pass(*waiting[0])
-    passed = over_c(sar(partner), sar(partner))
-    passed += pass_on(sar, zl, sar_x_copies)
-    col_passed[1] += column_pass(*waiting[1])
-    passed += pass_on(sar, 1 - zl, sar_x_relays)
+    column_relay(1, high_t, 1)
+    column_relay(1, high_t, 3)
+    sar_passed += pass_on(sar(0), zl, sar_x)
+    column_pass(1, 0)
+    column_pass(0, 1)
+    sar_passed += pass_on(sar(0), 1 - zl, sar_relays)
+    column_relay(1, high_t, 2)
+    column_pass(0, 2)
     load_feats[1].wait()
-    arrive(passed)
-    col_passed[2] += column_pass(*waiting[2])
+    arrive(sar_passed)
     every = slice(0, ROWS)
     embed(0, 0, every, rawbuf, 0)
+    unit, inverse = unit_of(rawbuf[every])
+    rows_u[...] = unit.astype(BF16)
+    column_pass(0, 3)
+    column_pass(1, 1)
+    sar_passed_second += pass_on(sar(1), zl, sar_x_second)
+    column_pass(1, 2)
+    sar_passed_second += pass_on(sar(1), 1 - zl, sar_relays_second)
+    arrive(sar_passed_second)
+    column_pass(1, 3)
     embed(1, 0, every, tanbuf, 0)
     unit, inverse = unit_of(rawbuf[every])
     turned, along = turn_of(tanbuf[every], unit, inverse)
-    rows_u[...] = unit.astype(BF16)
     rows_t[...] = turned.astype(BF16)
     row_slope = inverse * along
+
     NT = ((1,), (1,))
     tiles = COLS // TILE
-    for place, (high, copies) in enumerate(waiting):
-        if place == NH - 1:
-            col_passed[place] += column_pass(high, copies)
+    for place, high in enumerate(order):
         arrive(col_passed[place])
         piece = [cols[:, high, :, kind].reshape(NC * BLOCKS, WIDTH) for kind in range(2)]
         for target, rows, kind in ((scores, rows_u, 0), (left_ts, rows_t, 0), (right_ts, rows_u, 1)):
@@ -592,7 +667,7 @@
     bf16 = lambda *size: pltpu.VMEM(size, BF16)
     scratch = [
         bf16(2, ROWS, DEPTH), f32(2, PART, WIDTH), f32(2, PART, WIDTH),
-        bf16(2, 2, NM, PART, WIDTH), bf16(2, NY, NM - 1, QUARTER, WIDTH),
+        bf16(2, 2, 2, NM, PART, WIDE), bf16(2, 2, NY, NM - 1, QUARTER, WIDE),
         f32(ROWS + SHARE, WIDTH), f32(ROWS + SHARE, WIDTH),
         bf16(ROWS, WIDTH), bf16(ROWS, WIDTH),
         bf16(NC, NH, NY, 2, SHARE, WIDTH),
@@ -608,7 +683,7 @@
         f32(2, 2, NY, BLOCK, WIDE), f32(2, NY, BLOCK, WIDE),
         f32(2, NY - 1, BLOCK, WIDE), f32(2, NH, BLOCK, WIDE), f32(2, 2, PART, WIDE),
         f32(NC * NY, 8, 128), f32(NM, 8, 128), f32(8, WIDTH),
-        pltpu.SemaphoreType.DMA((SEMS,)), pltpu.SemaphoreType.DMA((SEMS,)), pltpu.SemaphoreType.DMA((12,)),
+        pltpu.SemaphoreType.DMA((SEMS,)), pltpu.SemaphoreType.DMA((SEMS,)), pltpu.SemaphoreType.DMA((16,)),
     ]
     hess = pl.pallas_call(
         kernel,

time: 126 us -> 122 us (0.968)
  Pallas kernels: 124 us -> 120 us
    pallas_call x1, Pallas kernels: 122 us -> 119 us  [body(): pl.pallas_call(kernel, name='cg_step', out_shape=jax.ShapeDtypeStruct((2...]
where the time goes in v8:
time: 122 us
  Pallas kernels  120 us (98%)
    pallas_call x1, Pallas kernels, body(): pl.pallas_call(kernel, name='cg_step', out_shape=jax.ShapeDtypeStruct((2...  119 us

profile of v8, /device:TPU:1, one launch (start us, length us, event | category | flops | bytes accessed | tf_op | source)
XLA Modules:
  0.0 122.1 jit_solution(4070468420062586331)
XLA Ops:
  0.6 0.0 copy-start.1
  0.6 0.0 copy-start.2
  0.7 0.0 copy-start.3
  0.7 118.6 %cg_step.1.hess = f32[264,768]{1,0:T(8,128)} custom-call(bf16[2,256,1024]{2,1,0:T(8,128)(2,1)} %feats_in.1, bf16[2,128,768]{2,1,0:T(8,128)(2,1)} %proj_in.1, f32[2,128,768]{2,1,0:T(8,128)} %direc.1, f32[2,128,768]{2,1,0:T(8,128)} %resid.1), custom_call_target="tpu_custom_call" | custom-call | tf_op jit(solution)/shard_map/cg_step/pallas_call | solution.py:688
  119.2 0.0 copy-done.1
  119.2 0.0 copy-done.2
  119.3 0.0 copy-done.3
  119.3 0.0 copy-start
  119.3 1.1 copy-done
  120.4 1.6 %updates.1 = (f32[2,128,768]{2,1,0:T(8,128)}, f32[2,128,768]{2,1,0:T(8,128)}, f32[2,128,768]{2,1,0:T(8,128)}) custom-call(f32[264,768]{1,0:T(8,128)S(1)} %copy-done, f32[2,128,768]{2,1,0:T(8,128)S(1)} %copy-done.1, f32[2,128,768]{2,1,0:T(8,128)S(1)} %copy-done.2, f32[2,128,768]{2,1,0:T(8,128)S(1)} %copy-done.3), custom_call_target="tpu_custom_call" | custom-call | tf_op jit(solution)/shard_map/updates/pallas_call | solution.py:700
Async XLA Ops:
  0.6 118.6 %copy-start.1 = (f32[2,128,768]{2,1,0:T(8,128)S(1)}, f32[2,128,768]{2,1,0:T(8,128)}, u32[]{:S(2)}) copy-start(f32[2,128,768]{2,1,0:T(8,128)} %direc.1) | copy-start | bytes 2359300
  0.6 118.6 %copy-start.2 = (f32[2,128,768]{2,1,0:T(8,128)S(1)}, f32[2,128,768]{2,1,0:T(8,128)}, u32[]{:S(2)}) copy-start(f32[2,128,768]{2,1,0:T(8,128)} %resid.1) | copy-start | bytes 2359300
  0.7 118.6 %copy-start.3 = (f32[2,128,768]{2,1,0:T(8,128)S(1)}, f32[2,128,768]{2,1,0:T(8,128)}, u32[]{:S(2)}) copy-start(f32[2,128,768]{2,1,0:T(8,128)} %solu.1) | copy-start | bytes 2359300
  119.3 1.1 copy-start

commit v9 on v8

--- a/solution.py
+++ b/solution.py
@@ -16,7 +16,8 @@
 ROWS, DEPTH, WIDTH = 256, 1024, 768
 PART = DEPTH // NM
 SHARE = ROWS // NM
-COLS = SHARE * NC * NY * NH
+COLS = SHARE * NY * NH
+BOTH = NC * ROWS
 PAIRS = ROWS * NC * NY * NH
 TILE = 256
 SEMS = 288
@@ -81,10 +82,10 @@
     feats_in, proj_in, direc_in, resid_in,
     hess_out,
     feats, direc, resid, weights, quarters, rawbuf, tanbuf, rows_u, rows_t, cols,
-    scores, left_ts, right_ts, dsc, tdsc, cvec,
-    row_slots, plane_stat, z_stat,
-    grad_slots, plane_grad, z_grad,
-    row_part, x_recv, l_recv, col_away, col_part, col_low, col_recv, y_recv, z_recv,
+    scores, left_ts, right_ts, dsc, tdsc, cvec, row_info,
+    core_rows, row_slots, y_stat, z_stat,
+    core_grad, grad_slots, y_grad, z_grad,
+    row_part, row_away, row_got, x_recv, l_recv, col_part, col_low, y_recv, z_recv,
     grad_cols, grad_rows, tdz, part_hess, core_hess, y_hess, z_hess, hess,
     norm_p, norm_m, info,
     send_sem, recv_sem, load_sem,
@@ -254,12 +255,11 @@
             into[first : first + total.shape[0], span] = total
 
     def column_block(kind, high, row):
-        return cols.at[c, high, row, kind]
+        return cols.at[high, row, kind]
 
     def column_rows(kind, high):
         block = column_block(kind, high, y)
-        col_passed[high_place(high)] += over_c(block, block)
-        waiting[kind].append((high, over_y(lambda r: block, lambda q: block)))
+        col_copies.extend(over_y(lambda r: block, lambda q: block))
 
     def column_start(kind):
         block = column_block(kind, zh, y)
@@ -269,25 +269,9 @@
 
     def column_relay(kind, copies, q):
         copies[q - 1].wait_recv()
-        column_rows(kind, highs[q])
-
-    def column_pass(kind, place):
-        high, copies = waiting[kind][place]
-        for q, copy in enumerate(copies, 1):
-            copy.wait_recv()
-            block = column_block(kind, high, (y + NY - q) % NY)
-            col_passed[place] += over_c(block, block)
-
-    highs = {q: (zh + NH - q) % NH for q in (0, 1, 3, 2)}
-    order = list(highs.values())
-
-    def high_place(high):
-        return next(place for place, other in enumerate(order) if other is high)
-
-    waiting = [[], []]
-    col_passed = [[], [], [], []]
-    highs[0] = order[0] = zh
-
+        column_rows(kind, (zh + NH - q) % NH)
+
+    col_copies = []
     quarter_copies = quarter_start(0)
     z_copies = over_z(optical(0))
     x_copies = spread_x(optical(0)(mp))
@@ -316,7 +300,7 @@
     share = slice(ROWS, ROWS + SHARE)
     embed(0, 1, own, rawbuf, ROWS)
     unit, inverse = unit_of(rawbuf[share])
-    cols[c, zh, y, 0] = unit.astype(BF16)
+    cols[zh, y, 0] = unit.astype(BF16)
     high_u = column_start(0)
     passed_second += pass_on(optical(1), zl, x_second)
     passed_second += quarter_pass(1, quarter_second)
@@ -327,60 +311,62 @@
     embed(1, 1, own, tanbuf, ROWS)
     unit, inverse = unit_of(rawbuf[share])
     turned, along = turn_of(tanbuf[share], unit, inverse)
-    cols[c, zh, y, 1] = turned.astype(BF16)
+    cols[zh, y, 1] = turned.astype(BF16)
     slope = inverse * along
     high_t = column_start(1)
     sar_x_second = spread_x(sar(1)(mp))
     sar_relays_second, sar_passed_second = relay(sar(1), sar_z[1])
     column_relay(0, high_u, 1)
     column_relay(0, high_u, 3)
-    column_pass(0, 0)
     column_relay(0, high_u, 2)
-    first_col = pl.multiple_of(((c * NH + zh) * NY + y) * SHARE, SHARE)
+    first_col = pl.multiple_of((zh * NY + y) * SHARE, SHARE)
     cvec[...] = jnp.zeros_like(cvec)
     cvec[pl.ds(first_col, SHARE)] = jnp.broadcast_to(slope, (SHARE, 128))
     slope_row = cvec[...].T[0:1]
     column_relay(1, high_t, 1)
     column_relay(1, high_t, 3)
     sar_passed += pass_on(sar(0), zl, sar_x)
-    column_pass(1, 0)
-    column_pass(0, 1)
     sar_passed += pass_on(sar(0), 1 - zl, sar_relays)
     column_relay(1, high_t, 2)
-    column_pass(0, 2)
     load_feats[1].wait()
     arrive(sar_passed)
     every = slice(0, ROWS)
     embed(0, 0, every, rawbuf, 0)
     unit, inverse = unit_of(rawbuf[every])
-    rows_u[...] = unit.astype(BF16)
-    column_pass(0, 3)
-    column_pass(1, 1)
+    rows_u[c] = unit.astype(BF16)
+    unit_copies = over_c(rows_u.at[c], rows_u.at[c])
     sar_passed_second += pass_on(sar(1), zl, sar_x_second)
-    column_pass(1, 2)
     sar_passed_second += pass_on(sar(1), 1 - zl, sar_relays_second)
     arrive(sar_passed_second)
-    column_pass(1, 3)
     embed(1, 0, every, tanbuf, 0)
     unit, inverse = unit_of(rawbuf[every])
     turned, along = turn_of(tanbuf[every], unit, inverse)
-    rows_t[...] = turned.astype(BF16)
+    rows_t[c] = turned.astype(BF16)
+    turned_copies = over_c(rows_t.at[c], rows_t.at[c])
     row_slope = inverse * along
+    row_slope = jnp.concatenate([jnp.where(c == core, row_slope, 0.0) for core in range(NC)], 0)
 
     NT = ((1,), (1,))
     tiles = COLS // TILE
-    for place, high in enumerate(order):
-        arrive(col_passed[place])
-        piece = [cols[:, high, :, kind].reshape(NC * BLOCKS, WIDTH) for kind in range(2)]
-        for target, rows, kind in ((scores, rows_u, 0), (left_ts, rows_t, 0), (right_ts, rows_u, 1)):
-            product = LOGIT_SCALE * dot(rows[...], piece[kind], NT)
-            for core in range(NC):
-                start = pl.multiple_of((core * NH + high) * BLOCKS, BLOCKS)
-                target[:, pl.ds(start, BLOCKS)] = product[:, core * BLOCKS : (core + 1) * BLOCKS]
+    arrive(unit_copies)
+    arrive(col_copies)
+
+    def score_tile(target, rows, kind, tile):
+        piece = cols[2 * tile : 2 * tile + 2, :, kind].reshape(TILE, WIDTH)
+        product = dot(rows[...].reshape(BOTH, WIDTH), piece, NT)
+        target[:, tile * TILE : (tile + 1) * TILE] = LOGIT_SCALE * product
+
+    for tile in range(tiles):
+        score_tile(scores, rows_u, 0, tile)
+        score_tile(right_ts, rows_u, 1, tile)
     row_max = jnp.max(scores[...], 1, keepdims=True)
     col_max = jnp.max(scores[...], 0, keepdims=True)
-    row_sum = jnp.zeros((ROWS, 1), F32)
-    row_weighted = jnp.zeros((ROWS, 1), F32)
+    arrive(turned_copies)
+    for tile in range(tiles):
+        score_tile(left_ts, rows_t, 0, tile)
+
+    row_sum = jnp.zeros((BOTH, 1), F32)
+    row_weighted = jnp.zeros((BOTH, 1), F32)
     col_sum, col_weighted = [], []
     for tile in range(tiles):
         span = slice(tile * TILE, (tile + 1) * TILE)
@@ -394,11 +380,10 @@
         col_weighted.append(jnp.sum(weight * tscore, 0, keepdims=True))
     load_resid.wait()
     resid_norm = jnp.sum(resid[...] * resid[...])
-    constant = lambda value: jnp.full((ROWS, 1), value, F32)
-    row_slots[pl.ds(mp, 1)] = pack_lanes(
-        [row_max, row_sum, row_weighted, constant(resid_norm)]
+    core_rows[pl.ds(c, 1)] = pack_lanes(
+        [row_max, row_sum, row_weighted, row_slope, jnp.full((BOTH, 1), resid_norm, F32)]
     )[None]
-    plane_stat[pl.ds(c * NY + y, 1)] = fold(
+    y_stat[pl.ds(y, 1)] = fold(
         [col_max, jnp.concatenate(col_sum, 1), jnp.concatenate(col_weighted, 1), slope_row]
     )[None]
 
@@ -411,34 +396,47 @@
     def sum_slots(slots, count):
         return functools.reduce(jnp.add, [slots[k] for k in range(count)])
 
+    def spread_y(slots):
+        return over_y(lambda r: slots.at[y], lambda q: slots.at[y])
+
     def spread_h(slots):
         return over_h(lambda h: slots.at[zh], lambda q: slots.at[zh])
 
     def spread_m(slots):
         return over_m(lambda m: slots.at[mp], lambda q: slots.at[mp])
 
-    copies = over_plane(plane_stat)
+    core_copies = over_c(core_rows.at[c], core_rows.at[c])
+    copies = spread_y(y_stat)
+
+    def join_rows(slots, count):
+        parts = [slots[k] for k in range(count)]
+        return softmax_join([(part[0:1], part[1:2], part[2:3]) for part in parts])
+
+    arrive(core_copies)
+    slopes = core_rows[0, 3:4] + core_rows[1, 3:4]
+    joined = join_rows(core_rows, NC)
+    row_slots[pl.ds(mp, 1)] = jnp.concatenate(
+        [*joined, core_rows[0, 4:5], jnp.zeros((4, BOTH), F32)], 0
+    )[None]
     row_copies = spread_m(row_slots)
     arrive(copies)
-    z_stat[pl.ds(zh, 1)] = fold(join_columns(plane_stat, NC * NY))[None]
+    z_stat[pl.ds(zh, 1)] = fold(join_columns(y_stat, NY))[None]
     copies = spread_h(z_stat)
     arrive(row_copies)
-    parts = [row_slots[k] for k in range(NM)]
-    top, total, weighted = softmax_join([(part[0:1], part[1:2], part[2:3]) for part in parts])
-    norms = functools.reduce(jnp.add, [part[3:4] for part in parts])
-    norm_old = norms[0:1, 0:1]
-    row_info = unpack_lanes(jnp.concatenate([top + jnp.log(total), weighted / total], 0))
+    top, total, weighted = join_rows(row_slots, NM)
+    norm_old = functools.reduce(jnp.add, [row_slots[k, 3:4] for k in range(NM)])[0:1, 0:1]
+    row_info[...] = unpack_lanes(jnp.concatenate([top + jnp.log(total), weighted / total, slopes], 0))
     row_lse, row_dot = row_info[:, 0:1], row_info[:, 1:2]
     arrive(copies)
     top, total, weighted, slopes = join_columns(z_stat, NH)
     col_lse, col_dot = top + jnp.log(total), weighted / total
     col_slope = unpack_lanes(slopes)
 
-    row_ids = lax.broadcasted_iota(jnp.int32, (ROWS, TILE), 0)
-    col_ids = lax.broadcasted_iota(jnp.int32, (ROWS, TILE), 1)
-    offset = mp * SHARE - first_col
-    row_along = jnp.zeros((ROWS, 1), F32)
-    row_turned = jnp.zeros((ROWS, 1), F32)
+    row_ids = lax.broadcasted_iota(jnp.int32, (BOTH, TILE), 0)
+    col_ids = lax.broadcasted_iota(jnp.int32, (BOTH, TILE), 1)
+    offset = c * ROWS + mp * SHARE - first_col
+    row_along = jnp.zeros((BOTH, 1), F32)
+    row_turned = jnp.zeros((BOTH, 1), F32)
     col_along, col_turned = [], []
     for tile in range(tiles):
         span = slice(tile * TILE, (tile + 1) * TILE)
@@ -459,52 +457,56 @@
         row_turned += jnp.sum(wide * left, 1, keepdims=True)
         col_along.append(jnp.sum(wide * score, 0, keepdims=True))
         col_turned.append(jnp.sum(wide * right, 0, keepdims=True))
-    grad_slots[pl.ds(mp, 1)] = pack_lanes([row_along, row_turned])[None]
-    plane_grad[pl.ds(c * NY + y, 1)] = fold([jnp.concatenate(col_along, 1), jnp.concatenate(col_turned, 1)])[None]
-    grad_copies = spread_m(grad_slots)
-    plane_copies = over_plane(plane_grad)
+    core_grad[pl.ds(c, 1)] = pack_lanes([row_along, row_turned])[None]
+    y_grad[pl.ds(y, 1)] = fold([jnp.concatenate(col_along, 1), jnp.concatenate(col_turned, 1)])[None]
+    core_copies = over_c(core_grad.at[c], core_grad.at[c])
+    y_grad_copies = spread_y(y_grad)
 
     TN = ((0,), (0,))
     cvec[...] = col_slope
 
-    def column_terms(core, high):
-        start = pl.multiple_of((core * NH + high) * BLOCKS, BLOCKS)
+    def column_terms(high):
+        start = pl.multiple_of(high * BLOCKS, BLOCKS)
         d_low, t_low = dsc[:, pl.ds(start, BLOCKS)], tdsc[:, pl.ds(start, BLOCKS)]
-        total = dot(t_low, rows_u[...], TN) + dot(d_low, rows_t[...], TN)
-        total -= cvec[pl.ds(start, BLOCKS), 0:1] * dot(d_low, rows_u[...], TN)
+        units, turns = rows_u[...].reshape(BOTH, WIDTH), rows_t[...].reshape(BOTH, WIDTH)
+        total = dot(t_low, units, TN) + dot(d_low, turns, TN)
+        total -= cvec[pl.ds(start, BLOCKS), 0:1] * dot(d_low, units, TN)
         return (LOGIT_SCALE * total).reshape(NY, SHARE, WIDTH)
 
+    def row_terms(core, into):
+        here = pl.ds(pl.multiple_of(core * ROWS, ROWS), ROWS)
+        d_low, t_low, slope = dsc[here], tdsc[here], row_info[here, 2:3]
+        for tile in range(WIDTH // TILE):
+            span = slice(tile * TILE, (tile + 1) * TILE)
+            u_piece = cols[:, :, 0, :, span].reshape(COLS, TILE)
+            t_piece = cols[:, :, 1, :, span].reshape(COLS, TILE)
+            total = dot(t_low, u_piece) + dot(d_low, t_piece) - slope * dot(d_low, u_piece)
+            into[:, :, :, span] = (LOGIT_SCALE * total).reshape(NL, NX, SHARE, TILE)
+
     steps = (2, 1, 3, 0)
-    passed = []
-
-    def away(place):
-        col_away[place] = column_terms(1 - c, h_at(steps[place]))
-        passed.extend(over_c(col_away.at[place], col_recv.at[place]))
-
-    away(0)
-    away(1)
-
-    for tile in range(WIDTH // TILE):
-        span = slice(tile * TILE, (tile + 1) * TILE)
-        u_piece = cols[:, :, :, 0, :, span].reshape(COLS, TILE)
-        t_piece = cols[:, :, :, 1, :, span].reshape(COLS, TILE)
-        total = dot(tdsc[...], u_piece) + dot(dsc[...], t_piece) - row_slope * dot(dsc[...], u_piece)
-        row_part[:, :, :, span] = (LOGIT_SCALE * total).reshape(NL, NX, SHARE, TILE)
-    x_copies = over_x(lambda k: row_part.at[:, k], lambda q: x_recv.at[q - 1])
-
     y_copies = []
-    for place, step in enumerate(steps):
-        terms = column_terms(c, h_at(step))
-        passed[place].wait_recv()
-        terms = terms + col_recv[place]
+
+    def column_out(place):
+        terms = column_terms(h_at(steps[place]))
         col_low[place] = terms.astype(BF16)
         col_part[place] = terms
         y_copies.append(over_y(lambda r: col_low.at[place, r], lambda q: y_recv.at[place, q - 1]))
-        if place + 2 < NH:
-            away(place + 2)
-
-    arrive(plane_copies)
-    z_grad[pl.ds(zh, 1)] = sum_slots(plane_grad, NC * NY)[None]
+
+    column_out(0)
+    row_terms(1 - c, row_away)
+    away_copies = over_c(row_away, row_got)
+    column_out(1)
+    row_terms(c, row_part)
+    arrive(away_copies)
+    row_part[...] += row_got[...]
+    x_copies = over_x(lambda k: row_part.at[:, k], lambda q: x_recv.at[q - 1])
+    column_out(2)
+    column_out(3)
+    arrive(core_copies)
+    grad_slots[pl.ds(mp, 1)] = sum_slots(core_grad, NC)[None]
+    grad_copies = spread_m(grad_slots)
+    arrive(y_grad_copies)
+    z_grad[pl.ds(zh, 1)] = sum_slots(y_grad, NY)[None]
     z_grad_copies = spread_h(z_grad)
 
     def column_sum(place):
@@ -537,7 +539,8 @@
         return over_m(lambda m: block, lambda q: block)
 
     arrive(l_copies)
-    tdz[0, mp] = finish(rawbuf[own], tanbuf[own], row_part[zl, x] + l_recv[...], grad_rows[own])
+    mine = pl.ds(pl.multiple_of(c * ROWS + mp * SHARE, SHARE), SHARE)
+    tdz[0, mp] = finish(rawbuf[own], tanbuf[own], row_part[zl, x] + l_recv[...], grad_rows[mine])
     sar_copies = spread_tdz(0)
     arrive(z_grad_copies)
     grad_cols[...] = unpack_lanes(unfold(sum_slots(z_grad, NH), 2))
@@ -669,16 +672,17 @@
         bf16(2, ROWS, DEPTH), f32(2, PART, WIDTH), f32(2, PART, WIDTH),
         bf16(2, 2, 2, NM, PART, WIDE), bf16(2, 2, NY, NM - 1, QUARTER, WIDE),
         f32(ROWS + SHARE, WIDTH), f32(ROWS + SHARE, WIDTH),
-        bf16(ROWS, WIDTH), bf16(ROWS, WIDTH),
-        bf16(NC, NH, NY, 2, SHARE, WIDTH),
-        f32(ROWS, COLS), f32(ROWS, COLS), f32(ROWS, COLS),
-        bf16(ROWS, COLS), bf16(ROWS, COLS), f32(COLS, 128),
-        f32(NM, 8, ROWS), f32(NC * NY, 8, COLS // 2), f32(NH, 8, COLS // 2),
-        f32(NM, 8, ROWS), f32(NC * NY, 8, COLS // 4), f32(NH, 8, COLS // 4),
-        f32(NL, NX, SHARE, WIDTH), f32(NX - 1, NL, SHARE, WIDTH), f32(SHARE, WIDTH),
-        f32(NH, NY, SHARE, WIDTH), f32(NH, NY, SHARE, WIDTH), bf16(NH, NY, SHARE, WIDTH),
-        f32(NH, NY, SHARE, WIDTH), bf16(NH, NY - 1, SHARE, WIDTH), f32(NH - 1, SHARE, WIDTH),
-        f32(COLS, 128), f32(ROWS, 128),
+        bf16(NC, ROWS, WIDTH), bf16(NC, ROWS, WIDTH),
+        bf16(NH, NY, 2, SHARE, WIDTH),
+        f32(BOTH, COLS), f32(BOTH, COLS), f32(BOTH, COLS),
+        bf16(BOTH, COLS), bf16(BOTH, COLS), f32(COLS, 128), f32(BOTH, 128),
+        f32(NC, 8, BOTH), f32(NM, 8, BOTH), f32(NY, 8, COLS // 2), f32(NH, 8, COLS // 2),
+        f32(NC, 8, BOTH), f32(NM, 8, BOTH), f32(NY, 8, COLS // 4), f32(NH, 8, COLS // 4),
+        f32(NL, NX, SHARE, WIDTH), f32(NL, NX, SHARE, WIDTH), f32(NL, NX, SHARE, WIDTH),
+        f32(NX - 1, NL, SHARE, WIDTH), f32(SHARE, WIDTH),
+        f32(NH, NY, SHARE, WIDTH), bf16(NH, NY, SHARE, WIDTH),
+        bf16(NH, NY - 1, SHARE, WIDTH), f32(NH - 1, SHARE, WIDTH),
+        f32(COLS, 128), f32(BOTH, 128),
         bf16(2, NM, SHARE, WIDTH),
         f32(2, 2, NY, BLOCK, WIDE), f32(2, NY, BLOCK, WIDE),
         f32(2, NY - 1, BLOCK, WIDE), f32(2, NH, BLOCK, WIDE), f32(2, 2, PART, WIDE),

time: 122 us -> 120 us (0.984)
  Pallas kernels: 120 us -> 118 us
    pallas_call x1, Pallas kernels: 119 us -> 116 us  [body(): pl.pallas_call(kernel, name='cg_step', out_shape=jax.ShapeDtypeStruct((2...]
where the time goes in v9:
time: 120 us
  Pallas kernels  118 us (98%)
    pallas_call x1, Pallas kernels, body(): pl.pallas_call(kernel, name='cg_step', out_shape=jax.ShapeDtypeStruct((2...  116 us

profile of v9, /device:TPU:1, one launch (start us, length us, event | category | flops | bytes accessed | tf_op | source)
XLA Modules:
  0.0 119.8 jit_solution(3348265073311624466)
XLA Ops:
  0.6 0.0 copy-start.1
  0.6 0.0 copy-start.2
  0.7 0.0 copy-start.3
  0.7 116.4 %cg_step.1.hess = f32[264,768]{1,0:T(8,128)} custom-call(bf16[2,256,1024]{2,1,0:T(8,128)(2,1)} %feats_in.1, bf16[2,128,768]{2,1,0:T(8,128)(2,1)} %proj_in.1, f32[2,128,768]{2,1,0:T(8,128)} %direc.1, f32[2,128,768]{2,1,0:T(8,128)} %resid.1), custom_call_target="tpu_custom_call" | custom-call | tf_op jit(solution)/shard_map/cg_step/pallas_call | solution.py:692
  117.0 0.0 copy-done.1
  117.0 0.0 copy-done.2
  117.0 0.0 copy-done.3
  117.1 0.0 copy-start
  117.1 1.1 copy-done
  118.2 1.6 %updates.1 = (f32[2,128,768]{2,1,0:T(8,128)}, f32[2,128,768]{2,1,0:T(8,128)}, f32[2,128,768]{2,1,0:T(8,128)}) custom-call(f32[264,768]{1,0:T(8,128)S(1)} %copy-done, f32[2,128,768]{2,1,0:T(8,128)S(1)} %copy-done.1, f32[2,128,768]{2,1,0:T(8,128)S(1)} %copy-done.2, f32[2,128,768]{2,1,0:T(8,128)S(1)} %copy-done.3), custom_call_target="tpu_custom_call" | custom-call | tf_op jit(solution)/shard_map/updates/pallas_call | solution.py:704
Async XLA Ops:
  0.6 116.4 %copy-start.1 = (f32[2,128,768]{2,1,0:T(8,128)S(1)}, f32[2,128,768]{2,1,0:T(8,128)}, u32[]{:S(2)}) copy-start(f32[2,128,768]{2,1,0:T(8,128)} %direc.1) | copy-start | bytes 2359300
  0.6 116.4 %copy-start.2 = (f32[2,128,768]{2,1,0:T(8,128)S(1)}, f32[2,128,768]{2,1,0:T(8,128)}, u32[]{:S(2)}) copy-start(f32[2,128,768]{2,1,0:T(8,128)} %resid.1) | copy-start | bytes 2359300
  0.7 116.4 %copy-start.3 = (f32[2,128,768]{2,1,0:T(8,128)S(1)}, f32[2,128,768]{2,1,0:T(8,128)}, u32[]{:S(2)}) copy-start(f32[2,128,768]{2,1,0:T(8,128)} %solu.1) | copy-start | bytes 2359300
  117.1 1.1 copy-start

commit v10 on v9

--- a/solution.py
+++ b/solution.py
@@ -275,24 +275,24 @@
     quarter_copies = quarter_start(0)
     z_copies = over_z(optical(0))
     x_copies = spread_x(optical(0)(mp))
+    quarter_second = quarter_start(1)
+    z_second = over_z(optical(1))
+    x_second = spread_x(optical(1)(mp))
     for copy in load_proj[1]:
         copy.wait()
     load_direc[1].wait()
     own_direction(0)
+    sar_z = [over_z(sar(kind)) for kind in range(2)]
     passed_first, quarter_copies = quarter_rows(0, quarter_copies)
-    quarter_second = quarter_start(1)
-    z_second = over_z(optical(1))
-    x_second = spread_x(optical(1)(mp))
     relays, passed = relay(optical(0), z_copies)
     passed_first += passed
-    sar_z = [over_z(sar(kind)) for kind in range(2)]
+    passed_second, quarter_second = quarter_rows(1, quarter_second)
+    relays_second, passed = relay(optical(1), z_second)
+    passed_second += passed
     passed_first += pass_on(optical(0), zl, x_copies)
-    passed_second, quarter_second = quarter_rows(1, quarter_second)
+    sar_x = spread_x(sar(0)(mp))
     passed_first += quarter_pass(0, quarter_copies)
     passed_first += pass_on(optical(0), 1 - zl, relays)
-    relays_second, passed = relay(optical(1), z_second)
-    passed_second += passed
-    sar_x = spread_x(sar(0)(mp))
     load_feats[0].wait()
     arrive(passed_first)
     assemble(0)
@@ -303,9 +303,11 @@
     cols[zh, y, 0] = unit.astype(BF16)
     high_u = column_start(0)
     passed_second += pass_on(optical(1), zl, x_second)
+    sar_relays, sar_passed = relay(sar(0), sar_z[0])
     passed_second += quarter_pass(1, quarter_second)
     passed_second += pass_on(optical(1), 1 - zl, relays_second)
-    sar_relays, sar_passed = relay(sar(0), sar_z[0])
+    sar_x_second = spread_x(sar(1)(mp))
+    sar_relays_second, sar_passed_second = relay(sar(1), sar_z[1])
     arrive(passed_second)
     assemble(1)
     embed(1, 1, own, tanbuf, ROWS)
@@ -314,8 +316,6 @@
     cols[zh, y, 1] = turned.astype(BF16)
     slope = inverse * along
     high_t = column_start(1)
-    sar_x_second = spread_x(sar(1)(mp))
-    sar_relays_second, sar_passed_second = relay(sar(1), sar_z[1])
     column_relay(0, high_u, 1)
     column_relay(0, high_u, 3)
     column_relay(0, high_u, 2)
@@ -496,18 +496,18 @@
     row_terms(1 - c, row_away)
     away_copies = over_c(row_away, row_got)
     column_out(1)
+    arrive(core_copies)
+    grad_slots[pl.ds(mp, 1)] = sum_slots(core_grad, NC)[None]
+    grad_copies = spread_m(grad_slots)
     row_terms(c, row_part)
     arrive(away_copies)
     row_part[...] += row_got[...]
     x_copies = over_x(lambda k: row_part.at[:, k], lambda q: x_recv.at[q - 1])
     column_out(2)
-    column_out(3)
-    arrive(core_copies)
-    grad_slots[pl.ds(mp, 1)] = sum_slots(core_grad, NC)[None]
-    grad_copies = spread_m(grad_slots)
     arrive(y_grad_copies)
     z_grad[pl.ds(zh, 1)] = sum_slots(y_grad, NY)[None]
     z_grad_copies = spread_h(z_grad)
+    column_out(3)
 
     def column_sum(place):
         arrive(y_copies[place])

time: 120 us -> 119 us (level)
  no operation moved by 1% of the time
where the time goes in v10:
time: 119 us
  Pallas kernels  117 us (98%)
    pallas_call x1, Pallas kernels, body(): pl.pallas_call(kernel, name='cg_step', out_shape=jax.ShapeDtypeStruct((2...  115 us

profile of v10, /device:TPU:1, one launch (start us, length us, event | category | flops | bytes accessed | tf_op | source)
XLA Modules:
  0.0 118.8 jit_solution(10624079160192375017)
XLA Ops:
  0.6 0.0 copy-start.1
  0.6 0.0 copy-start.2
  0.7 0.0 copy-start.3
  0.7 115.4 %cg_step.1.hess = f32[264,768]{1,0:T(8,128)} custom-call(bf16[2,256,1024]{2,1,0:T(8,128)(2,1)} %feats_in.1, bf16[2,128,768]{2,1,0:T(8,128)(2,1)} %proj_in.1, f32[2,128,768]{2,1,0:T(8,128)} %direc.1, f32[2,128,768]{2,1,0:T(8,128)} %resid.1), custom_call_target="tpu_custom_call" | custom-call | tf_op jit(solution)/shard_map/cg_step/pallas_call | solution.py:692
  116.0 0.0 copy-done.1
  116.0 0.0 copy-done.2
  116.1 0.0 copy-done.3
  116.1 0.0 copy-start
  116.1 1.1 copy-done
  117.2 1.6 %updates.1 = (f32[2,128,768]{2,1,0:T(8,128)}, f32[2,128,768]{2,1,0:T(8,128)}, f32[2,128,768]{2,1,0:T(8,128)}) custom-call(f32[264,768]{1,0:T(8,128)S(1)} %copy-done, f32[2,128,768]{2,1,0:T(8,128)S(1)} %copy-done.1, f32[2,128,768]{2,1,0:T(8,128)S(1)} %copy-done.2, f32[2,128,768]{2,1,0:T(8,128)S(1)} %copy-done.3), custom_call_target="tpu_custom_call" | custom-call | tf_op jit(solution)/shard_map/updates/pallas_call | solution.py:704
Async XLA Ops:
  0.6 115.4 %copy-start.1 = (f32[2,128,768]{2,1,0:T(8,128)S(1)}, f32[2,128,768]{2,1,0:T(8,128)}, u32[]{:S(2)}) copy-start(f32[2,128,768]{2,1,0:T(8,128)} %direc.1) | copy-start | bytes 2359300
  0.6 115.4 %copy-start.2 = (f32[2,128,768]{2,1,0:T(8,128)S(1)}, f32[2,128,768]{2,1,0:T(8,128)}, u32[]{:S(2)}) copy-start(f32[2,128,768]{2,1,0:T(8,128)} %resid.1) | copy-start | bytes 2359300
  0.7 115.4 %copy-start.3 = (f32[2,128,768]{2,1,0:T(8,128)S(1)}, f32[2,128,768]{2,1,0:T(8,128)}, u32[]{:S(2)}) copy-start(f32[2,128,768]{2,1,0:T(8,128)} %solu.1) | copy-start | bytes 2359300
  116.1 1.1 copy-start

commit v11 on v10

--- a/solution.py
+++ b/solution.py
@@ -82,7 +82,7 @@
     feats_in, proj_in, direc_in, resid_in,
     hess_out,
     feats, direc, resid, weights, quarters, rawbuf, tanbuf, rows_u, rows_t, cols,
-    scores, left_ts, right_ts, dsc, tdsc, cvec, row_info,
+    scores, left_ts, right_ts, row_weight, col_weight, dsc, tdsc, cvec, row_info,
     core_rows, row_slots, y_stat, z_stat,
     core_grad, grad_slots, y_grad, z_grad,
     row_part, row_away, row_got, x_recv, l_recv, col_part, col_low, y_recv, z_recv,
@@ -259,7 +259,7 @@
 
     def column_rows(kind, high):
         block = column_block(kind, high, y)
-        col_copies.extend(over_y(lambda r: block, lambda q: block))
+        col_copies[kind].extend(over_y(lambda r: block, lambda q: block))
 
     def column_start(kind):
         block = column_block(kind, zh, y)
@@ -271,7 +271,7 @@
         copies[q - 1].wait_recv()
         column_rows(kind, (zh + NH - q) % NH)
 
-    col_copies = []
+    col_copies = ([], [])
     quarter_copies = quarter_start(0)
     z_copies = over_z(optical(0))
     x_copies = spread_x(optical(0)(mp))
@@ -337,6 +337,30 @@
     unit_copies = over_c(rows_u.at[c], rows_u.at[c])
     sar_passed_second += pass_on(sar(1), zl, sar_x_second)
     sar_passed_second += pass_on(sar(1), 1 - zl, sar_relays_second)
+    NT = ((1,), (1,))
+    tiles = COLS // TILE
+
+    def score_tile(target, rows, kind, tile):
+        piece = cols[2 * tile : 2 * tile + 2, :, kind].reshape(TILE, WIDTH)
+        product = dot(rows[...].reshape(BOTH, WIDTH), piece, NT)
+        target[:, tile * TILE : (tile + 1) * TILE] = LOGIT_SCALE * product
+
+    arrive(unit_copies)
+    arrive(col_copies[0])
+    for tile in range(tiles):
+        score_tile(scores, rows_u, 0, tile)
+    row_max = jnp.max(scores[...], 1, keepdims=True)
+    col_max = jnp.max(scores[...], 0, keepdims=True)
+    row_sum = jnp.zeros((BOTH, 1), F32)
+    col_sum = []
+    for tile in range(tiles):
+        span = slice(tile * TILE, (tile + 1) * TILE)
+        weight = jnp.exp(scores[:, span] - row_max)
+        row_weight[:, span] = weight
+        row_sum += jnp.sum(weight, 1, keepdims=True)
+        weight = jnp.exp(scores[:, span] - col_max[:, span])
+        col_weight[:, span] = weight
+        col_sum.append(jnp.sum(weight, 0, keepdims=True))
     arrive(sar_passed_second)
     embed(1, 0, every, tanbuf, 0)
     unit, inverse = unit_of(rawbuf[every])
@@ -345,39 +369,18 @@
     turned_copies = over_c(rows_t.at[c], rows_t.at[c])
     row_slope = inverse * along
     row_slope = jnp.concatenate([jnp.where(c == core, row_slope, 0.0) for core in range(NC)], 0)
-
-    NT = ((1,), (1,))
-    tiles = COLS // TILE
-    arrive(unit_copies)
-    arrive(col_copies)
-
-    def score_tile(target, rows, kind, tile):
-        piece = cols[2 * tile : 2 * tile + 2, :, kind].reshape(TILE, WIDTH)
-        product = dot(rows[...].reshape(BOTH, WIDTH), piece, NT)
-        target[:, tile * TILE : (tile + 1) * TILE] = LOGIT_SCALE * product
-
+    arrive(col_copies[1])
     for tile in range(tiles):
-        score_tile(scores, rows_u, 0, tile)
         score_tile(right_ts, rows_u, 1, tile)
-    row_max = jnp.max(scores[...], 1, keepdims=True)
-    col_max = jnp.max(scores[...], 0, keepdims=True)
     arrive(turned_copies)
-    for tile in range(tiles):
-        score_tile(left_ts, rows_t, 0, tile)
-
-    row_sum = jnp.zeros((BOTH, 1), F32)
     row_weighted = jnp.zeros((BOTH, 1), F32)
-    col_sum, col_weighted = [], []
+    col_weighted = []
     for tile in range(tiles):
         span = slice(tile * TILE, (tile + 1) * TILE)
-        score = scores[:, span]
+        score_tile(left_ts, rows_t, 0, tile)
         tscore = left_ts[:, span] + right_ts[:, span]
-        weight = jnp.exp(score - row_max)
-        row_sum += jnp.sum(weight, 1, keepdims=True)
-        row_weighted += jnp.sum(weight * tscore, 1, keepdims=True)
-        weight = jnp.exp(score - col_max[:, span])
-        col_sum.append(jnp.sum(weight, 0, keepdims=True))
-        col_weighted.append(jnp.sum(weight * tscore, 0, keepdims=True))
+        row_weighted += jnp.sum(row_weight[:, span] * tscore, 1, keepdims=True)
+        col_weighted.append(jnp.sum(col_weight[:, span] * tscore, 0, keepdims=True))
     load_resid.wait()
     resid_norm = jnp.sum(resid[...] * resid[...])
     core_rows[pl.ds(c, 1)] = pack_lanes(
@@ -674,7 +677,7 @@
         f32(ROWS + SHARE, WIDTH), f32(ROWS + SHARE, WIDTH),
         bf16(NC, ROWS, WIDTH), bf16(NC, ROWS, WIDTH),
         bf16(NH, NY, 2, SHARE, WIDTH),
-        f32(BOTH, COLS), f32(BOTH, COLS), f32(BOTH, COLS),
+        f32(BOTH, COLS), f32(BOTH, COLS), f32(BOTH, COLS), f32(BOTH, COLS), f32(BOTH, COLS),
         bf16(BOTH, COLS), bf16(BOTH, COLS), f32(COLS, 128), f32(BOTH, 128),
         f32(NC, 8, BOTH), f32(NM, 8, BOTH), f32(NY, 8, COLS // 2), f32(NH, 8, COLS // 2),
         f32(NC, 8, BOTH), f32(NM, 8, BOTH), f32(NY, 8, COLS // 4), f32(NH, 8, COLS // 4),

time: 119 us -> 119 us (level)
  no operation moved by 1% of the time
where the time goes in v11:
time: 119 us
  Pallas kernels  117 us (98%)
    pallas_call x1, Pallas kernels, body(): pl.pallas_call(kernel, name='cg_step', out_shape=jax.ShapeDtypeStruct((2...  115 us

profile of v11, /device:TPU:1, one launch (start us, length us, event | category | flops | bytes accessed | tf_op | source)
XLA Modules:
  0.0 118.6 jit_solution(6437880486000794156)
XLA Ops:
  0.6 0.0 copy-start.1
  0.6 0.0 copy-start.2
  0.7 0.0 copy-start.3
  0.7 115.2 %cg_step.1.hess = f32[264,768]{1,0:T(8,128)} custom-call(bf16[2,256,1024]{2,1,0:T(8,128)(2,1)} %feats_in.1, bf16[2,128,768]{2,1,0:T(8,128)(2,1)} %proj_in.1, f32[2,128,768]{2,1,0:T(8,128)} %direc.1, f32[2,128,768]{2,1,0:T(8,128)} %resid.1), custom_call_target="tpu_custom_call" | custom-call | tf_op jit(solution)/shard_map/cg_step/pallas_call | solution.py:695
  115.8 0.0 copy-done.1
  115.8 0.0 copy-done.2
  115.8 0.0 copy-done.3
  115.9 0.0 copy-start
  115.9 1.1 copy-done
  117.0 1.6 %updates.1 = (f32[2,128,768]{2,1,0:T(8,128)}, f32[2,128,768]{2,1,0:T(8,128)}, f32[2,128,768]{2,1,0:T(8,128)}) custom-call(f32[264,768]{1,0:T(8,128)S(1)} %copy-done, f32[2,128,768]{2,1,0:T(8,128)S(1)} %copy-done.1, f32[2,128,768]{2,1,0:T(8,128)S(1)} %copy-done.2, f32[2,128,768]{2,1,0:T(8,128)S(1)} %copy-done.3), custom_call_target="tpu_custom_call" | custom-call | tf_op jit(solution)/shard_map/updates/pallas_call | solution.py:707
Async XLA Ops:
  0.6 115.2 %copy-start.1 = (f32[2,128,768]{2,1,0:T(8,128)S(1)}, f32[2,128,768]{2,1,0:T(8,128)}, u32[]{:S(2)}) copy-start(f32[2,128,768]{2,1,0:T(8,128)} %direc.1) | copy-start | bytes 2359300
  0.6 115.2 %copy-start.2 = (f32[2,128,768]{2,1,0:T(8,128)S(1)}, f32[2,128,768]{2,1,0:T(8,128)}, u32[]{:S(2)}) copy-start(f32[2,128,768]{2,1,0:T(8,128)} %resid.1) | copy-start | bytes 2359300
  0.7 115.2 %copy-start.3 = (f32[2,128,768]{2,1,0:T(8,128)S(1)}, f32[2,128,768]{2,1,0:T(8,128)}, u32[]{:S(2)}) copy-start(f32[2,128,768]{2,1,0:T(8,128)} %solu.1) | copy-start | bytes 2359300
  115.9 1.1 copy-start

commit v12 on v11

--- a/solution.py
+++ b/solution.py
@@ -700,7 +700,7 @@
         out_specs=pl.BlockSpec(memory_space=pl.ANY),
         scratch_shapes=scratch,
         compiler_params=pltpu.CompilerParams(
-            collective_id=0, has_side_effects=True, vmem_limit_bytes=58 * 2**20
+            collective_id=0, has_side_effects=True, vmem_limit_bytes=48 * 2**20
         ),
     )(features, projections, direction, residual)
     shape = jax.ShapeDtypeStruct(direction.shape, F32)

time: 119 us -> 121 us (1.017)
  local copies, waits for them, and re-layouts: 1.15 us -> 4.48 us
    unnamed x8 -> x10, local copies, waits for them, and re-layouts: 1.15 us -> 4.48 us
where the time goes in v12:
time: 121 us
  Pallas kernels  116 us (96%)
  local copies, waits for them, and re-layouts  4.48 us (4%)
    pallas_call x1, Pallas kernels, body(): pl.pallas_call(kernel, name='cg_step', out_shape=jax.ShapeDtypeStruct((2...  114 us
    unnamed x10, local copies, waits for them, and re-layouts  4.48 us

profile of v12, /device:TPU:1, one launch (start us, length us, event | category | flops | bytes accessed | tf_op | source)
XLA Modules:
  0.0 120.7 jit_solution(4915963511989292462)
XLA Ops:
  0.6 0.0 copy-start
  0.6 1.1 copy-done
  1.8 0.0 copy-start.1
  1.8 1.1 copy-done.1
  2.9 0.0 copy-start.2
  2.9 1.2 %copy-done.2 = bf16[2,256,1024]{2,1,0:T(8,128)(2,1)S(1)} copy-done((bf16[2,256,1024]{2,1,0:T(8,128)(2,1)S(1)}, bf16[2,256,1024]{2,1,0:T(8,128)(2,1)}, u32[]{:S(2)}) %copy-start.2) | copy-done | bytes 1048600
  4.1 0.0 copy-start.4
  4.1 1.0 copy-done.4
  5.1 0.0 copy-start.3
  5.1 114.0 %cg_step.1.hess = f32[264,768]{1,0:T(8,128)S(1)} custom-call(bf16[2,256,1024]{2,1,0:T(8,128)(2,1)S(1)} %copy-done.2, bf16[2,128,768]{2,1,0:T(8,128)(2,1)S(1)} %copy-done.4, f32[2,128,768]{2,1,0:T(8,128)S(1)} %copy-done, f32[2,128,768]{2,1,0:T(8,128)S(1)} %copy-done.1), custom_call_target="tpu_custom_call" | custom-call | tf_op jit(solution)/shard_map/cg_step/pallas_call | solution.py:695
  119.1 0.0 copy-done.3
  119.1 1.6 %updates.1 = (f32[2,128,768]{2,1,0:T(8,128)}, f32[2,128,768]{2,1,0:T(8,128)}, f32[2,128,768]{2,1,0:T(8,128)}) custom-call(f32[264,768]{1,0:T(8,128)S(1)} %cg_step.1.hess, f32[2,128,768]{2,1,0:T(8,128)S(1)} %copy-done, f32[2,128,768]{2,1,0:T(8,128)S(1)} %copy-done.1, f32[2,128,768]{2,1,0:T(8,128)S(1)} %copy-done.3), custom_call_target="tpu_custom_call" | custom-call | tf_op jit(solution)/shard_map/updates/pallas_call | solution.py:707
Async XLA Ops:
  0.6 1.1 copy-start
  1.8 1.1 copy-start.1
  2.9 1.2 %copy-start.2 = (bf16[2,256,1024]{2,1,0:T(8,128)(2,1)S(1)}, bf16[2,256,1024]{2,1,0:T(8,128)(2,1)}, u32[]{:S(2)}) copy-start(bf16[2,256,1024]{2,1,0:T(8,128)(2,1)} %feats_in.1) | copy-start | bytes 3145732
  4.1 1.0 copy-start.4
  5.1 114.0 %copy-start.3 = (f32[2,128,768]{2,1,0:T(8,128)S(1)}, f32[2,128,768]{2,1,0:T(8,128)}, u32[]{:S(2)}) copy-start(f32[2,128,768]{2,1,0:T(8,128)} %solu.1) | copy-start | bytes 2359300
